TPU v7x, 1024 devices: a whole 4x4x32 slice. The times are simulated.
1024 devices in a mesh: dp: 64 (over z, core), expert: 16 (over x, y).
Axes of the slice: x: 4, y: 4, z: 32, core: 2. Of those that a mesh axis runs over, the one named last changes fastest.
Arguments:
- tokens: bfloat16 [768, 3072], P('expert', 'dp'), may hold values from -6 to 6
- cotangent: bfloat16 [768, 3072], P('expert', 'dp'), may hold values from -6 to 6
- routes: int32 [768, 4], P('expert'), may hold values from 0 to 15, all different within a row; in each aligned block of 48 rows (0 to 47, 48 to 95, ...) at most 16 rows name the same one
- route_weights: float32 [768, 4], P('expert'), may hold values from 0.05 to 0.6
- gate_up: bfloat16 [16, 2, 5376, 3072], P('expert', None, 'dp'), may hold values from -0.109375 to 0.109375
- down_proj: bfloat16 [16, 5376, 3072], P('expert', 'dp'), may hold values from -0.078125 to 0.078125
Outputs:
- grad_tokens: bfloat16 [768, 3072], P('expert', 'dp')
- grad_gate_up: bfloat16 [16, 2, 5376, 3072], P('expert', None, 'dp')
- grad_down: bfloat16 [16, 5376, 3072], P('expert', 'dp')
Inputs may be any that keep to these rules, and one draw needn't show every extreme that they name: `routes`: each token names 4 different experts. Within the tokens of one index of the expert axis (aligned blocks of 48 rows) no expert is named more than 16 times, and in every draw some expert is named exactly 16 times in some block.
All inputs are finite; a program needn't handle non-finite values.
Results may differ from a plain program's by a relative error of at most 0.0064.
Values may be sent and summed in bfloat16 or wider, within the bound.
No kernel may reach another device: no remote copies, remote signals or barrier semaphores. Data moves between devices by JAX's collectives and lax.ppermute only.
A program may use at most 32 MiB of HBM per device.

v0:
```python
import jax
import jax.numpy as jnp
from jax import lax
from jax.sharding import PartitionSpec as P


def contract_last(left, right):
    return lax.dot_general(
        left, right, (((1,), (1,)), ((), ())), preferred_element_type=jnp.float32
    )


def contract_first(left, right):
    return lax.dot_general(
        left, right, (((0,), (0,)), ((), ())), preferred_element_type=jnp.float32
    )


def contract_hidden(weight_cols, grads):
    return lax.dot_general(
        weight_cols, grads, (((0,), (1,)), ((), ())), preferred_element_type=jnp.float32
    )


def hidden_term_of(w_gate, w_up, grad_gate, grad_up):
    return contract_hidden(w_gate, grad_gate) + contract_hidden(w_up, grad_up)


def on_device(tokens, cotangent, routes, route_weights, gate_up, down_proj):
    experts = lax.axis_size("expert")
    tok_count, top_count = routes.shape
    capacity = min(tok_count, tok_count * top_count * 4 // (3 * experts))
    slot_total = experts * capacity
    flat_routes = routes.reshape(-1)
    hot_expert = (flat_routes[:, None] == jnp.arange(experts, dtype=jnp.int32)[None, :]).astype(
        jnp.int32
    )
    earlier = jnp.cumsum(hot_expert, axis=0) - hot_expert
    position = jnp.sum(earlier * hot_expert, axis=1)
    slot_ids = flat_routes * capacity + position
    slot_table = (slot_ids[None, :] == jnp.arange(slot_total, dtype=jnp.int32)[:, None]).astype(
        jnp.float32
    )
    slot_token = slot_table.reshape(slot_total, tok_count, top_count).sum(axis=2)
    slot_scale = jnp.sum(slot_table * route_weights.reshape(-1)[None, :], axis=1)
    picker = slot_token.astype(jnp.bfloat16)
    send_rows = jnp.dot(picker, tokens, preferred_element_type=jnp.float32).astype(jnp.bfloat16)
    grad_rows = jnp.dot(picker, cotangent, preferred_element_type=jnp.float32).astype(jnp.bfloat16)
    send_grad = (slot_scale[:, None] * grad_rows.astype(jnp.float32)).astype(jnp.bfloat16)
    recv_rows, recv_grad = (
        lax.all_to_all(send_rows, "expert", split_axis=0, concat_axis=0, tiled=True),
        lax.all_to_all(send_grad, "expert", split_axis=0, concat_axis=0, tiled=True),
    )
    w_gate = gate_up[0, 0]
    w_up = gate_up[0, 1]
    w_down = down_proj[0]
    full_x, full_dz = (
        lax.all_gather(recv_rows, "dp", axis=1, tiled=True),
        lax.all_gather(recv_grad, "dp", axis=1, tiled=True),
    )
    gate_part = contract_last(full_x, w_gate)
    up_part = contract_last(full_x, w_up)
    back_grad = contract_last(full_dz, w_down)
    sig_gate = jax.nn.sigmoid(gate_part)
    activated = (gate_part * sig_gate * up_part).astype(jnp.bfloat16)
    grad_gate = (back_grad * up_part * sig_gate * (1.0 + gate_part * (1.0 - sig_gate))).astype(
        jnp.bfloat16
    )
    grad_up = (back_grad * gate_part * sig_gate).astype(jnp.bfloat16)
    shares = lax.psum_scatter(
        hidden_term_of(w_gate, w_up, grad_gate, grad_up), "dp", scatter_dimension=0, tiled=True
    )
    returned = lax.all_to_all(
        shares.astype(jnp.bfloat16), "expert", split_axis=1, concat_axis=1, tiled=True
    )
    grad_tokens = lax.dot_general(
        picker, returned, (((0,), (1,)), ((), ())), preferred_element_type=jnp.float32
    ).astype(jnp.bfloat16)
    grad_in_gate = contract_first(grad_gate, full_x)
    grad_in_up = contract_first(grad_up, full_x)
    grad_out = contract_first(activated, full_dz)
    grad_gate_up = jnp.stack([grad_in_gate, grad_in_up]).astype(jnp.bfloat16)
    return (grad_tokens, grad_gate_up[None], grad_out.astype(jnp.bfloat16)[None])


def solution(mesh):
    in_specs = (
        P("expert", "dp"),
        P("expert", "dp"),
        P("expert", None),
        P("expert", None),
        P("expert", None, "dp", None),
        P("expert", "dp", None),
    )
    out_specs = (P("expert", "dp"), P("expert", None, "dp", None), P("expert", "dp", None))
    return jax.shard_map(
        on_device, mesh=mesh, in_specs=in_specs, out_specs=out_specs, check_vma=False
    )
```

profile of v0, /device:TPU:1, one launch (start us, length us, event | category | flops | bytes accessed | tf_op | source)
XLA Modules:
  0.0 530.4 jit_solution(16597510617512565491)
XLA Ops:
  7.2 0.0 copy-start
  7.2 0.0 copy-start.3
  7.2 0.0 all-gather.5.cloned.1.call-start
  7.2 0.9 copy.49
  8.1 0.1 eq.42
  8.2 0.6 reduce-window.6
  8.8 0.2 slice_reduce_fusion
  9.1 0.1 bitcast_bitcast_fusion
  9.2 0.1 reduce_sum.30
  9.3 0.1 copy.52
  9.3 0.7 multiply_add_fusion
  10.0 0.1 convert_reduce_fusion
  10.1 0.9 convolution_convert_fusion.3
  11.1 0.1 copy.56
  11.2 0.1 reshape.84
  11.3 13.8 %all_to_all.36 = bf16[16,2,384]{2,1,0:T(2,128)(2,1)S(1)} all-to-all(bf16[16,2,384]{2,1,0:T(2,128)(2,1)S(1)} %reshape.84), channel_id=1, replica_groups=mesh['dp'=64,'expert'=16] {'expert'}, dimensions={0} | all-to-all | bytes 49152 | tf_op jit(solution)/shard_map/all_to_all | solution.py:51
  25.2 0.1 reshape.85
  25.3 0.7 copy.57
  26.0 0.0 all-gather.5.cloned.1.call-update
  26.0 0.0 all-gather.3.cloned.1.call-start
  26.0 0.8 copy.53
  26.8 0.1 mul.65
  26.9 0.1 select_reduce_fusion
  27.1 0.9 fusion.6
  28.0 0.1 copy.54
  28.1 0.1 reshape.86
  28.2 9.2 %all_to_all.37 = bf16[16,2,384]{2,1,0:T(2,128)(2,1)S(1)} all-to-all(bf16[16,2,384]{2,1,0:T(2,128)(2,1)S(1)} %reshape.86), channel_id=1, replica_groups=mesh['dp'=64,'expert'=16] {'expert'}, dimensions={0} | all-to-all | bytes 49152 | tf_op jit(solution)/shard_map/all_to_all | solution.py:52
  37.5 0.1 reshape.87
  37.6 0.7 copy.55
  38.3 0.0 all-gather.3.cloned.1.call-update
  38.3 0.0 reduce-scatter.4.cloned.1.call-start
  38.4 0.0 copy-done.3
  38.4 2.3 fusion.19
  40.6 127.6 %all-gather.5.cloned.1.call-done = bf16[256,3072]{0,1:T(8,128)(2,1)} async-done(((bf16[256,48]{0,1:T(8,128)(2,1)}), bf16[256,3072]{0,1:T(8,128)(2,1)}) %all-gather.5.cloned.1.call-update) | async-done | bytes 1572880 | tf_op jit(solution)/shard_map/all_gather | solution.py:58
  168.2 0.0 copy-start.1
  168.2 1.9 fusion.9
  170.1 0.0 copy-done.1
  170.1 1.6 fusion.11
  171.7 126.9 %all-gather.3.cloned.1.call-done = bf16[256,3072]{0,1:T(8,128)(2,1)} async-done(((bf16[256,48]{0,1:T(8,128)(2,1)}), bf16[256,3072]{0,1:T(8,128)(2,1)}) %all-gather.3.cloned.1.call-update) | async-done | bytes 1572880 | tf_op jit(solution)/shard_map/all_gather | solution.py:59
  298.6 0.0 copy-done
  298.6 0.0 copy-start.2
  298.6 1.9 multiply_convert_fusion.1
  300.5 0.0 copy-done.2
  300.5 0.6 fusion.10
  301.1 2.3 fusion
  303.4 3.5 copy.61
  307.0 0.0 reduce-scatter.4.cloned.1.call-update
  307.0 0.6 fusion.2
  307.6 0.6 fusion.1
  308.2 0.0 copy-start.4
  308.2 0.1 pad_maximum_fusion
  308.3 199.2 %reduce-scatter.4.cloned.1.call-done = f32[48,256]{1,0:T(8,128)} async-done(((f32[3072,256]{1,0:T(8,128)}), f32[48,256]{1,0:T(8,128)}) %reduce-scatter.4.cloned.1.call-update) | async-done | bytes 49168
  507.5 0.9 copy.62
  508.4 0.7 reshape.88
  509.2 7.4 %all-to-all-start.2 = ((bf16[16,2,384]{2,1,0:T(2,128)(2,1)}), bf16[16,2,384]{2,1,0:T(2,128)(2,1)S(1)}, u32[]{:S(2)}, u32[]{:S(2)}) async-start(bf16[16,2,384]{2,1,0:T(2,128)(2,1)} %reshape.88), calls=%async_computation.2 | async-start | bytes 49152 | tf_op jit(solution)/shard_map/all_to_all | solution.py:73
  516.5 0.0 copy-done.4
  516.6 1.4 fusion.3
  518.0 2.0 copy.60
  520.0 3.0 all-to-all-done.2
  523.0 0.1 reshape.89
  523.1 0.7 convolution_convert_fusion.5
  (6 shorter events, 0.1 us)
Async XLA Ops:
  7.2 291.4 %copy-start = (bf16[1,84,3072]{2,1,0:T(8,128)(2,1)S(1)}, bf16[1,84,3072]{2,1,0:T(8,128)(2,1)}, u32[]{:S(2)}) copy-start(bf16[1,84,3072]{2,1,0:T(8,128)(2,1)} %param.11) | copy-start | bytes 1548292
  7.2 31.2 %copy-start.3 = (bf16[1,2,84,3072]{3,1,2,0:T(2,128)(2,1)S(1)}, bf16[1,2,84,3072]{3,1,2,0:T(2,128)(2,1)}, u32[]{:S(2)}) copy-start(bf16[1,2,84,3072]{3,1,2,0:T(2,128)(2,1)} %param.10) | copy-start | bytes 3096580
  7.2 161.0 %all-gather.5.cloned.1.call-start = ((), (), s32[]{:S(2)}) async-start(), calls=%async_computation.5 | async-start | bytes 1597440 | tf_op jit(solution)/shard_map/all_gather | solution.py:58
  26.0 272.6 %all-gather.3.cloned.1.call-start = ((), (), s32[]{:S(2)}) async-start(), calls=%async_computation.4 | async-start | bytes 1597440 | tf_op jit(solution)/shard_map/all_gather | solution.py:59
  38.3 469.2 %reduce-scatter.4.cloned.1.call-start = ((), (), s32[]{:S(2)}) async-start(), calls=%async_computation.6 | async-start | bytes 3194880
  168.2 1.9 copy-start.1
  298.6 1.9 copy-start.2
  308.2 208.3 %copy-start.4 = (bf16[256,3072]{0,1:T(8,128)(2,1)S(1)}, bf16[256,3072]{0,1:T(8,128)(2,1)}, u32[]{:S(2)}) copy-start(bf16[256,3072]{0,1:T(8,128)(2,1)} %all-gather.3.cloned.1.call-done) | copy-start | bytes 4718596
  509.2 13.8 %all-to-all-start.2 = ((bf16[16,2,384]{2,1,0:T(2,128)(2,1)}), bf16[16,2,384]{2,1,0:T(2,128)(2,1)S(1)}, u32[]{:S(2)}, u32[]{:S(2)}) async-start(bf16[16,2,384]{2,1,0:T(2,128)(2,1)} %reshape.88), calls=%async_computation.2 | async-start | bytes 49152 | tf_op jit(solution)/shard_map/all_to_all | solution.py:73
Sparse Core Ops, SparseCore 0:
  26.1 142.0 all-gather.4
  170.9 127.6 all-gather.2
  307.1 200.3 reduce-scatter.3
where the time goes:
time: 534 us; the launch traced here: 530 us
  waiting for transfers between devices  457 us (86%)
  blocking collectives  23.1 us (4%)
  local copies, waits for them, and re-layouts  13.9 us (3%)
  between operations  13.9 us (3%)
  matrix products  13.4 us (3%)
  starting transfers between devices  7.49 us (1%)
    unnamed x4, waiting for transfers between devices  199 us
    all_gather x1, waiting for transfers between devices, on_device(): lax.all_gather(recv_rows, 'dp', axis=1, tiled=True)  128 us
    all_gather x1, waiting for transfers between devices, on_device(): lax.all_gather(recv_grad, 'dp', axis=1, tiled=True)  127 us
    all_to_all x1, blocking collectives, on_device(): lax.all_to_all(send_rows, 'expert', split_axis=0, concat_axis=0, tiled=True)  13.8 us
  transfers between devices with their start and end apart: 4, of which 4 were waited for; matrix products, arithmetic and copies ran while one was open for 3% of the time, Pallas kernels for 0%

commit v1 on v0

v1 whole, which is shorter than its diff:
```python
import jax
import jax.numpy as jnp
import numpy as np
from jax import lax
from jax.sharding import Mesh, PartitionSpec as P

FAR, NEAR, CORE, EXPERT = "zfar", "znear", "core", "expert"
Z = (FAR, NEAR)
F32, BF16 = jnp.float32, jnp.bfloat16


def dot(left, right, contract):
    return lax.dot_general(left, right, (contract, ((), ())), preferred_element_type=F32)


def exchange(value, axes):
    return lax.all_to_all(value, axes, split_axis=0, concat_axis=0, tiled=True)


def swap_cores(value):
    return lax.ppermute(value, CORE, [(0, 1), (1, 0)])


def slot_tables(routes, route_weights, experts, capacity):
    tok_count, top_count = routes.shape
    slot_total = experts * capacity
    flat_routes = routes.reshape(-1)
    hot_expert = (flat_routes[:, None] == jnp.arange(experts, dtype=jnp.int32)[None, :]).astype(
        jnp.int32
    )
    earlier = jnp.cumsum(hot_expert, axis=0) - hot_expert
    position = jnp.sum(earlier * hot_expert, axis=1)
    slot_ids = flat_routes * capacity + position
    slot_table = (slot_ids[None, :] == jnp.arange(slot_total, dtype=jnp.int32)[:, None]).astype(F32)
    slot_token = slot_table.reshape(slot_total, tok_count, top_count).sum(axis=2)
    slot_scale = jnp.sum(slot_table * route_weights.reshape(-1)[None, :], axis=1)
    return slot_token.astype(BF16), slot_scale


def on_device(tokens, cotangent, routes, route_weights, gate_up, down_proj):
    far, near, experts = (lax.axis_size(name) for name in (FAR, NEAR, EXPERT))
    core = lax.axis_index(CORE)
    tok_count, top_count = routes.shape
    feat = tokens.shape[1]
    width = feat * far * near * 2
    capacity = min(tok_count, tok_count * top_count * 4 // (3 * experts))
    slots = experts * capacity
    picker, slot_scale = slot_tables(routes, route_weights, experts, capacity)

    both = jnp.stack([tokens.T, cotangent.T])
    sent = jnp.broadcast_to(both[None], (far, 2, feat, tok_count)).reshape(far * 2, feat, tok_count)
    column = exchange(sent, (FAR, CORE))
    column = jnp.broadcast_to(column[None], (near,) + column.shape)
    column = exchange(column, NEAR)
    column = column.reshape(near, far, 2, feat, tok_count).transpose(1, 0, 2, 3, 4)
    column = column.reshape(width, tok_count)

    rows = dot(picker, column, ((1,), (1,))).astype(BF16)
    scale = jnp.where(core == 0, 1.0, slot_scale)
    rows = (scale[:, None] * rows.astype(F32)).astype(BF16)
    held = exchange(rows.reshape(experts, capacity, width), EXPERT).reshape(slots, width)
    twin = swap_cores(held)
    full_x = jnp.where(core == 0, held, twin)
    full_dz = jnp.where(core == 0, twin, held)

    w_gate, w_up, w_down = gate_up[0, 0], gate_up[0, 1], down_proj[0]
    hidden = w_gate.shape[0]
    by_core = jnp.concatenate([w_gate, w_up]).reshape(2 * hidden, far * near, 2, feat)
    own_cols = jnp.where(core == 0, by_core[:, :, 0], by_core[:, :, 1]).reshape(2 * hidden, -1)
    twin_cols = jnp.where(core == 0, by_core[:, :, 1], by_core[:, :, 0]).reshape(2 * hidden, -1)
    own_cols, twin_cols = lax.optimization_barrier((own_cols, twin_cols))

    last = ((1,), (1,))
    gate_part = dot(full_x, w_gate, last)
    up_part = dot(full_x, w_up, last)
    back_grad = dot(full_dz, w_down, last)
    sig_gate = jax.nn.sigmoid(gate_part)
    activated = (gate_part * sig_gate * up_part).astype(BF16)
    grad_gate = (back_grad * up_part * sig_gate * (1.0 + gate_part * (1.0 - sig_gate))).astype(BF16)
    grad_up = (back_grad * gate_part * sig_gate).astype(BF16)

    grads = jnp.concatenate([grad_gate, grad_up], axis=1)
    twin_part = dot(grads, twin_cols, ((1,), (0,))).astype(BF16)
    arrived = swap_cores(twin_part)
    share = (dot(grads, own_cols, ((1,), (0,))) + arrived.astype(F32)).astype(BF16)
    returned = exchange(share.reshape(experts, capacity, -1), EXPERT).reshape(slots, -1)
    summed = dot(returned, picker, ((0,), (0,))).astype(BF16)
    pieces = exchange(summed.reshape(far * near, feat, tok_count), Z)
    grad_tokens = jnp.sum(pieces.astype(F32), axis=0).astype(BF16).T

    first = ((0,), (0,))
    grad_in = jnp.stack([dot(grad_gate, full_x, first), dot(grad_up, full_x, first)]).astype(BF16)
    grad_out = dot(activated, full_dz, first).astype(BF16)
    return grad_tokens, grad_in[None], grad_out[None]


def solution(mesh):
    dp, experts = mesh.devices.shape
    near = 4 if dp % 8 == 0 else 1
    split = Mesh(
        mesh.devices.reshape(dp // (2 * near), near, 2, experts), (FAR, NEAR, CORE, EXPERT)
    )
    shards = (FAR, NEAR, CORE)
    in_specs = (
        P(EXPERT, shards),
        P(EXPERT, shards),
        P(EXPERT, None),
        P(EXPERT, None),
        P(EXPERT, None, shards, None),
        P(EXPERT, shards, None),
    )
    out_specs = (P(EXPERT, shards), P(EXPERT, None, shards, None), P(EXPERT, shards, None))
    return jax.shard_map(
        on_device, mesh=split, in_specs=in_specs, out_specs=out_specs, check_vma=False
    )
```

time: 534 us -> 184 us (0.34)
  waiting for transfers between devices: 457 us -> 34.3 us
  blocking collectives: 23.1 us -> 100 us
  between operations: 13.9 us -> 0.93 us
  matrix products: 13.4 us -> 5.65 us
  starting transfers between devices: 7.49 us -> 14.7 us
    all_gather x2 -> x0, waiting for transfers between devices: 255 us -> none  [the longest x1 128 us: on_device(): lax.all_gather(recv_rows, 'dp', axis=1, tiled=True)]
    unnamed x4 -> x0, waiting for transfers between devices: 199 us -> none
    all_to_all x2 -> x3, blocking collectives: 23.1 us -> 100 us  [exchange(): return lax.all_to_all(value, axes, split_axis=0, concat_axis=0, tiled=True)]
    all_to_all x1 -> x2, waiting for transfers between devices: 3.02 us -> 32.4 us  [exchange(): return lax.all_to_all(value, axes, split_axis=0, concat_axis=0, tiled=True)]
    dot_general x11 -> x10, matrix products: 13.4 us -> 5.65 us  [dot(): lax.dot_general(left, right, (contract, ((), ())), preferred_element_type...]
    slice x2 -> x4, local copies, waits for them, and re-layouts: 2.44 us -> 8.09 us  [the longest x3 7.91 us: on_device(): w_gate, w_up, w_down = (gate_up[0, 0], gate_up[0, 1], down_proj[0])]
  transfers between devices with their start and end apart: 4 -> 4, of which waited for: 4 -> 3; matrix products, arithmetic and copies ran while one was open for 3% -> 9% of each run, Pallas kernels for 0% -> 0%
where the time goes in v1:
time: 184 us; the launch traced here: 181 us
  blocking collectives  100 us (54%)
  waiting for transfers between devices  34.3 us (19%)
  local copies, waits for them, and re-layouts  18.8 us (10%)
  starting transfers between devices  14.7 us (8%)
  other arithmetic  7 us (4%)
  matrix products  5.65 us (3%)
    all_to_all x3, blocking collectives, exchange(): return lax.all_to_all(value, axes, split_axis=0, concat_axis=0, tiled=True)  100 us
    all_to_all x2, waiting for transfers between devices, exchange(): return lax.all_to_all(value, axes, split_axis=0, concat_axis=0, tiled=True)  32.4 us
    all_to_all x2, starting transfers between devices, exchange(): return lax.all_to_all(value, axes, split_axis=0, concat_axis=0, tiled=True)  9.46 us
    slice x3, local copies, waits for them, and re-layouts, on_device(): w_gate, w_up, w_down = (gate_up[0, 0], gate_up[0, 1], down_proj[0])  7.91 us
    unnamed x25, local copies, waits for them, and re-layouts  7.15 us
    dot_general x10, matrix products, dot(): lax.dot_general(left, right, (contract, ((), ())), preferred_element_type...  5.65 us
    ppermute x2, starting transfers between devices, swap_cores(): return lax.ppermute(value, CORE, [(0, 1), (1, 0)])  5.23 us
  transfers between devices with their start and end apart: 4, of which 3 were waited for; matrix products, arithmetic and copies ran while one was open for 9% of the time, Pallas kernels for 0%

profile of v1, /device:TPU:1, one launch (start us, length us, event | category | flops | bytes accessed | tf_op | source)
XLA Modules:
  0.0 181.4 jit_solution(4047611936616886142)
XLA Ops:
  0.6 0.0 copy-start
  0.6 0.8 pad_maximum_fusion.7
  1.4 0.1 copy.71
  1.6 0.3 reshape.130
  1.9 0.0 copy-start.6
  1.9 0.0 copy-start.7
  1.9 54.3 %all_to_all.25 = bf16[16,2,1152]{2,1,0:T(2,128)(2,1)S(1)} all-to-all(bf16[16,2,1152]{2,1,0:T(2,128)(2,1)S(1)} %reshape.130), channel_id=1, replica_groups=mesh['zfar'=8,'znear'=4,'core'=2,'expert'=16] {'zfar','core'}, dimensions={0} | all-to-all | bytes 147456 | tf_op jit(solution)/shard_map/all_to_all | solution.py:17
  56.2 0.2 reshape.131
  56.4 0.1 broadcast_in_dim.11
  56.5 2.0 %reshape.132 = bf16[4,2,18432]{2,1,0:T(2,128)(2,1)} reshape(bf16[4,16,48,48]{3,2,1,0:T(8,128)(2,1)S(1)} %broadcast_in_dim.11) | data formatting | bytes 589824
  58.5 4.5 %all-to-all-start.1 = ((bf16[4,2,18432]{2,1,0:T(2,128)(2,1)}), bf16[4,2,18432]{2,1,0:T(2,128)(2,1)S(1)}, u32[]{:S(2)}, u32[]{:S(2)}) async-start(bf16[4,2,18432]{2,1,0:T(2,128)(2,1)} %reshape.132), calls=%async_computation.1 | async-start | bytes 589824 | tf_op jit(solution)/shard_map/all_to_all | solution.py:17
  63.0 0.0 copy-done.6
  63.0 0.1 copy.66
  63.1 0.1 reshape.117
  63.3 0.6 reduce-window.6
  63.9 0.2 slice_reduce_fusion
  64.1 0.0 copy-done.7
  64.1 0.1 copy.69
  64.2 0.1 mul.63
  64.3 0.1 bitcast_bitcast_fusion
  64.4 0.1 reduce_sum.43
  64.5 0.1 copy.70
  64.6 0.1 convert_reduce_fusion
  64.7 0.1 select_reduce_fusion
  64.9 7.2 %all-to-all-done.1 = bf16[4,2,18432]{2,1,0:T(2,128)(2,1)S(1)} async-done(((bf16[4,2,18432]{2,1,0:T(2,128)(2,1)}), bf16[4,2,18432]{2,1,0:T(2,128)(2,1)S(1)}, u32[]{:S(2)}, u32[]{:S(2)}) %all-to-all-start.1) | async-done | bytes 294944 | tf_op jit(solution)/shard_map/all_to_all | solution.py:17
  72.1 0.8 reshape.133
  72.8 1.0 copy.72
  73.9 1.4 reshape.122
  75.3 0.6 fusion.2
  75.9 0.0 copy-start.5
  75.9 29.4 %all_to_all.26 = bf16[16,16,3072]{2,1,0:T(8,128)(2,1)S(1)} all-to-all(bf16[16,16,3072]{2,1,0:T(8,128)(2,1)S(1)} %bitcast.73), channel_id=1, replica_groups=mesh['zfar'=8,'znear'=4,'core'=2,'expert'=16] {'expert'}, dimensions={0} | all-to-all | bytes 3145728 | tf_op jit(solution)/shard_map/all_to_all | solution.py:17
  105.3 2.2 %collective-permute-start = (bf16[256,3072]{1,0:T(8,128)(2,1)S(1)}, bf16[256,3072]{1,0:T(8,128)(2,1)}, u32[]{:S(2)}, u32[]{:S(2)}) collective-permute-start(bf16[256,3072]{1,0:T(8,128)(2,1)S(1)} %bitcast.70), channel_id=1, source_target_pairs={{0,16},{16,0},{1,17},{17,1},{2,18},{18,2},{3,19},{19,3},{4,20},{20... | collective-permute-start | bytes 4718600 | tf_op jit(solution)/shard_map/ppermute | solution.py:21
  107.4 0.0 copy-done.5
  107.4 2.3 %fusion.20 = (bf16[1,1,84,3072]{3,1,2,0:T(2,128)(2,1)S(1)}, bf16[1,1,84,3072]{3,1,2,0:T(2,128)(2,1)}) fusion(bf16[1,2,84,3072]{3,1,2,0:T(2,128)(2,1)S(1)} %copy-done.5), kind=kLoop, calls=%fused_computation.58 | loop fusion | bytes 2064384 | tf_op jit(solution)/shard_map/slice | solution.py:66
  109.7 0.0 copy-done.1
  109.7 2.0 %copy.75 = bf16[1,1,84,3072]{2,3,1,0:T(8,128)(2,1)} copy(bf16[1,1,84,3072]{3,1,2,0:T(2,128)(2,1)S(1)} %get-tuple-element.27) | data formatting | bytes 1032192 | tf_op jit(solution)/shard_map/slice | solution.py:66
  111.7 3.6 %copy.76 = bf16[1,1,84,3072]{2,3,1,0:T(8,128)(2,1)} copy(bf16[1,1,84,3072]{3,1,2,0:T(2,128)(2,1)} %get-tuple-element.28) | data formatting | bytes 1032192 | tf_op jit(solution)/shard_map/slice | solution.py:66
  115.4 2.8 %broadcast_select_fusion.2 = (bf16[168,32,1,48]{0,3,2,1:T(8,128)(2,1)S(1)}, bf16[168,32,1,48]{0,3,2,1:T(8,128)(2,1)S(1)}) fusion(pred[]{:T(512)S(6)} %eq.47, bf16[84,32,2,48]{0,3,2,1:T(8,128)(2,1)} %bitcast.78, bf16[84,32,2,48]{0,3,2,1:T(8,128)(2,1)} %bitcast.77), kind=kLoop, calls=%fused_computation.20 | loop fusion | flops 3612672 | bytes 2064385 | tf_op jit(solution)/shard_map/jit(_where)/select_n | solution.py:70
  118.1 0.0 copy-start.4
  118.1 0.0 collective-permute-done
  118.1 0.0 copy-done.2
  118.2 1.7 broadcast_select_fusion
  119.8 0.0 copy-done.4
  119.8 0.6 fusion.9
  120.5 0.6 fusion.8
  121.1 0.6 multiply_convert_fusion.2
  121.7 0.4 convolution_convert_fusion.4
  122.2 3.1 %collective-permute-start.1 = (bf16[256,1536]{1,0:T(8,128)(2,1)S(1)}, bf16[256,1536]{1,0:T(8,128)(2,1)S(1)}, u32[]{:S(2)}, u32[]{:S(2)}) collective-permute-start(bf16[256,1536]{1,0:T(8,128)(2,1)S(1)} %convolution_convert_fusion.4), channel_id=1, source_target_pairs={{0,16},{16,0},{1,17},{17,1},{2,18},{18,2},{3,19},{19,3},{4,20},{20... | collective-permute-start | bytes 2359304 | tf_op jit(solution)/shard_map/ppermute | solution.py:21
  125.2 1.9 %collective-permute-done.1 = bf16[256,1536]{1,0:T(8,128)(2,1)S(1)} collective-permute-done((bf16[256,1536]{1,0:T(8,128)(2,1)S(1)}, bf16[256,1536]{1,0:T(8,128)(2,1)S(1)}, u32[]{:S(2)}, u32[]{:S(2)}) %collective-permute-start.1) | collective-permute-done | bytes 786464 | tf_op jit(solution)/shard_map/ppermute | solution.py:21
  127.1 0.4 add_convert_fusion
  127.6 16.4 %all_to_all.27 = bf16[16,16,1536]{2,1,0:T(8,128)(2,1)S(1)} all-to-all(bf16[16,16,1536]{2,1,0:T(8,128)(2,1)S(1)} %bitcast.75), channel_id=1, replica_groups=mesh['zfar'=8,'znear'=4,'core'=2,'expert'=16] {'expert'}, dimensions={0} | all-to-all | bytes 1572864 | tf_op jit(solution)/shard_map/all_to_all | solution.py:17
  143.9 0.2 convolution_convert_fusion.5
  144.2 0.4 reshape.127
  144.6 0.2 copy.92
  144.7 1.2 reshape.134
  146.0 4.9 %all-to-all-start.4 = ((bf16[32,2,1152]{2,1,0:T(2,128)(2,1)}), bf16[32,2,1152]{2,1,0:T(2,128)(2,1)S(1)}, u32[]{:S(2)}, u32[]{:S(2)}) async-start(bf16[32,2,1152]{2,1,0:T(2,128)(2,1)} %reshape.134), calls=%async_computation.4 | async-start | bytes 294912 | tf_op jit(solution)/shard_map/all_to_all | solution.py:17
  150.9 0.4 fusion.3
  151.3 0.4 fusion.4
  151.7 0.1 pad_maximum_fusion
  151.8 2.0 %copy.78 = bf16[1,2,84,3072]{3,1,2,0:T(2,128)(2,1)} copy(bf16[1,2,84,3072]{3,2,1,0:T(8,128)(2,1)S(1)} %pad_maximum_fusion) | data formatting | bytes 2064384
  153.8 1.3 fusion.5
  155.2 25.2 %all-to-all-done.4 = bf16[32,2,1152]{2,1,0:T(2,128)(2,1)S(1)} async-done(((bf16[32,2,1152]{2,1,0:T(2,128)(2,1)}), bf16[32,2,1152]{2,1,0:T(2,128)(2,1)S(1)}, u32[]{:S(2)}, u32[]{:S(2)}) %all-to-all-start.4) | async-done | bytes 147488 | tf_op jit(solution)/shard_map/all_to_all | solution.py:17
  180.4 0.4 reshape.135
  180.8 0.7 bitcast_reduce_fusion
  (14 shorter events, 0.1 us)
Async XLA Ops:
  0.6 120.4 %copy-start = (bf16[1,84,3072]{2,1,0:T(8,128)(2,1)S(1)}, bf16[1,84,3072]{2,1,0:T(8,128)(2,1)}, u32[]{:S(2)}) copy-start(bf16[1,84,3072]{2,1,0:T(8,128)(2,1)} %param.11) | copy-start | bytes 1548292
  1.9 61.2 %copy-start.6 = (s32[48,4]{0,1:T(4,128)S(1)}, s32[48,4]{0,1:T(4,128)}, u32[]{:S(2)}) copy-start(s32[48,4]{0,1:T(4,128)} %param.8) | copy-start | bytes 2308
  1.9 62.2 %copy-start.7 = (f32[48,4]{0,1:T(4,128)S(1)}, f32[48,4]{0,1:T(4,128)}, u32[]{:S(2)}) copy-start(f32[48,4]{0,1:T(4,128)} %param.9) | copy-start | bytes 2308
  58.5 13.6 %all-to-all-start.1 = ((bf16[4,2,18432]{2,1,0:T(2,128)(2,1)}), bf16[4,2,18432]{2,1,0:T(2,128)(2,1)S(1)}, u32[]{:S(2)}, u32[]{:S(2)}) async-start(bf16[4,2,18432]{2,1,0:T(2,128)(2,1)} %reshape.132), calls=%async_computation.1 | async-start | bytes 589824 | tf_op jit(solution)/shard_map/all_to_all | solution.py:17
  75.9 31.6 %copy-start.5 = (bf16[1,2,84,3072]{3,1,2,0:T(2,128)(2,1)S(1)}, bf16[1,2,84,3072]{3,1,2,0:T(2,128)(2,1)}, u32[]{:S(2)}) copy-start(bf16[1,2,84,3072]{3,1,2,0:T(2,128)(2,1)} %param.10) | copy-start | bytes 3096580
  105.3 4.4 %copy-start.1 = (bf16[16,16,3072]{2,1,0:T(8,128)(2,1)}, bf16[16,16,3072]{2,1,0:T(8,128)(2,1)S(1)}, u32[]{:S(2)}) copy-start(bf16[16,16,3072]{2,1,0:T(8,128)(2,1)S(1)} %all_to_all.26) | copy-start | bytes 4718596
  105.3 12.9 %collective-permute-start = (bf16[256,3072]{1,0:T(8,128)(2,1)S(1)}, bf16[256,3072]{1,0:T(8,128)(2,1)}, u32[]{:S(2)}, u32[]{:S(2)}) collective-permute-start(bf16[256,3072]{1,0:T(8,128)(2,1)S(1)} %bitcast.70), channel_id=1, source_target_pairs={{0,16},{16,0},{1,17},{17,1},{2,18},{18,2},{3,19},{19,3},{4,20},{20... | collective-permute-start | bytes 4718600 | tf_op jit(solution)/shard_map/ppermute | solution.py:21
  115.4 2.8 %copy-start.2 = (bf16[16,16,3072]{2,1,0:T(8,128)(2,1)S(1)}, bf16[16,16,3072]{2,1,0:T(8,128)(2,1)}, u32[]{:S(2)}) copy-start(bf16[16,16,3072]{2,1,0:T(8,128)(2,1)} %copy-done.1) | copy-start | bytes 4718596
  118.1 1.7 copy-start.4
  122.2 5.0 %collective-permute-start.1 = (bf16[256,1536]{1,0:T(8,128)(2,1)S(1)}, bf16[256,1536]{1,0:T(8,128)(2,1)S(1)}, u32[]{:S(2)}, u32[]{:S(2)}) collective-permute-start(bf16[256,1536]{1,0:T(8,128)(2,1)S(1)} %convolution_convert_fusion.4), channel_id=1, source_target_pairs={{0,16},{16,0},{1,17},{17,1},{2,18},{18,2},{3,19},{19,3},{4,20},{20... | collective-permute-start | bytes 2359304 | tf_op jit(solution)/shard_map/ppermute | solution.py:21
  146.0 34.4 %all-to-all-start.4 = ((bf16[32,2,1152]{2,1,0:T(2,128)(2,1)}), bf16[32,2,1152]{2,1,0:T(2,128)(2,1)S(1)}, u32[]{:S(2)}, u32[]{:S(2)}) async-start(bf16[32,2,1152]{2,1,0:T(2,128)(2,1)} %reshape.134), calls=%async_computation.4 | async-start | bytes 294912 | tf_op jit(solution)/shard_map/all_to_all | solution.py:17
  151.8 2.0 %copy-start.3 = (bf16[16,16,3072]{2,1,0:T(8,128)(2,1)S(1)}, bf16[16,16,3072]{2,1,0:T(8,128)(2,1)}, u32[]{:S(2)}) copy-start(bf16[16,16,3072]{2,1,0:T(8,128)(2,1)} %copy-done.1) | copy-start | bytes 4718596

commit v2 on v1

v2 whole, which is shorter than its diff:
```python
import jax
import jax.numpy as jnp
from jax import lax
from jax.experimental.layout import Layout, with_layout_constraint
from jax.sharding import PartitionSpec as P

DP, EXPERT = "dp", "expert"
F32, BF16 = jnp.float32, jnp.bfloat16
LAST, FIRST, INNER = ((1,), (1,)), ((0,), (0,)), ((1,), (0,))


def dot(left, right, contract):
    return lax.dot_general(left, right, (contract, ((), ())), preferred_element_type=F32)


def exchange(value, axis, groups=None):
    return lax.all_to_all(
        value, axis, split_axis=0, concat_axis=0, tiled=True, axis_index_groups=groups
    )


def slot_tables(routes, route_weights, experts, capacity):
    tok_count, top_count = routes.shape
    slot_total = experts * capacity
    flat_routes = routes.reshape(-1)
    hot_expert = (flat_routes[:, None] == jnp.arange(experts, dtype=jnp.int32)[None, :]).astype(
        jnp.int32
    )
    earlier = jnp.cumsum(hot_expert, axis=0) - hot_expert
    position = jnp.sum(earlier * hot_expert, axis=1)
    slot_ids = flat_routes * capacity + position
    slot_table = (slot_ids[None, :] == jnp.arange(slot_total, dtype=jnp.int32)[:, None]).astype(F32)
    slot_token = slot_table.reshape(slot_total, tok_count, top_count).sum(axis=2)
    slot_scale = jnp.sum(slot_table * route_weights.reshape(-1)[None, :], axis=1)
    return slot_token.astype(BF16), slot_scale


def on_device(tokens, cotangent, routes, route_weights, gate_up, down_proj):
    dp, experts = lax.axis_size(DP), lax.axis_size(EXPERT)
    depth = dp // 2
    near = 4 if depth % 4 == 0 else 1
    far = depth // near
    core = lax.axis_index(DP) % 2
    tok_count, top_count = routes.shape
    feat = tokens.shape[1]
    width = feat * dp
    capacity = min(tok_count, tok_count * top_count * 4 // (3 * experts))
    slots = experts * capacity

    turn = far // 2
    far_order = [(j + turn) % far for j in range(far)]
    z_order = [f * near + n for f in far_order for n in range(near)]
    far_groups = [[(f * near + n) * 2 + c for f in far_order for c in (0, 1)] for n in range(near)]
    near_groups = [
        [(f * near + n) * 2 + c for n in range(near)] for f in range(far) for c in (0, 1)
    ]
    z_groups = [[z * 2 + c for z in z_order] for c in (0, 1)]

    def swap_cores(value):
        return lax.ppermute(value, DP, [(i, i ^ 1) for i in range(dp)])

    picker, slot_scale = slot_tables(routes, route_weights, experts, capacity)

    block = (2, feat * tok_count // 2)
    both = lax.optimization_barrier(jnp.stack([tokens, cotangent]))
    both = both.transpose(0, 2, 1).reshape(1, 2, *block)
    sent = jnp.broadcast_to(both, (far, 2, *block)).reshape(far * 2, *block)
    column = exchange(sent, DP, far_groups)

    w_gate, w_up, w_down = gate_up[0, 0], gate_up[0, 1], down_proj[0]
    hidden = w_gate.shape[0]
    w_in = jnp.concatenate([w_gate, w_up])
    w_all = jnp.concatenate([w_in, w_down])
    by_core = jnp.roll(w_in.reshape(2 * hidden, depth, 2, feat), -turn * near, axis=1)
    own_cols = jnp.where(core == 0, by_core[:, :, 0], by_core[:, :, 1]).reshape(2 * hidden, -1)
    twin_cols = jnp.where(core == 0, by_core[:, :, 1], by_core[:, :, 0]).reshape(2 * hidden, -1)
    column, w_all, own_cols, twin_cols = lax.optimization_barrier(
        (column, w_all, own_cols, twin_cols)
    )

    column = jnp.broadcast_to(column[None], (near,) + column.shape).reshape(-1, *block)
    column = exchange(column, DP, near_groups)
    column = column.reshape(near, far, 2, feat, tok_count)
    column = jnp.roll(column, turn, axis=1).transpose(1, 0, 2, 3, 4)
    column = with_layout_constraint(column.reshape(width, tok_count), Layout((0, 1)))

    rows = dot(picker, column, LAST).astype(BF16)
    scale = jnp.where(core == 0, 1.0, slot_scale)
    rows = (scale[:, None] * rows.astype(F32)).astype(BF16)
    held = exchange(rows.reshape(experts, capacity, width), EXPERT).reshape(slots, width)
    twin = swap_cores(held)
    from_held, twin = lax.optimization_barrier((dot(held, w_all, LAST), twin))
    from_twin = dot(twin, w_all, LAST)
    full_x = jnp.where(core == 0, held, twin)
    full_dz = jnp.where(core == 0, twin, held)
    from_x = jnp.where(core == 0, from_held, from_twin)
    gate_part, up_part = from_x[:, :hidden], from_x[:, hidden : 2 * hidden]
    back_grad = jnp.where(core == 0, from_twin, from_held)[:, 2 * hidden :]
    sig_gate = jax.nn.sigmoid(gate_part)
    activated = (gate_part * sig_gate * up_part).astype(BF16)
    grad_gate = (back_grad * up_part * sig_gate * (1.0 + gate_part * (1.0 - sig_gate))).astype(BF16)
    grad_up = (back_grad * gate_part * sig_gate).astype(BF16)

    grads = jnp.concatenate([grad_gate, grad_up], axis=1)
    twin_part = dot(grads, twin_cols, INNER).astype(BF16)
    arrived = swap_cores(twin_part)
    share = (dot(grads, own_cols, INNER) + arrived.astype(F32)).astype(BF16)
    returned = exchange(share.reshape(experts, capacity, -1), EXPERT).reshape(slots, -1)
    summed = dot(returned, picker, FIRST).astype(BF16)
    pieces = exchange(summed.reshape(depth, feat, tok_count), DP, z_groups)
    grad_tokens = jnp.sum(pieces.astype(F32), axis=0).astype(BF16).T

    grad_in = jnp.stack([dot(grad_gate, full_x, FIRST), dot(grad_up, full_x, FIRST)]).astype(BF16)
    grad_out = dot(activated, full_dz, FIRST).astype(BF16)
    return grad_tokens, grad_in[None], grad_out[None]


def solution(mesh):
    in_specs = (
        P(EXPERT, DP),
        P(EXPERT, DP),
        P(EXPERT, None),
        P(EXPERT, None),
        P(EXPERT, None, DP, None),
        P(EXPERT, DP, None),
    )
    out_specs = (P(EXPERT, DP), P(EXPERT, None, DP, None), P(EXPERT, DP, None))
    return jax.shard_map(
        on_device, mesh=mesh, in_specs=in_specs, out_specs=out_specs, check_vma=False
    )
```

time: 184 us -> 165 us (0.90); the launches traced: 181 us -> 165 us
  blocking collectives: 100 us -> 42.4 us
  starting transfers between devices: 14.7 us -> 68.7 us
  waiting for transfers between devices: 34.3 us -> 19.5 us
    all_to_all x3 -> x2, blocking collectives: 100 us -> 42.4 us  [exchange(): lax.all_to_all(value, axis, split_axis=0, concat_axis=0, tiled=True, axis...]
    all_to_all x2 -> x3, starting transfers between devices: 9.46 us -> 60.3 us  [exchange(): lax.all_to_all(value, axis, split_axis=0, concat_axis=0, tiled=True, axis...]
    all_to_all x2 -> x3, waiting for transfers between devices: 32.4 us -> 15.2 us  [exchange(): lax.all_to_all(value, axis, split_axis=0, concat_axis=0, tiled=True, axis...]
    slice x3 -> x1, local copies, waits for them, and re-layouts: 7.91 us -> 2.26 us  [on_device(): w_gate, w_up, w_down = (gate_up[0, 0], gate_up[0, 1], down_proj[0])]
    unnamed x25 -> x24, local copies, waits for them, and re-layouts: 7.15 us -> 10.7 us
    ppermute x2, starting transfers between devices: 5.23 us -> 8.4 us  [swap_cores(): return lax.ppermute(value, DP, [(i, i ^ 1) for i in range(dp)])]
    concatenate x0 -> x3, other arithmetic: none -> 2.85 us  [the longest x1 2.03 us: on_device(): w_all = jnp.concatenate([w_in, w_down])]
    reshape x3, local copies, waits for them, and re-layouts: 1.94 us -> 4.72 us  [the longest x2 3.95 us: on_device(): pieces = exchange(summed.reshape(depth, feat, tok_count), DP, z_groups)]
  transfers between devices with their start and end apart: 4 -> 5, of which waited for: 3 -> 4; matrix products, arithmetic and copies ran while one was open for 9% -> 11% of each run, Pallas kernels for 0% -> 0%
where the time goes in v2:
time: 165 us
  starting transfers between devices  68.7 us (42%)
  blocking collectives  42.4 us (26%)
  local copies, waits for them, and re-layouts  20.1 us (12%)
  waiting for transfers between devices  19.5 us (12%)
  other arithmetic  7.06 us (4%)
  matrix products  5.86 us (4%)
    all_to_all x3, starting transfers between devices, exchange(): lax.all_to_all(value, axis, split_axis=0, concat_axis=0, tiled=True, axis...  60.3 us
    all_to_all x2, blocking collectives, exchange(): lax.all_to_all(value, axis, split_axis=0, concat_axis=0, tiled=True, axis...  42.4 us
    all_to_all x3, waiting for transfers between devices, exchange(): lax.all_to_all(value, axis, split_axis=0, concat_axis=0, tiled=True, axis...  15.2 us
    unnamed x24, local copies, waits for them, and re-layouts  10.7 us
    ppermute x2, starting transfers between devices, swap_cores(): return lax.ppermute(value, DP, [(i, i ^ 1) for i in range(dp)])  8.4 us
    dot_general x9, matrix products, dot(): lax.dot_general(left, right, (contract, ((), ())), preferred_element_type...  5.86 us
    ppermute x2, waiting for transfers between devices, swap_cores(): return lax.ppermute(value, DP, [(i, i ^ 1) for i in range(dp)])  4.31 us
    reshape x2, local copies, waits for them, and re-layouts, on_device(): pieces = exchange(summed.reshape(depth, feat, tok_count), DP, z_groups)  3.95 us
  transfers between devices with their start and end apart: 5, of which 4 were waited for; matrix products, arithmetic and copies ran while one was open for 11% of the time, Pallas kernels for 0%

profile of v2, /device:TPU:1, one launch (start us, length us, event | category | flops | bytes accessed | tf_op | source)
XLA Modules:
  0.0 164.6 jit_solution(9641150193156544134)
XLA Ops:
  0.6 0.0 copy-start.1
  0.6 0.8 pad_maximum_fusion.8
  1.5 0.1 copy.65
  1.6 0.1 broadcast_in_dim.13
  1.7 0.7 broadcast_in_dim.14
  2.3 35.5 %all-to-all-start = ((bf16[16,2,1152]{2,1,0:T(2,128)(2,1)}), bf16[16,2,1152]{2,1,0:T(2,128)(2,1)S(1)}, u32[]{:S(2)}, u32[]{:S(2)}) async-start(bf16[16,2,1152]{2,1,0:T(2,128)(2,1)} %bitcast.4), calls=%async_computation | async-start | bytes 147456 | tf_op jit(solution)/shard_map/all_to_all | solution.py:17
  37.9 1.4 copy.68
  39.3 2.3 %fusion.19 = (bf16[1,1,84,3072]{3,1,2,0:T(2,128)(2,1)}, bf16[1,1,84,3072]{3,1,2,0:T(2,128)(2,1)S(1)}) fusion(bf16[1,2,84,3072]{3,1,2,0:T(2,128)(2,1)S(1)} %copy-done.1), kind=kLoop, calls=%fused_computation.58 | loop fusion | bytes 2064384 | tf_op jit(solution)/shard_map/slice | solution.py:70
  41.6 2.6 %copy.75 = bf16[1,1,84,3072]{2,3,1,0:T(8,128)(2,1)S(1)} copy(bf16[1,1,84,3072]{3,1,2,0:T(2,128)(2,1)} %get-tuple-element.32) | data formatting | bytes 1032192
  44.1 1.0 copy.76
  45.1 0.3 fusion.9
  45.5 0.5 fusion.6
  45.9 1.3 broadcast_select_fusion.1
  47.2 2.0 %pad_maximum_fusion.1 = bf16[252,3072]{0,1:T(8,128)(2,1)} fusion(bf16[84,3072]{0,1:T(8,128)(2,1)S(1)} %bitcast.74, bf16[84,3072]{0,1:T(8,128)(2,1)S(1)} %bitcast.67, bf16[84,3072]{0,1:T(8,128)(2,1)S(1)} %bitcast.64), kind=kLoop, calls=%fused_computation.14 | loop fusion | flops 4644864 | bytes 3096576 | tf_op jit(solution)/shard_map/concatenate | solution.py:73
  49.3 0.0 all-to-all-done
  49.3 0.9 broadcast_in_dim.28
  50.1 3.5 %all-to-all-start.1 = ((bf16[64,2,1152]{2,1,0:T(2,128)(2,1)}), bf16[64,2,1152]{2,1,0:T(2,128)(2,1)S(1)}, u32[]{:S(2)}, u32[]{:S(2)}) async-start(bf16[64,2,1152]{2,1,0:T(2,128)(2,1)} %bitcast.12), calls=%async_computation.1 | async-start | bytes 589824 | tf_op jit(solution)/shard_map/all_to_all | solution.py:17
  53.6 0.1 copy.63
  53.7 0.1 mul.63
  53.8 0.1 copy.60
  53.9 0.1 reshape.121
  54.0 0.6 reduce-window.6
  54.6 0.2 slice_reduce_fusion
  54.8 0.1 bitcast_bitcast_fusion
  55.0 0.1 reduce_sum.43
  55.1 0.1 copy.64
  55.1 0.1 convert_reduce_fusion
  55.3 0.1 select_reduce_fusion
  55.4 6.3 %all-to-all-done.1 = bf16[64,2,1152]{2,1,0:T(2,128)(2,1)S(1)} async-done(((bf16[64,2,1152]{2,1,0:T(2,128)(2,1)}), bf16[64,2,1152]{2,1,0:T(2,128)(2,1)S(1)}, u32[]{:S(2)}, u32[]{:S(2)}) %all-to-all-start.1) | async-done | bytes 294944 | tf_op jit(solution)/shard_map/all_to_all | solution.py:17
  61.7 0.8 reshape.126
  62.5 0.1 fusion.20
  62.5 0.2 maximum_bitcast_fusion
  62.7 0.1 copy.69
  62.8 0.6 fusion.2
  63.4 26.1 %all_to_all.25 = bf16[16,16,3072]{2,1,0:T(8,128)(2,1)S(1)} all-to-all(bf16[16,16,3072]{2,1,0:T(8,128)(2,1)S(1)} %bitcast.68), channel_id=1, replica_groups=mesh['dp'=64,'expert'=16] {'expert'}, dimensions={0} | all-to-all | bytes 3145728 | tf_op jit(solution)/shard_map/all_to_all | solution.py:17
  89.6 6.1 %collective-permute-start = (bf16[256,3072]{1,0:T(8,128)(2,1)S(1)}, bf16[256,3072]{1,0:T(8,128)(2,1)S(1)}, u32[]{:S(2)}, u32[]{:S(2)}) collective-permute-start(bf16[256,3072]{1,0:T(8,128)(2,1)S(1)} %bitcast.57), channel_id=1, source_target_pairs={{0,16},{16,0},{32,48},{48,32},{64,80},{80,64},{96,112},{112,96},{1... | collective-permute-start | bytes 4718600 | tf_op jit(solution)/shard_map/ppermute | solution.py:60
  95.7 0.0 copy-done
  95.7 0.6 fusion.21
  96.3 0.0 copy-start.3
  96.3 2.4 %collective-permute-done = bf16[256,3072]{1,0:T(8,128)(2,1)S(1)} collective-permute-done((bf16[256,3072]{1,0:T(8,128)(2,1)S(1)}, bf16[256,3072]{1,0:T(8,128)(2,1)S(1)}, u32[]{:S(2)}, u32[]{:S(2)}) %collective-permute-start) | collective-permute-done | bytes 1572896 | tf_op jit(solution)/shard_map/ppermute | solution.py:60
  98.7 0.6 broadcast_select_fusion.5
  99.3 0.2 multiply_convert_fusion.2
  99.5 0.0 copy-done.3
  99.5 0.4 convolution_convert_fusion.4
  99.9 0.0 copy-start.5
  99.9 2.3 %collective-permute-start.1 = (bf16[256,1536]{1,0:T(8,128)(2,1)S(1)}, bf16[256,1536]{1,0:T(8,128)(2,1)S(1)}, u32[]{:S(2)}, u32[]{:S(2)}) collective-permute-start(bf16[256,1536]{1,0:T(8,128)(2,1)S(1)} %convolution_convert_fusion.4), channel_id=1, source_target_pairs={{0,16},{16,0},{32,48},{48,32},{64,80},{80,64},{96,112},{112,96},{1... | collective-permute-start | bytes 2359304 | tf_op jit(solution)/shard_map/ppermute | solution.py:60
  102.2 1.9 %collective-permute-done.1 = bf16[256,1536]{1,0:T(8,128)(2,1)S(1)} collective-permute-done((bf16[256,1536]{1,0:T(8,128)(2,1)S(1)}, bf16[256,1536]{1,0:T(8,128)(2,1)S(1)}, u32[]{:S(2)}, u32[]{:S(2)}) %collective-permute-start.1) | collective-permute-done | bytes 786464 | tf_op jit(solution)/shard_map/ppermute | solution.py:60
  104.1 0.0 copy-done.2
  104.1 0.4 add_convert_fusion
  104.5 16.3 %all_to_all.26 = bf16[16,16,1536]{2,1,0:T(8,128)(2,1)S(1)} all-to-all(bf16[16,16,1536]{2,1,0:T(8,128)(2,1)S(1)} %bitcast.69), channel_id=1, replica_groups=mesh['dp'=64,'expert'=16] {'expert'}, dimensions={0} | all-to-all | bytes 1572864 | tf_op jit(solution)/shard_map/all_to_all | solution.py:17
  120.8 0.0 copy-done.5
  120.8 0.9 convolution_convert_fusion.5
  121.8 2.1 %reshape.132 = bf16[32,48,48]{1,0,2:T(8,128)(2,1)} reshape(bf16[1536,48]{0,1:T(8,128)(2,1)} %convolution_convert_fusion.5) | data formatting | bytes 294912 | tf_op jit(solution)/shard_map/reshape | solution.py:110
  123.8 1.9 %copy.82 = bf16[32,48,48]{1,2,0:T(8,128)(2,1)} copy(bf16[32,48,48]{1,0,2:T(8,128)(2,1)} %reshape.132) | data formatting | bytes 294912 | tf_op jit(solution)/shard_map/reshape | solution.py:110
  125.7 2.2 %reshape.135 = bf16[32,2,1152]{2,1,0:T(2,128)(2,1)} reshape(bf16[32,48,48]{2,1,0:T(8,128)(2,1)} %bitcast.75) | data formatting | bytes 294912
  127.9 21.3 %all-to-all-start.4 = ((bf16[32,2,1152]{2,1,0:T(2,128)(2,1)}), bf16[32,2,1152]{2,1,0:T(2,128)(2,1)}, u32[]{:S(2)}, u32[]{:S(2)}) async-start(bf16[32,2,1152]{2,1,0:T(2,128)(2,1)} %reshape.135), calls=%async_computation.4 | async-start | bytes 294912 | tf_op jit(solution)/shard_map/all_to_all | solution.py:17
  149.2 0.5 fusion.3
  149.7 0.5 fusion.4
  150.2 0.1 pad_maximum_fusion.2
  150.3 2.0 %copy.73 = bf16[1,2,84,3072]{3,1,2,0:T(2,128)(2,1)} copy(bf16[1,2,84,3072]{3,2,1,0:T(8,128)(2,1)S(1)} %pad_maximum_fusion.2) | data formatting | bytes 2064384
  152.3 1.4 fusion.5
  153.7 8.9 %all-to-all-done.4 = bf16[32,2,1152]{2,1,0:T(2,128)(2,1)} async-done(((bf16[32,2,1152]{2,1,0:T(2,128)(2,1)}), bf16[32,2,1152]{2,1,0:T(2,128)(2,1)}, u32[]{:S(2)}, u32[]{:S(2)}) %all-to-all-start.4) | async-done | bytes 147488 | tf_op jit(solution)/shard_map/all_to_all | solution.py:17
  162.6 1.3 reshape.136
  163.9 0.7 bitcast_reduce_fusion
  (17 shorter events, 0.1 us)
Async XLA Ops:
  0.6 38.7 %copy-start.1 = (bf16[1,2,84,3072]{3,1,2,0:T(2,128)(2,1)S(1)}, bf16[1,2,84,3072]{3,1,2,0:T(2,128)(2,1)}, u32[]{:S(2)}) copy-start(bf16[1,2,84,3072]{3,1,2,0:T(2,128)(2,1)} %param.10) | copy-start | bytes 3096580
  2.3 46.9 %all-to-all-start = ((bf16[16,2,1152]{2,1,0:T(2,128)(2,1)}), bf16[16,2,1152]{2,1,0:T(2,128)(2,1)S(1)}, u32[]{:S(2)}, u32[]{:S(2)}) async-start(bf16[16,2,1152]{2,1,0:T(2,128)(2,1)} %bitcast.4), calls=%async_computation | async-start | bytes 147456 | tf_op jit(solution)/shard_map/all_to_all | solution.py:17
  47.2 6.4 %copy-start.7 = (f32[48,4]{0,1:T(4,128)S(1)}, f32[48,4]{0,1:T(4,128)}, u32[]{:S(2)}) copy-start(f32[48,4]{0,1:T(4,128)} %param.9) | copy-start | bytes 2308
  47.2 6.6 %copy-start.6 = (s32[48,4]{0,1:T(4,128)S(1)}, s32[48,4]{0,1:T(4,128)}, u32[]{:S(2)}) copy-start(s32[48,4]{0,1:T(4,128)} %param.8) | copy-start | bytes 2308
  50.1 11.6 %all-to-all-start.1 = ((bf16[64,2,1152]{2,1,0:T(2,128)(2,1)}), bf16[64,2,1152]{2,1,0:T(2,128)(2,1)S(1)}, u32[]{:S(2)}, u32[]{:S(2)}) async-start(bf16[64,2,1152]{2,1,0:T(2,128)(2,1)} %bitcast.12), calls=%async_computation.1 | async-start | bytes 589824 | tf_op jit(solution)/shard_map/all_to_all | solution.py:17
  55.3 7.5 %copy-start.4 = (bf16[256,48]{0,1:T(8,128)(2,1)}, bf16[256,48]{0,1:T(8,128)(2,1)S(1)}, u32[]{:S(2)}) copy-start(bf16[256,48]{0,1:T(8,128)(2,1)S(1)} %convert_reduce_fusion) | copy-start | bytes 73732
  63.4 32.3 %copy-start = (bf16[252,3072]{0,1:T(8,128)(2,1)S(1)}, bf16[252,3072]{0,1:T(8,128)(2,1)}, u32[]{:S(2)}) copy-start(bf16[252,3072]{0,1:T(8,128)(2,1)} %pad_maximum_fusion.1) | copy-start | bytes 4644868
  89.6 9.1 %collective-permute-start = (bf16[256,3072]{1,0:T(8,128)(2,1)S(1)}, bf16[256,3072]{1,0:T(8,128)(2,1)S(1)}, u32[]{:S(2)}, u32[]{:S(2)}) collective-permute-start(bf16[256,3072]{1,0:T(8,128)(2,1)S(1)} %bitcast.57), channel_id=1, source_target_pairs={{0,16},{16,0},{32,48},{48,32},{64,80},{80,64},{96,112},{112,96},{1... | collective-permute-start | bytes 4718600 | tf_op jit(solution)/shard_map/ppermute | solution.py:60
  96.3 3.2 %copy-start.3 = (bf16[168,32,1,48]{0,3,2,1:T(8,128)(2,1)S(1)}, bf16[168,32,1,48]{0,3,2,1:T(8,128)(2,1)}, u32[]{:S(2)}) copy-start(bf16[168,32,1,48]{0,3,2,1:T(8,128)(2,1)} %get-tuple-element.30) | copy-start | bytes 1548292
  99.3 4.8 %copy-start.2 = (bf16[168,32,1,48]{0,3,2,1:T(8,128)(2,1)S(1)}, bf16[168,32,1,48]{0,3,2,1:T(8,128)(2,1)}, u32[]{:S(2)}) copy-start(bf16[168,32,1,48]{0,3,2,1:T(8,128)(2,1)} %get-tuple-element.31) | copy-start | bytes 1548292
  99.9 20.9 %copy-start.5 = (bf16[256,48]{0,1:T(8,128)(2,1)S(1)}, bf16[256,48]{0,1:T(8,128)(2,1)}, u32[]{:S(2)}) copy-start(bf16[256,48]{0,1:T(8,128)(2,1)} %copy-done.4) | copy-start | bytes 73732
  99.9 4.2 %collective-permute-start.1 = (bf16[256,1536]{1,0:T(8,128)(2,1)S(1)}, bf16[256,1536]{1,0:T(8,128)(2,1)S(1)}, u32[]{:S(2)}, u32[]{:S(2)}) collective-permute-start(bf16[256,1536]{1,0:T(8,128)(2,1)S(1)} %convolution_convert_fusion.4), channel_id=1, source_target_pairs={{0,16},{16,0},{32,48},{48,32},{64,80},{80,64},{96,112},{112,96},{1... | collective-permute-start | bytes 2359304 | tf_op jit(solution)/shard_map/ppermute | solution.py:60
  127.9 34.7 %all-to-all-start.4 = ((bf16[32,2,1152]{2,1,0:T(2,128)(2,1)}), bf16[32,2,1152]{2,1,0:T(2,128)(2,1)}, u32[]{:S(2)}, u32[]{:S(2)}) async-start(bf16[32,2,1152]{2,1,0:T(2,128)(2,1)} %reshape.135), calls=%async_computation.4 | async-start | bytes 294912 | tf_op jit(solution)/shard_map/all_to_all | solution.py:17

commit v3 on v2

--- a/solution.py
+++ b/solution.py
@@ -11,6 +11,9 @@
 
 def dot(left, right, contract):
     return lax.dot_general(left, right, (contract, ((), ())), preferred_element_type=F32)
+
+
+hold = lax.optimization_barrier
 
 
 def exchange(value, axis, groups=None):
@@ -59,37 +62,37 @@
     def swap_cores(value):
         return lax.ppermute(value, DP, [(i, i ^ 1) for i in range(dp)])
 
-    picker, slot_scale = slot_tables(routes, route_weights, experts, capacity)
-
     block = (2, feat * tok_count // 2)
-    both = lax.optimization_barrier(jnp.stack([tokens, cotangent]))
+    both = hold((jnp.stack([tokens, cotangent]),))[0]
     both = both.transpose(0, 2, 1).reshape(1, 2, *block)
     sent = jnp.broadcast_to(both, (far, 2, *block)).reshape(far * 2, *block)
     column = exchange(sent, DP, far_groups)
-
-    w_gate, w_up, w_down = gate_up[0, 0], gate_up[0, 1], down_proj[0]
-    hidden = w_gate.shape[0]
-    w_in = jnp.concatenate([w_gate, w_up])
-    w_all = jnp.concatenate([w_in, w_down])
-    by_core = jnp.roll(w_in.reshape(2 * hidden, depth, 2, feat), -turn * near, axis=1)
-    own_cols = jnp.where(core == 0, by_core[:, :, 0], by_core[:, :, 1]).reshape(2 * hidden, -1)
-    twin_cols = jnp.where(core == 0, by_core[:, :, 1], by_core[:, :, 0]).reshape(2 * hidden, -1)
-    column, w_all, own_cols, twin_cols = lax.optimization_barrier(
-        (column, w_all, own_cols, twin_cols)
-    )
+    picker, slot_scale = slot_tables(routes, route_weights, experts, capacity)
+    scale = jnp.where(core == 0, 1.0, slot_scale)
+    column, picker, scale, gate_up, down_proj = hold((column, picker, scale, gate_up, down_proj))
 
     column = jnp.broadcast_to(column[None], (near,) + column.shape).reshape(-1, *block)
     column = exchange(column, DP, near_groups)
+    w_gate, w_up, w_down = gate_up[0, 0], gate_up[0, 1], down_proj[0]
+    hidden = w_gate.shape[0]
+    w_all = jnp.concatenate([w_gate, w_up, w_down])
+    column, w_all = hold((column, w_all))
+
     column = column.reshape(near, far, 2, feat, tok_count)
     column = jnp.roll(column, turn, axis=1).transpose(1, 0, 2, 3, 4)
     column = with_layout_constraint(column.reshape(width, tok_count), Layout((0, 1)))
+    rows = dot(picker, column, LAST).astype(BF16)
+    rows = (scale[:, None] * rows.astype(F32)).astype(BF16)
+    rows, w_all = hold((rows, w_all))
+    held = exchange(rows.reshape(experts, capacity, width), EXPERT).reshape(slots, width)
+    by_core = w_all[: 2 * hidden].reshape(2 * hidden, depth, 2, feat)
+    by_core = jnp.roll(by_core, -turn * near, axis=1)
+    own_cols = jnp.where(core == 0, by_core[:, :, 0], by_core[:, :, 1]).reshape(2 * hidden, -1)
+    twin_cols = jnp.where(core == 0, by_core[:, :, 1], by_core[:, :, 0]).reshape(2 * hidden, -1)
+    held, own_cols, twin_cols = hold((held, own_cols, twin_cols))
 
-    rows = dot(picker, column, LAST).astype(BF16)
-    scale = jnp.where(core == 0, 1.0, slot_scale)
-    rows = (scale[:, None] * rows.astype(F32)).astype(BF16)
-    held = exchange(rows.reshape(experts, capacity, width), EXPERT).reshape(slots, width)
     twin = swap_cores(held)
-    from_held, twin = lax.optimization_barrier((dot(held, w_all, LAST), twin))
+    from_held, twin = hold((dot(held, w_all, LAST), twin))
     from_twin = dot(twin, w_all, LAST)
     full_x = jnp.where(core == 0, held, twin)
     full_dz = jnp.where(core == 0, twin, held)
@@ -106,12 +109,12 @@
     arrived = swap_cores(twin_part)
     share = (dot(grads, own_cols, INNER) + arrived.astype(F32)).astype(BF16)
     returned = exchange(share.reshape(experts, capacity, -1), EXPERT).reshape(slots, -1)
+    grad_in = jnp.stack([dot(grad_gate, full_x, FIRST), dot(grad_up, full_x, FIRST)]).astype(BF16)
+    grad_out = dot(activated, full_dz, FIRST).astype(BF16)
+    returned, grad_in, grad_out = hold((returned, grad_in, grad_out))
     summed = dot(returned, picker, FIRST).astype(BF16)
     pieces = exchange(summed.reshape(depth, feat, tok_count), DP, z_groups)
     grad_tokens = jnp.sum(pieces.astype(F32), axis=0).astype(BF16).T
-
-    grad_in = jnp.stack([dot(grad_gate, full_x, FIRST), dot(grad_up, full_x, FIRST)]).astype(BF16)
-    grad_out = dot(activated, full_dz, FIRST).astype(BF16)
     return grad_tokens, grad_in[None], grad_out[None]
 
 

time: 165 us -> 163 us (0.988)
  blocking collectives: 42.4 us -> 0 us
  waiting for transfers between devices: 19.5 us -> 52.8 us
  starting transfers between devices: 68.7 us -> 80.5 us
  local copies, waits for them, and re-layouts: 20.1 us -> 12.6 us
  matrix products: 5.86 us -> 9.21 us
    all_to_all x2 -> x0, blocking collectives: 42.4 us -> none  [exchange(): lax.all_to_all(value, axis, split_axis=0, concat_axis=0, tiled=True, axis...]
    all_to_all x3 -> x5, waiting for transfers between devices: 15.2 us -> 49.8 us  [exchange(): lax.all_to_all(value, axis, split_axis=0, concat_axis=0, tiled=True, axis...]
    all_to_all x3 -> x5, starting transfers between devices: 60.3 us -> 72 us  [exchange(): lax.all_to_all(value, axis, split_axis=0, concat_axis=0, tiled=True, axis...]
    unnamed x24 -> x21, local copies, waits for them, and re-layouts: 10.7 us -> 6.21 us
    reshape x2, local copies, waits for them, and re-layouts: 3.95 us -> 0.55 us  [on_device(): pieces = exchange(summed.reshape(depth, feat, tok_count), DP, z_groups)]
    dot_general x9, matrix products: 5.86 us -> 9.21 us  [dot(): lax.dot_general(left, right, (contract, ((), ())), preferred_element_type...]
    optimization_barrier x0 -> x2, local copies, waits for them, and re-layouts: none -> 2.46 us  [on_device(): hold((column, picker, scale, gate_up, down_proj))]
    slice x1, local copies, waits for them, and re-layouts: 2.26 us -> 0.1 us  [on_device(): by_core = jnp.roll(by_core, -turn * near, axis=1)]
  transfers between devices with their start and end apart: 5 -> 7, of which waited for: 4 -> 7; matrix products, arithmetic and copies ran while one was open for 11% -> 9% of each run, Pallas kernels for 0% -> 0%
where the time goes in v3:
time: 163 us; the launch traced here: 162 us
  starting transfers between devices  80.5 us (49%)
  waiting for transfers between devices  52.8 us (32%)
  local copies, waits for them, and re-layouts  12.6 us (8%)
  matrix products  9.21 us (6%)
  other arithmetic  6.05 us (4%)
    all_to_all x5, starting transfers between devices, exchange(): lax.all_to_all(value, axis, split_axis=0, concat_axis=0, tiled=True, axis...  72 us
    all_to_all x5, waiting for transfers between devices, exchange(): lax.all_to_all(value, axis, split_axis=0, concat_axis=0, tiled=True, axis...  49.8 us
    dot_general x9, matrix products, dot(): lax.dot_general(left, right, (contract, ((), ())), preferred_element_type...  9.21 us
    ppermute x2, starting transfers between devices, swap_cores(): return lax.ppermute(value, DP, [(i, i ^ 1) for i in range(dp)])  8.51 us
    unnamed x21, local copies, waits for them, and re-layouts  6.21 us
  transfers between devices with their start and end apart: 7, of which 7 were waited for; matrix products, arithmetic and copies ran while one was open for 9% of the time, Pallas kernels for 0%

profile of v3, /device:TPU:1, one launch (start us, length us, event | category | flops | bytes accessed | tf_op | source)
XLA Modules:
  0.0 162.1 jit_solution(7547558116077397792)
XLA Ops:
  0.6 0.0 copy-start.7
  0.6 0.0 copy-start.6
  0.7 0.8 pad_maximum_fusion.8
  1.5 0.1 copy.60
  1.6 0.1 broadcast_in_dim.14
  1.7 0.7 broadcast_in_dim.28
  2.4 35.5 %all-to-all-start = ((bf16[16,2,1152]{2,1,0:T(2,128)(2,1)}), bf16[16,2,1152]{2,1,0:T(2,128)(2,1)S(1)}, u32[]{:S(2)}, u32[]{:S(2)}) async-start(bf16[16,2,1152]{2,1,0:T(2,128)(2,1)} %bitcast.3), calls=%async_computation | async-start | bytes 147456 | tf_op jit(solution)/shard_map/all_to_all | solution.py:20
  37.9 0.8 copy.65
  38.7 0.1 mul.65
  38.8 0.8 copy.61
  39.5 0.1 eq.54
  39.7 0.6 reduce-window.6
  40.3 0.2 slice_reduce_fusion
  40.5 0.1 bitcast_bitcast_fusion
  40.6 0.1 reduce_sum.42
  40.7 0.1 copy.64
  40.8 0.7 multiply_add_fusion
  41.5 0.1 convert_reduce_fusion
  41.6 0.1 select_reduce_fusion
  41.7 3.9 %all-to-all-done = bf16[16,2,1152]{2,1,0:T(2,128)(2,1)S(1)} async-done(((bf16[16,2,1152]{2,1,0:T(2,128)(2,1)}), bf16[16,2,1152]{2,1,0:T(2,128)(2,1)S(1)}, u32[]{:S(2)}, u32[]{:S(2)}) %all-to-all-start) | async-done | bytes 73760 | tf_op jit(solution)/shard_map/all_to_all | solution.py:20
  45.7 0.9 broadcast_in_dim.30
  46.5 3.5 %all-to-all-start.1 = ((bf16[64,2,1152]{2,1,0:T(2,128)(2,1)}), bf16[64,2,1152]{2,1,0:T(2,128)(2,1)S(1)}, u32[]{:S(2)}, u32[]{:S(2)}) async-start(bf16[64,2,1152]{2,1,0:T(2,128)(2,1)} %bitcast.5), calls=%async_computation.1 | async-start | bytes 589824 | tf_op jit(solution)/shard_map/all_to_all | solution.py:20
  50.0 1.2 copy.68
  51.2 1.3 copy.66
  52.5 0.0 copy-start.4
  52.5 0.1 slice_bitcast_fusion.1
  52.6 1.0 copy-done.4
  53.6 0.9 pad_maximum_fusion
  54.5 5.1 %all-to-all-done.1 = bf16[64,2,1152]{2,1,0:T(2,128)(2,1)S(1)} async-done(((bf16[64,2,1152]{2,1,0:T(2,128)(2,1)}), bf16[64,2,1152]{2,1,0:T(2,128)(2,1)S(1)}, u32[]{:S(2)}, u32[]{:S(2)}) %all-to-all-start.1) | async-done | bytes 294944 | tf_op jit(solution)/shard_map/all_to_all | solution.py:20
  59.6 0.8 reshape.86
  60.4 0.1 fusion.16
  60.5 0.2 maximum_bitcast_fusion
  60.7 0.1 copy.69
  60.7 1.8 %fusion.2 = bf16[256,3072]{1,0:T(8,128)(2,1)} fusion(bf16[256,48]{0,1:T(8,128)(2,1)S(1)} %convert_reduce_fusion, bf16[3072,48]{1,0:T(8,128)(2,1)S(1)} %bitcast.68, f32[256]{0:T(256)S(1)} %broadcast_select_fusion.6), kind=kOutput, calls=%fused_computation.3 | convolution fusion | flops 78643200 | bytes 1893376 | tf_op jit(solution)/shard_map/dot_general | solution.py:13
  62.5 6.8 %all-to-all-start.2 = ((bf16[16,16,3072]{2,1,0:T(8,128)(2,1)}), bf16[16,16,3072]{2,1,0:T(8,128)(2,1)S(1)}, u32[]{:S(2)}, u32[]{:S(2)}) async-start(bf16[16,16,3072]{2,1,0:T(8,128)(2,1)} %bitcast.65), calls=%async_computation.2 | async-start | bytes 3145728 | tf_op jit(solution)/shard_map/all_to_all | solution.py:20
  69.3 0.1 fusion.15
  69.4 1.5 broadcast_select_fusion.1
  70.9 19.0 %all-to-all-done.2 = bf16[16,16,3072]{2,1,0:T(8,128)(2,1)S(1)} async-done(((bf16[16,16,3072]{2,1,0:T(8,128)(2,1)}), bf16[16,16,3072]{2,1,0:T(8,128)(2,1)S(1)}, u32[]{:S(2)}, u32[]{:S(2)}) %all-to-all-start.2) | async-done | bytes 1572896 | tf_op jit(solution)/shard_map/all_to_all | solution.py:20
  89.8 6.1 %collective-permute-start = (bf16[256,3072]{1,0:T(8,128)(2,1)S(1)}, bf16[256,3072]{1,0:T(8,128)(2,1)S(1)}, u32[]{:S(2)}, u32[]{:S(2)}) collective-permute-start(bf16[256,3072]{1,0:T(8,128)(2,1)S(1)} %bitcast.59), channel_id=1, source_target_pairs={{0,16},{16,0},{32,48},{48,32},{64,80},{80,64},{96,112},{112,96},{1... | collective-permute-start | bytes 4718600 | tf_op jit(solution)/shard_map/ppermute | solution.py:63
  95.9 0.6 fusion.17
  96.5 0.0 copy-start.3
  96.5 2.4 %collective-permute-done = bf16[256,3072]{1,0:T(8,128)(2,1)S(1)} collective-permute-done((bf16[256,3072]{1,0:T(8,128)(2,1)S(1)}, bf16[256,3072]{1,0:T(8,128)(2,1)S(1)}, u32[]{:S(2)}, u32[]{:S(2)}) %collective-permute-start) | collective-permute-done | bytes 1572896 | tf_op jit(solution)/shard_map/ppermute | solution.py:63
  98.9 0.6 broadcast_select_fusion.5
  99.5 0.2 multiply_convert_fusion.2
  99.7 0.4 convolution_convert_fusion.4
  100.1 0.0 copy-start.2
  100.2 2.4 %collective-permute-start.1 = (bf16[256,1536]{1,0:T(8,128)(2,1)S(1)}, bf16[256,1536]{1,0:T(8,128)(2,1)S(1)}, u32[]{:S(2)}, u32[]{:S(2)}) collective-permute-start(bf16[256,1536]{1,0:T(8,128)(2,1)S(1)} %convolution_convert_fusion.4), channel_id=1, source_target_pairs={{0,16},{16,0},{32,48},{48,32},{64,80},{80,64},{96,112},{112,96},{1... | collective-permute-start | bytes 2359304 | tf_op jit(solution)/shard_map/ppermute | solution.py:63
  102.6 1.3 fusion.3
  103.9 0.6 collective-permute-done.1
  104.5 1.3 add_convert_fusion
  105.8 4.3 %all-to-all-start.3 = ((bf16[16,16,1536]{2,1,0:T(8,128)(2,1)}), bf16[16,16,1536]{2,1,0:T(8,128)(2,1)}, u32[]{:S(2)}, u32[]{:S(2)}) async-start(bf16[16,16,1536]{2,1,0:T(8,128)(2,1)} %bitcast.67), calls=%async_computation.3 | async-start | bytes 1572864 | tf_op jit(solution)/shard_map/all_to_all | solution.py:20
  110.1 0.5 fusion.4
  110.6 1.4 convolution_convert_fusion.1
  112.0 0.1 pad_maximum_fusion.1
  112.1 10.8 %all-to-all-done.3 = bf16[16,16,1536]{2,1,0:T(8,128)(2,1)} async-done(((bf16[16,16,1536]{2,1,0:T(8,128)(2,1)}), bf16[16,16,1536]{2,1,0:T(8,128)(2,1)}, u32[]{:S(2)}, u32[]{:S(2)}) %all-to-all-start.3) | async-done | bytes 786464 | tf_op jit(solution)/shard_map/all_to_all | solution.py:20
  122.9 1.4 convolution_convert_fusion.5
  124.3 0.4 reshape.93
  124.7 0.2 copy.80
  124.8 1.2 reshape.96
  126.1 22.0 %all-to-all-start.4 = ((bf16[32,2,1152]{2,1,0:T(2,128)(2,1)}), bf16[32,2,1152]{2,1,0:T(2,128)(2,1)S(1)}, u32[]{:S(2)}, u32[]{:S(2)}) async-start(bf16[32,2,1152]{2,1,0:T(2,128)(2,1)} %reshape.96), calls=%async_computation.4 | async-start | bytes 294912 | tf_op jit(solution)/shard_map/all_to_all | solution.py:20
  148.0 2.0 %copy.73 = bf16[1,2,84,3072]{3,1,2,0:T(2,128)(2,1)} copy(bf16[1,2,84,3072]{3,2,1,0:T(8,128)(2,1)S(1)} %bitcast.66) | data formatting | bytes 2064384
  150.1 11.0 %all-to-all-done.4 = bf16[32,2,1152]{2,1,0:T(2,128)(2,1)S(1)} async-done(((bf16[32,2,1152]{2,1,0:T(2,128)(2,1)}), bf16[32,2,1152]{2,1,0:T(2,128)(2,1)S(1)}, u32[]{:S(2)}, u32[]{:S(2)}) %all-to-all-start.4) | async-done | bytes 147488 | tf_op jit(solution)/shard_map/all_to_all | solution.py:20
  161.1 0.4 reshape.97
  161.5 0.7 bitcast_reduce_fusion
  (17 shorter events, 0.1 us)
Async XLA Ops:
  0.6 49.4 %copy-start.7 = (bf16[1,84,3072]{2,1,0:T(8,128)(2,1)S(1)}, bf16[1,84,3072]{2,1,0:T(8,128)(2,1)}, u32[]{:S(2)}) copy-start(bf16[1,84,3072]{2,1,0:T(8,128)(2,1)} %param.11) | copy-start | bytes 1548292
  0.6 50.6 %copy-start.6 = (bf16[1,2,84,3072]{3,1,2,0:T(2,128)(2,1)S(1)}, bf16[1,2,84,3072]{3,1,2,0:T(2,128)(2,1)}, u32[]{:S(2)}) copy-start(bf16[1,2,84,3072]{3,1,2,0:T(2,128)(2,1)} %param.10) | copy-start | bytes 3096580
  2.4 43.3 %all-to-all-start = ((bf16[16,2,1152]{2,1,0:T(2,128)(2,1)}), bf16[16,2,1152]{2,1,0:T(2,128)(2,1)S(1)}, u32[]{:S(2)}, u32[]{:S(2)}) async-start(bf16[16,2,1152]{2,1,0:T(2,128)(2,1)} %bitcast.3), calls=%async_computation | async-start | bytes 147456 | tf_op jit(solution)/shard_map/all_to_all | solution.py:20
  46.5 13.1 %all-to-all-start.1 = ((bf16[64,2,1152]{2,1,0:T(2,128)(2,1)}), bf16[64,2,1152]{2,1,0:T(2,128)(2,1)S(1)}, u32[]{:S(2)}, u32[]{:S(2)}) async-start(bf16[64,2,1152]{2,1,0:T(2,128)(2,1)} %bitcast.5), calls=%async_computation.1 | async-start | bytes 589824 | tf_op jit(solution)/shard_map/all_to_all | solution.py:20
  52.5 1.1 copy-start.4
  62.5 27.3 %all-to-all-start.2 = ((bf16[16,16,3072]{2,1,0:T(8,128)(2,1)}), bf16[16,16,3072]{2,1,0:T(8,128)(2,1)S(1)}, u32[]{:S(2)}, u32[]{:S(2)}) async-start(bf16[16,16,3072]{2,1,0:T(8,128)(2,1)} %bitcast.65), calls=%async_computation.2 | async-start | bytes 3145728 | tf_op jit(solution)/shard_map/all_to_all | solution.py:20
  89.8 9.1 %collective-permute-start = (bf16[256,3072]{1,0:T(8,128)(2,1)S(1)}, bf16[256,3072]{1,0:T(8,128)(2,1)S(1)}, u32[]{:S(2)}, u32[]{:S(2)}) collective-permute-start(bf16[256,3072]{1,0:T(8,128)(2,1)S(1)} %bitcast.59), channel_id=1, source_target_pairs={{0,16},{16,0},{32,48},{48,32},{64,80},{80,64},{96,112},{112,96},{1... | collective-permute-start | bytes 4718600 | tf_op jit(solution)/shard_map/ppermute | solution.py:63
  96.5 3.2 %copy-start.3 = (bf16[168,32,1,48]{0,3,2,1:T(8,128)(2,1)S(1)}, bf16[168,32,1,48]{0,3,2,1:T(8,128)(2,1)}, u32[]{:S(2)}) copy-start(bf16[168,32,1,48]{0,3,2,1:T(8,128)(2,1)} %get-tuple-element.52) | copy-start | bytes 1548292
  98.9 3.6 %copy-start = (bf16[256,3072]{1,0:T(8,128)(2,1)}, bf16[256,3072]{1,0:T(8,128)(2,1)S(1)}, u32[]{:S(2)}) copy-start(bf16[256,3072]{1,0:T(8,128)(2,1)S(1)} %collective-permute-done) | copy-start | bytes 4718596
  100.1 4.3 %copy-start.2 = (bf16[168,32,1,48]{0,3,2,1:T(8,128)(2,1)S(1)}, bf16[168,32,1,48]{0,3,2,1:T(8,128)(2,1)}, u32[]{:S(2)}) copy-start(bf16[168,32,1,48]{0,3,2,1:T(8,128)(2,1)} %get-tuple-element.53) | copy-start | bytes 1548292
  100.2 4.3 %collective-permute-start.1 = (bf16[256,1536]{1,0:T(8,128)(2,1)S(1)}, bf16[256,1536]{1,0:T(8,128)(2,1)S(1)}, u32[]{:S(2)}, u32[]{:S(2)}) collective-permute-start(bf16[256,1536]{1,0:T(8,128)(2,1)S(1)} %convolution_convert_fusion.4), channel_id=1, source_target_pairs={{0,16},{16,0},{32,48},{48,32},{64,80},{80,64},{96,112},{112,96},{1... | collective-permute-start | bytes 2359304 | tf_op jit(solution)/shard_map/ppermute | solution.py:63
  103.9 6.2 %copy-start.1 = (bf16[256,3072]{1,0:T(8,128)(2,1)S(1)}, bf16[256,3072]{1,0:T(8,128)(2,1)}, u32[]{:S(2)}) copy-start(bf16[256,3072]{1,0:T(8,128)(2,1)} %copy-done) | copy-start | bytes 4718596
  105.8 17.1 %all-to-all-start.3 = ((bf16[16,16,1536]{2,1,0:T(8,128)(2,1)}), bf16[16,16,1536]{2,1,0:T(8,128)(2,1)}, u32[]{:S(2)}, u32[]{:S(2)}) async-start(bf16[16,16,1536]{2,1,0:T(8,128)(2,1)} %bitcast.67), calls=%async_computation.3 | async-start | bytes 1572864 | tf_op jit(solution)/shard_map/all_to_all | solution.py:20
  110.6 1.4 copy-start.5
  126.1 35.0 %all-to-all-start.4 = ((bf16[32,2,1152]{2,1,0:T(2,128)(2,1)}), bf16[32,2,1152]{2,1,0:T(2,128)(2,1)S(1)}, u32[]{:S(2)}, u32[]{:S(2)}) async-start(bf16[32,2,1152]{2,1,0:T(2,128)(2,1)} %reshape.96), calls=%async_computation.4 | async-start | bytes 294912 | tf_op jit(solution)/shard_map/all_to_all | solution.py:20

commit v4 on v3

--- a/solution.py
+++ b/solution.py
@@ -6,11 +6,11 @@
 
 DP, EXPERT = "dp", "expert"
 F32, BF16 = jnp.float32, jnp.bfloat16
-LAST, FIRST, INNER = ((1,), (1,)), ((0,), (0,)), ((1,), (0,))
+LAST, FIRST = ((1,), (1,)), ((0,), (0,))
 
 
-def dot(left, right, contract):
-    return lax.dot_general(left, right, (contract, ((), ())), preferred_element_type=F32)
+def dot(left, right, contract, batch=((), ())):
+    return lax.dot_general(left, right, (contract, batch), preferred_element_type=F32)
 
 
 hold = lax.optimization_barrier
@@ -43,7 +43,8 @@
     depth = dp // 2
     near = 4 if depth % 4 == 0 else 1
     far = depth // near
-    core = lax.axis_index(DP) % 2
+    pairs = depth // 2
+    core = lax.axis_index(DP) & 1
     tok_count, top_count = routes.shape
     feat = tokens.shape[1]
     width = feat * dp
@@ -52,12 +53,17 @@
 
     turn = far // 2
     far_order = [(j + turn) % far for j in range(far)]
-    z_order = [f * near + n for f in far_order for n in range(near)]
     far_groups = [[(f * near + n) * 2 + c for f in far_order for c in (0, 1)] for n in range(near)]
     near_groups = [
         [(f * near + n) * 2 + c for n in range(near)] for f in range(far) for c in (0, 1)
     ]
-    z_groups = [[z * 2 + c for z in z_order] for c in (0, 1)]
+    half_order = [(j + pairs // 2) % pairs for j in range(pairs)]
+    half_groups = [[(j * 2 + p) * 2 + c for j in half_order] for p in (0, 1) for c in (0, 1)]
+    pair_groups = [
+        [((j * 2 + p) * 2 + c) * experts + e for p in (0, 1) for e in range(experts)]
+        for j in range(pairs)
+        for c in (0, 1)
+    ]
 
     def swap_cores(value):
         return lax.ppermute(value, DP, [(i, i ^ 1) for i in range(dp)])
@@ -76,21 +82,19 @@
     w_gate, w_up, w_down = gate_up[0, 0], gate_up[0, 1], down_proj[0]
     hidden = w_gate.shape[0]
     w_all = jnp.concatenate([w_gate, w_up, w_down])
-    column, w_all = hold((column, w_all))
+    by_core = w_all[: 2 * hidden].reshape(2 * hidden, pairs, 2, 2, feat)
+    by_core = jnp.roll(by_core, -(pairs // 2), axis=1).transpose(3, 2, 0, 1, 4)
+    by_core = by_core.reshape(2, 2, 2 * hidden, pairs * feat)
+    own_cols = jnp.where(core == 0, by_core[0], by_core[1])
+    twin_cols = jnp.where(core == 0, by_core[1], by_core[0])
+    column, w_all, own_cols, twin_cols = hold((column, w_all, own_cols, twin_cols))
 
     column = column.reshape(near, far, 2, feat, tok_count)
     column = jnp.roll(column, turn, axis=1).transpose(1, 0, 2, 3, 4)
     column = with_layout_constraint(column.reshape(width, tok_count), Layout((0, 1)))
     rows = dot(picker, column, LAST).astype(BF16)
     rows = (scale[:, None] * rows.astype(F32)).astype(BF16)
-    rows, w_all = hold((rows, w_all))
     held = exchange(rows.reshape(experts, capacity, width), EXPERT).reshape(slots, width)
-    by_core = w_all[: 2 * hidden].reshape(2 * hidden, depth, 2, feat)
-    by_core = jnp.roll(by_core, -turn * near, axis=1)
-    own_cols = jnp.where(core == 0, by_core[:, :, 0], by_core[:, :, 1]).reshape(2 * hidden, -1)
-    twin_cols = jnp.where(core == 0, by_core[:, :, 1], by_core[:, :, 0]).reshape(2 * hidden, -1)
-    held, own_cols, twin_cols = hold((held, own_cols, twin_cols))
-
     twin = swap_cores(held)
     from_held, twin = hold((dot(held, w_all, LAST), twin))
     from_twin = dot(twin, w_all, LAST)
@@ -105,15 +109,19 @@
     grad_up = (back_grad * gate_part * sig_gate).astype(BF16)
 
     grads = jnp.concatenate([grad_gate, grad_up], axis=1)
-    twin_part = dot(grads, twin_cols, INNER).astype(BF16)
+    grads = jnp.broadcast_to(grads[None], (2,) + grads.shape)
+    twin_part = dot(grads, twin_cols, ((2,), (1,)), ((0,), (0,))).astype(BF16)
     arrived = swap_cores(twin_part)
-    share = (dot(grads, own_cols, INNER) + arrived.astype(F32)).astype(BF16)
-    returned = exchange(share.reshape(experts, capacity, -1), EXPERT).reshape(slots, -1)
+    share = dot(grads, own_cols, ((2,), (1,)), ((0,), (0,))) + arrived.astype(F32)
+    share = share.astype(BF16)
+    share, grad_gate, grad_up, activated = hold((share, grad_gate, grad_up, activated))
+    share = share.reshape(2 * experts, capacity, -1)
+    returned = exchange(share, (DP, EXPERT), pair_groups).reshape(2 * slots, -1)
     grad_in = jnp.stack([dot(grad_gate, full_x, FIRST), dot(grad_up, full_x, FIRST)]).astype(BF16)
     grad_out = dot(activated, full_dz, FIRST).astype(BF16)
     returned, grad_in, grad_out = hold((returned, grad_in, grad_out))
-    summed = dot(returned, picker, FIRST).astype(BF16)
-    pieces = exchange(summed.reshape(depth, feat, tok_count), DP, z_groups)
+    summed = dot(returned, jnp.concatenate([picker, picker]), FIRST).astype(BF16)
+    pieces = exchange(summed.reshape(pairs, feat, tok_count), DP, half_groups)
     grad_tokens = jnp.sum(pieces.astype(F32), axis=0).astype(BF16).T
     return grad_tokens, grad_in[None], grad_out[None]
 

time: 163 us -> 155 us (0.951)
  waiting for transfers between devices: 52.8 us -> 22.3 us
  blocking collectives: 0 us -> 28.1 us
  starting transfers between devices: 80.5 us -> 71.7 us
    all_to_all x5 -> x4, waiting for transfers between devices: 49.8 us -> 18 us  [exchange(): lax.all_to_all(value, axis, split_axis=0, concat_axis=0, tiled=True, axis...]
    all_to_all x0 -> x1, blocking collectives: none -> 28.1 us  [exchange(): lax.all_to_all(value, axis, split_axis=0, concat_axis=0, tiled=True, axis...]
    all_to_all x5 -> x4, starting transfers between devices: 72 us -> 65.2 us  [exchange(): lax.all_to_all(value, axis, split_axis=0, concat_axis=0, tiled=True, axis...]
    ppermute x2, starting transfers between devices: 8.51 us -> 6.45 us  [swap_cores(): return lax.ppermute(value, DP, [(i, i ^ 1) for i in range(dp)])]
    select_n x0 -> x2, local copies, waits for them, and re-layouts: none -> 1.87 us  [the longest x1 0.94 us: on_device(): own_cols = jnp.where(core == 0, by_core[0], by_core[1])]
    unnamed x21 -> x13, local copies, waits for them, and re-layouts: 6.21 us -> 5.04 us
  transfers between devices with their start and end apart: 7 -> 6, of which waited for: 7 -> 6; matrix products, arithmetic and copies ran while one was open for 9% -> 11% of each run, Pallas kernels for 0% -> 0%
where the time goes in v4:
time: 155 us; the launch traced here: 153 us
  starting transfers between devices  71.7 us (46%)
  blocking collectives  28.1 us (18%)
  waiting for transfers between devices  22.3 us (14%)
  local copies, waits for them, and re-layouts  14 us (9%)
  matrix products  8.36 us (5%)
  other arithmetic  7.25 us (5%)
    all_to_all x4, starting transfers between devices, exchange(): lax.all_to_all(value, axis, split_axis=0, concat_axis=0, tiled=True, axis...  65.2 us
    all_to_all x1, blocking collectives, exchange(): lax.all_to_all(value, axis, split_axis=0, concat_axis=0, tiled=True, axis...  28.1 us
    all_to_all x4, waiting for transfers between devices, exchange(): lax.all_to_all(value, axis, split_axis=0, concat_axis=0, tiled=True, axis...  18 us
    dot_general x9, matrix products, dot(): lax.dot_general(left, right, (contract, batch), preferred_element_type=F32)  8.36 us
    ppermute x2, starting transfers between devices, swap_cores(): return lax.ppermute(value, DP, [(i, i ^ 1) for i in range(dp)])  6.45 us
    unnamed x13, local copies, waits for them, and re-layouts  5.04 us
    ppermute x2, waiting for transfers between devices, swap_cores(): return lax.ppermute(value, DP, [(i, i ^ 1) for i in range(dp)])  4.32 us
    optimization_barrier x2, local copies, waits for them, and re-layouts, on_device(): hold((column, picker, scale, gate_up, down_proj))  3.16 us
  transfers between devices with their start and end apart: 6, of which 6 were waited for; matrix products, arithmetic and copies ran while one was open for 11% of the time, Pallas kernels for 0%

profile of v4, /device:TPU:1, one launch (start us, length us, event | category | flops | bytes accessed | tf_op | source)
XLA Modules:
  0.0 152.7 jit_solution(16326138416892249955)
XLA Ops:
  0.6 0.8 pad_maximum_fusion.4
  1.4 0.1 copy.78
  1.5 0.1 broadcast_in_dim.16
  1.6 0.7 broadcast_in_dim.17
  2.3 35.5 %all-to-all-start = ((bf16[16,2,1152]{2,1,0:T(2,128)(2,1)}), bf16[16,2,1152]{2,1,0:T(2,128)(2,1)S(1)}, u32[]{:S(2)}, u32[]{:S(2)}) async-start(bf16[16,2,1152]{2,1,0:T(2,128)(2,1)} %bitcast.3), calls=%async_computation | async-start | bytes 147456 | tf_op jit(solution)/shard_map/all_to_all | solution.py:20
  37.8 0.8 copy.83
  38.6 0.1 mul.65
  38.7 0.8 copy.79
  39.5 0.1 eq.52
  39.6 0.6 reduce-window.6
  40.2 0.2 slice_reduce_fusion
  40.4 0.1 bitcast_bitcast_fusion
  40.5 0.1 reduce_sum.42
  40.6 0.1 copy.82
  40.7 0.7 multiply_add_fusion
  41.4 0.1 convert_reduce_fusion
  41.5 0.1 select_reduce_fusion
  41.7 3.9 %all-to-all-done = bf16[16,2,1152]{2,1,0:T(2,128)(2,1)S(1)} async-done(((bf16[16,2,1152]{2,1,0:T(2,128)(2,1)}), bf16[16,2,1152]{2,1,0:T(2,128)(2,1)S(1)}, u32[]{:S(2)}, u32[]{:S(2)}) %all-to-all-start) | async-done | bytes 73760 | tf_op jit(solution)/shard_map/all_to_all | solution.py:20
  45.6 0.9 broadcast_in_dim.36
  46.5 3.5 %all-to-all-start.1 = ((bf16[64,2,1152]{2,1,0:T(2,128)(2,1)}), bf16[64,2,1152]{2,1,0:T(2,128)(2,1)S(1)}, u32[]{:S(2)}, u32[]{:S(2)}) async-start(bf16[64,2,1152]{2,1,0:T(2,128)(2,1)} %bitcast.5), calls=%async_computation.1 | async-start | bytes 589824 | tf_op jit(solution)/shard_map/all_to_all | solution.py:20
  49.9 0.4 copy.86
  50.3 2.8 %copy.84 = bf16[1,2,84,3072]{2,3,1,0:T(8,128)(2,1)S(1)} copy(bf16[1,2,84,3072]{3,1,2,0:T(2,128)(2,1)} %param.10) | data formatting | bytes 2064384 | tf_op jit(solution)/shard_map/optimization_barrier | solution.py:78
  53.1 0.4 fusion.21
  53.5 0.3 fusion.9
  53.9 0.5 fusion.6
  54.4 0.1 broadcast_select_fusion.1
  54.5 0.9 copy.88
  55.4 0.9 copy.87
  56.3 2.0 %pad_maximum_fusion.1 = bf16[252,3072]{0,1:T(8,128)(2,1)} fusion(bf16[84,3072]{0,1:T(8,128)(2,1)S(1)} %bitcast.76, bf16[84,3072]{0,1:T(8,128)(2,1)S(1)} %get-tuple-element.58, bf16[84,3072]{0,1:T(8,128)(2,1)S(1)} %get-tuple-element.57), kind=kLoop, calls=%fused_computation.12 | loop fusion | flops 4644864 | bytes 3096576 | tf_op jit(solution)/shard_map/concatenate | solution.py:84
  58.4 1.2 all-to-all-done.1
  59.6 0.8 reshape.88
  60.4 0.1 fusion.22
  60.4 0.2 maximum_bitcast_fusion
  60.6 0.1 copy.89
  60.7 0.6 fusion.2
  61.3 28.1 %all_to_all.25 = bf16[16,16,3072]{2,1,0:T(8,128)(2,1)S(1)} all-to-all(bf16[16,16,3072]{2,1,0:T(8,128)(2,1)S(1)} %bitcast.70), channel_id=1, replica_groups=mesh['dp'=64,'expert'=16] {'expert'}, dimensions={0} | all-to-all | bytes 3145728 | tf_op jit(solution)/shard_map/all_to_all | solution.py:20
  89.4 4.2 %collective-permute-start = (bf16[256,3072]{1,0:T(8,128)(2,1)S(1)}, bf16[256,3072]{1,0:T(8,128)(2,1)S(1)}, u32[]{:S(2)}, u32[]{:S(2)}) collective-permute-start(bf16[256,3072]{1,0:T(8,128)(2,1)S(1)} %bitcast.61), channel_id=1, source_target_pairs={{0,16},{16,0},{32,48},{48,32},{64,80},{80,64},{96,112},{112,96},{1... | collective-permute-start | bytes 4718600 | tf_op jit(solution)/shard_map/ppermute | solution.py:69
  93.6 0.6 fusion.23
  94.2 2.4 %collective-permute-done = bf16[256,3072]{1,0:T(8,128)(2,1)S(1)} collective-permute-done((bf16[256,3072]{1,0:T(8,128)(2,1)S(1)}, bf16[256,3072]{1,0:T(8,128)(2,1)S(1)}, u32[]{:S(2)}, u32[]{:S(2)}) %collective-permute-start) | collective-permute-done | bytes 1572896 | tf_op jit(solution)/shard_map/ppermute | solution.py:69
  96.6 0.6 broadcast_select_fusion.5
  97.2 0.8 multiply_convert_fusion.2
  98.0 0.1 pad_maximum_fusion.3
  98.1 0.1 copy.92
  98.2 1.6 %convolution_convert_fusion.4 = bf16[2,256,768]{2,1,0:T(8,128)(2,1)S(1)} fusion(bf16[2,168,768]{1,2,0:T(8,128)(2,1)} %bitcast.72, bf16[256,168]{0,1:T(8,128)(2,1)S(1)} %copy.92), kind=kOutput, calls=%fused_computation.19 | convolution fusion | flops 132513792 | bytes 1388544 | tf_op jit(solution)/shard_map/dot_general | solution.py:13
  99.8 2.3 %collective-permute-start.1 = (bf16[2,256,768]{2,1,0:T(8,128)(2,1)S(1)}, bf16[2,256,768]{2,1,0:T(8,128)(2,1)S(1)}, u32[]{:S(2)}, u32[]{:S(2)}) collective-permute-start(bf16[2,256,768]{2,1,0:T(8,128)(2,1)S(1)} %convolution_convert_fusion.4), channel_id=1, source_target_pairs={{0,16},{16,0},{32,48},{48,32},{64,80},{80,64},{96,112},{112,96},{1... | collective-permute-start | bytes 2359304 | tf_op jit(solution)/shard_map/ppermute | solution.py:69
  102.1 1.9 %collective-permute-done.1 = bf16[2,256,768]{2,1,0:T(8,128)(2,1)S(1)} collective-permute-done((bf16[2,256,768]{2,1,0:T(8,128)(2,1)S(1)}, bf16[2,256,768]{2,1,0:T(8,128)(2,1)S(1)}, u32[]{:S(2)}, u32[]{:S(2)}) %collective-permute-start.1) | collective-permute-done | bytes 786464 | tf_op jit(solution)/shard_map/ppermute | solution.py:69
  104.0 1.3 add_convert_fusion
  105.3 4.6 %all-to-all-start.3 = ((bf16[32,16,768]{2,1,0:T(8,128)(2,1)}), bf16[32,16,768]{2,1,0:T(8,128)(2,1)}, u32[]{:S(2)}, u32[]{:S(2)}) async-start(bf16[32,16,768]{2,1,0:T(8,128)(2,1)} %bitcast.74), calls=%async_computation.3 | async-start | bytes 1572864 | tf_op jit(solution)/shard_map/all_to_all | solution.py:20
  110.0 0.5 fusion.3
  110.5 0.0 copy-start.3
  110.5 0.5 fusion.4
  111.0 0.4 copy-done.3
  111.3 1.3 convolution_convert_fusion.1
  112.6 0.1 pad_maximum_fusion.2
  112.7 10.1 %all-to-all-done.3 = bf16[32,16,768]{2,1,0:T(8,128)(2,1)} async-done(((bf16[32,16,768]{2,1,0:T(8,128)(2,1)}), bf16[32,16,768]{2,1,0:T(8,128)(2,1)}, u32[]{:S(2)}, u32[]{:S(2)}) %all-to-all-start.3) | async-done | bytes 786464 | tf_op jit(solution)/shard_map/all_to_all | solution.py:20
  122.8 1.4 convolution_convert_fusion.5
  124.2 0.2 reshape.94
  124.4 0.1 copy.105
  124.4 0.9 reshape.97
  125.3 21.6 %all-to-all-start.4 = ((bf16[16,2,1152]{2,1,0:T(2,128)(2,1)}), bf16[16,2,1152]{2,1,0:T(2,128)(2,1)S(1)}, u32[]{:S(2)}, u32[]{:S(2)}) async-start(bf16[16,2,1152]{2,1,0:T(2,128)(2,1)} %reshape.97), calls=%async_computation.4 | async-start | bytes 147456 | tf_op jit(solution)/shard_map/all_to_all | solution.py:20
  147.0 2.0 %copy.96 = bf16[1,2,84,3072]{3,1,2,0:T(2,128)(2,1)} copy(bf16[1,2,84,3072]{3,2,1,0:T(8,128)(2,1)S(1)} %bitcast.71) | data formatting | bytes 2064384
  149.0 2.8 %all-to-all-done.4 = bf16[16,2,1152]{2,1,0:T(2,128)(2,1)S(1)} async-done(((bf16[16,2,1152]{2,1,0:T(2,128)(2,1)}), bf16[16,2,1152]{2,1,0:T(2,128)(2,1)S(1)}, u32[]{:S(2)}, u32[]{:S(2)}) %all-to-all-start.4) | async-done | bytes 73760 | tf_op jit(solution)/shard_map/all_to_all | solution.py:20
  151.8 0.2 reshape.98
  152.0 0.6 bitcast_reduce_fusion
  (13 shorter events, 0.1 us)
Async XLA Ops:
  0.6 49.3 %copy-start.2 = (bf16[1,84,3072]{2,1,0:T(8,128)(2,1)S(1)}, bf16[1,84,3072]{2,1,0:T(8,128)(2,1)}, u32[]{:S(2)}) copy-start(bf16[1,84,3072]{2,1,0:T(8,128)(2,1)} %param.11) | copy-start | bytes 1548292
  2.3 43.3 %all-to-all-start = ((bf16[16,2,1152]{2,1,0:T(2,128)(2,1)}), bf16[16,2,1152]{2,1,0:T(2,128)(2,1)S(1)}, u32[]{:S(2)}, u32[]{:S(2)}) async-start(bf16[16,2,1152]{2,1,0:T(2,128)(2,1)} %bitcast.3), calls=%async_computation | async-start | bytes 147456 | tf_op jit(solution)/shard_map/all_to_all | solution.py:20
  46.5 13.1 %all-to-all-start.1 = ((bf16[64,2,1152]{2,1,0:T(2,128)(2,1)}), bf16[64,2,1152]{2,1,0:T(2,128)(2,1)S(1)}, u32[]{:S(2)}, u32[]{:S(2)}) async-start(bf16[64,2,1152]{2,1,0:T(2,128)(2,1)} %bitcast.5), calls=%async_computation.1 | async-start | bytes 589824 | tf_op jit(solution)/shard_map/all_to_all | solution.py:20
  61.3 32.3 %copy-start = (bf16[252,3072]{0,1:T(8,128)(2,1)S(1)}, bf16[252,3072]{0,1:T(8,128)(2,1)}, u32[]{:S(2)}) copy-start(bf16[252,3072]{0,1:T(8,128)(2,1)} %pad_maximum_fusion.1) | copy-start | bytes 4644868
  89.4 7.2 %collective-permute-start = (bf16[256,3072]{1,0:T(8,128)(2,1)S(1)}, bf16[256,3072]{1,0:T(8,128)(2,1)S(1)}, u32[]{:S(2)}, u32[]{:S(2)}) collective-permute-start(bf16[256,3072]{1,0:T(8,128)(2,1)S(1)} %bitcast.61), channel_id=1, source_target_pairs={{0,16},{16,0},{32,48},{48,32},{64,80},{80,64},{96,112},{112,96},{1... | collective-permute-start | bytes 4718600 | tf_op jit(solution)/shard_map/ppermute | solution.py:69
  98.2 5.8 %copy-start.1 = (bf16[1,2,168,16,48]{2,4,3,1,0:T(8,128)(2,1)S(1)}, bf16[1,2,168,16,48]{2,4,3,1,0:T(8,128)(2,1)}, u32[]{:S(2)}) copy-start(bf16[1,2,168,16,48]{2,4,3,1,0:T(8,128)(2,1)} %copy.87) | copy-start | bytes 1548292
  99.8 4.2 %collective-permute-start.1 = (bf16[2,256,768]{2,1,0:T(8,128)(2,1)S(1)}, bf16[2,256,768]{2,1,0:T(8,128)(2,1)S(1)}, u32[]{:S(2)}, u32[]{:S(2)}) collective-permute-start(bf16[2,256,768]{2,1,0:T(8,128)(2,1)S(1)} %convolution_convert_fusion.4), channel_id=1, source_target_pairs={{0,16},{16,0},{32,48},{48,32},{64,80},{80,64},{96,112},{112,96},{1... | collective-permute-start | bytes 2359304 | tf_op jit(solution)/shard_map/ppermute | solution.py:69
  105.3 17.4 %all-to-all-start.3 = ((bf16[32,16,768]{2,1,0:T(8,128)(2,1)}), bf16[32,16,768]{2,1,0:T(8,128)(2,1)}, u32[]{:S(2)}, u32[]{:S(2)}) async-start(bf16[32,16,768]{2,1,0:T(8,128)(2,1)} %bitcast.74), calls=%async_computation.3 | async-start | bytes 1572864 | tf_op jit(solution)/shard_map/all_to_all | solution.py:20
  110.5 0.8 copy-start.3
  125.3 26.5 %all-to-all-start.4 = ((bf16[16,2,1152]{2,1,0:T(2,128)(2,1)}), bf16[16,2,1152]{2,1,0:T(2,128)(2,1)S(1)}, u32[]{:S(2)}, u32[]{:S(2)}) async-start(bf16[16,2,1152]{2,1,0:T(2,128)(2,1)} %reshape.97), calls=%async_computation.4 | async-start | bytes 147456 | tf_op jit(solution)/shard_map/all_to_all | solution.py:20

commit v5 on v4

--- a/solution.py
+++ b/solution.py
@@ -72,22 +72,17 @@
     both = hold((jnp.stack([tokens, cotangent]),))[0]
     both = both.transpose(0, 2, 1).reshape(1, 2, *block)
     sent = jnp.broadcast_to(both, (far, 2, *block)).reshape(far * 2, *block)
+    sent, gate_up, down_proj = hold((sent, gate_up, down_proj))
     column = exchange(sent, DP, far_groups)
+    w_in = jnp.concatenate([gate_up[0, 0], gate_up[0, 1]])
+    w_in, w_down = with_layout_constraint(w_in, Layout((0, 1))), down_proj[0]
     picker, slot_scale = slot_tables(routes, route_weights, experts, capacity)
     scale = jnp.where(core == 0, 1.0, slot_scale)
-    column, picker, scale, gate_up, down_proj = hold((column, picker, scale, gate_up, down_proj))
+    column, picker, scale, w_in, w_down = hold((column, picker, scale, w_in, w_down))
 
     column = jnp.broadcast_to(column[None], (near,) + column.shape).reshape(-1, *block)
     column = exchange(column, DP, near_groups)
-    w_gate, w_up, w_down = gate_up[0, 0], gate_up[0, 1], down_proj[0]
-    hidden = w_gate.shape[0]
-    w_all = jnp.concatenate([w_gate, w_up, w_down])
-    by_core = w_all[: 2 * hidden].reshape(2 * hidden, pairs, 2, 2, feat)
-    by_core = jnp.roll(by_core, -(pairs // 2), axis=1).transpose(3, 2, 0, 1, 4)
-    by_core = by_core.reshape(2, 2, 2 * hidden, pairs * feat)
-    own_cols = jnp.where(core == 0, by_core[0], by_core[1])
-    twin_cols = jnp.where(core == 0, by_core[1], by_core[0])
-    column, w_all, own_cols, twin_cols = hold((column, w_all, own_cols, twin_cols))
+    twin_in, twin_down = swap_cores(w_in), swap_cores(w_down)
 
     column = column.reshape(near, far, 2, feat, tok_count)
     column = jnp.roll(column, turn, axis=1).transpose(1, 0, 2, 3, 4)
@@ -95,30 +90,53 @@
     rows = dot(picker, column, LAST).astype(BF16)
     rows = (scale[:, None] * rows.astype(F32)).astype(BF16)
     held = exchange(rows.reshape(experts, capacity, width), EXPERT).reshape(slots, width)
-    twin = swap_cores(held)
-    from_held, twin = hold((dot(held, w_all, LAST), twin))
-    from_twin = dot(twin, w_all, LAST)
-    full_x = jnp.where(core == 0, held, twin)
-    full_dz = jnp.where(core == 0, twin, held)
-    from_x = jnp.where(core == 0, from_held, from_twin)
-    gate_part, up_part = from_x[:, :hidden], from_x[:, hidden : 2 * hidden]
-    back_grad = jnp.where(core == 0, from_twin, from_held)[:, 2 * hidden :]
+
+    hidden = w_down.shape[0]
+    own = (w_in[:hidden], w_in[hidden:], w_down)
+    twin = (twin_in[:hidden], twin_in[hidden:], twin_down)
+    unit = 2 * hidden
+    w_chip = jnp.where(
+        core == 0,
+        jnp.concatenate([own[0], twin[0], own[1], twin[1]]),
+        jnp.concatenate([twin[2], own[2], twin[2], own[2]]),
+    )
+    columns = [
+        array.reshape(hidden, pairs, 2, 2, feat)[:, :, :, c]
+        for array, c in (
+            [(own[0], 0), (twin[0], 0), (own[1], 0), (twin[1], 0)]
+            + [(twin[0], 1), (own[0], 1), (twin[1], 1), (own[1], 1)]
+        )
+    ]
+    columns = jnp.where(core == 0, jnp.concatenate(columns[:4]), jnp.concatenate(columns[4:]))
+    columns = jnp.roll(columns, -(pairs // 2), axis=1).transpose(0, 2, 1, 3)
+    columns = columns.reshape(2 * unit, 2 * pairs * feat)
+    held, w_chip, columns = hold((held, w_chip, columns))
+
+    mine = dot(w_chip, held, LAST)
+    theirs = swap_cores(mine)
+    gate_up_part = jnp.where(core == 0, mine, theirs)
+    gate_part, up_part = gate_up_part[:unit], gate_up_part[unit:]
+    back_grad = jnp.where(core == 0, theirs, mine)[:unit]
     sig_gate = jax.nn.sigmoid(gate_part)
     activated = (gate_part * sig_gate * up_part).astype(BF16)
     grad_gate = (back_grad * up_part * sig_gate * (1.0 + gate_part * (1.0 - sig_gate))).astype(BF16)
     grad_up = (back_grad * gate_part * sig_gate).astype(BF16)
 
-    grads = jnp.concatenate([grad_gate, grad_up], axis=1)
-    grads = jnp.broadcast_to(grads[None], (2,) + grads.shape)
-    twin_part = dot(grads, twin_cols, ((2,), (1,)), ((0,), (0,))).astype(BF16)
-    arrived = swap_cores(twin_part)
-    share = dot(grads, own_cols, ((2,), (1,)), ((0,), (0,))) + arrived.astype(F32)
-    share = share.astype(BF16)
-    share, grad_gate, grad_up, activated = hold((share, grad_gate, grad_up, activated))
+    share = dot(jnp.concatenate([grad_gate, grad_up]), columns, FIRST).astype(BF16)
+    share = share.reshape(slots, 2, -1).transpose(1, 0, 2)
+    share, grad_gate, grad_up, activated, held = hold((share, grad_gate, grad_up, activated, held))
     share = share.reshape(2 * experts, capacity, -1)
     returned = exchange(share, (DP, EXPERT), pair_groups).reshape(2 * slots, -1)
-    grad_in = jnp.stack([dot(grad_gate, full_x, FIRST), dot(grad_up, full_x, FIRST)]).astype(BF16)
-    grad_out = dot(activated, full_dz, FIRST).astype(BF16)
+    other = swap_cores(held)
+    full_x = jnp.where(core == 0, held, other)
+    full_dz = jnp.where(core == 0, other, held)
+    grad_gate, grad_up, activated = (
+        jnp.where(core == 0, both[:hidden], both[hidden:])
+        for both in (grad_gate, grad_up, activated)
+    )
+    plain = ((1,), (0,))
+    grad_in = jnp.stack([dot(grad_gate, full_x, plain), dot(grad_up, full_x, plain)]).astype(BF16)
+    grad_out = dot(activated, full_dz, plain).astype(BF16)
     returned, grad_in, grad_out = hold((returned, grad_in, grad_out))
     summed = dot(returned, jnp.concatenate([picker, picker]), FIRST).astype(BF16)
     pieces = exchange(summed.reshape(pairs, feat, tok_count), DP, half_groups)

time: 155 us -> 153 us (0.987)
  blocking collectives: 28.1 us -> 0 us
  starting transfers between devices: 71.7 us -> 85 us
  local copies, waits for them, and re-layouts: 14 us -> 24.3 us
  other arithmetic: 7.25 us -> 8.92 us
    all_to_all x1 -> x0, blocking collectives: 28.1 us -> none  [exchange(): lax.all_to_all(value, axis, split_axis=0, concat_axis=0, tiled=True, axis...]
    all_to_all x4 -> x5, starting transfers between devices: 65.2 us -> 73.7 us  [exchange(): lax.all_to_all(value, axis, split_axis=0, concat_axis=0, tiled=True, axis...]
    slice x1 -> x7, local copies, waits for them, and re-layouts: 0.41 us -> 8.25 us  [the longest x3 5.6 us: on_device(): twin = (twin_in[:hidden], twin_in[hidden:], twin_down)]
    select_n x1 -> x3, other arithmetic: 0.11 us -> 5.12 us  [the longest x1 3.43 us: on_device(): jnp.where(core == 0, jnp.concatenate([own[0], twin[0], own[1], twin[1]]),...]
    ppermute x2 -> x4, starting transfers between devices: 6.45 us -> 11.2 us  [swap_cores(): return lax.ppermute(value, DP, [(i, i ^ 1) for i in range(dp)])]
    squeeze x0 -> x3, local copies, waits for them, and re-layouts: none -> 4.2 us  [the longest x2 4.12 us: on_device(): array.reshape(hidden, pairs, 2, 2, feat)[:, :, :, c]]
    concatenate x3 -> x1, other arithmetic: 2.48 us -> 0.15 us  [on_device(): w_in = jnp.concatenate([gate_up[0, 0], gate_up[0, 1]])]
    select_n x2 -> x0, local copies, waits for them, and re-layouts: 1.87 us -> none  [the longest x1 0.94 us: on_device(): own_cols = jnp.where(core == 0, by_core[0], by_core[1])]
  transfers between devices with their start and end apart: 6 -> 9, of which waited for: 6 -> 6; matrix products, arithmetic and copies ran while one was open for 11% -> 21% of each run, Pallas kernels for 0% -> 0%
where the time goes in v5:
time: 153 us; the launch traced here: 150 us
  starting transfers between devices  85 us (56%)
  local copies, waits for them, and re-layouts  24.3 us (16%)
  waiting for transfers between devices  23.4 us (15%)
  other arithmetic  8.92 us (6%)
  matrix products  7.29 us (5%)
    all_to_all x5, starting transfers between devices, exchange(): lax.all_to_all(value, axis, split_axis=0, concat_axis=0, tiled=True, axis...  73.7 us
    all_to_all x5, waiting for transfers between devices, exchange(): lax.all_to_all(value, axis, split_axis=0, concat_axis=0, tiled=True, axis...  19.3 us
    ppermute x4, starting transfers between devices, swap_cores(): return lax.ppermute(value, DP, [(i, i ^ 1) for i in range(dp)])  11.2 us
    dot_general x7, matrix products, dot(): lax.dot_general(left, right, (contract, batch), preferred_element_type=F32)  7.29 us
    slice x3, local copies, waits for them, and re-layouts, on_device(): twin = (twin_in[:hidden], twin_in[hidden:], twin_down)  5.6 us
    unnamed x17, local copies, waits for them, and re-layouts  4.89 us
    squeeze x2, local copies, waits for them, and re-layouts, on_device(): array.reshape(hidden, pairs, 2, 2, feat)[:, :, :, c]  4.12 us
    ppermute x4, waiting for transfers between devices, swap_cores(): return lax.ppermute(value, DP, [(i, i ^ 1) for i in range(dp)])  4.1 us
  transfers between devices with their start and end apart: 9, of which 6 were waited for; matrix products, arithmetic and copies ran while one was open for 21% of the time, Pallas kernels for 0%

profile of v5, /device:TPU:1, one launch (start us, length us, event | category | flops | bytes accessed | tf_op | source)
XLA Modules:
  0.0 149.8 jit_solution(6405264104550699289)
XLA Ops:
  0.6 0.7 pad_maximum_fusion.2
  1.4 0.1 copy.92
  1.5 0.1 broadcast_in_dim.14
  1.6 0.7 broadcast_in_dim.28
  2.2 35.5 %all-to-all-start = ((bf16[16,2,1152]{2,1,0:T(2,128)(2,1)}), bf16[16,2,1152]{2,1,0:T(2,128)(2,1)S(1)}, u32[]{:S(2)}, u32[]{:S(2)}) async-start(bf16[16,2,1152]{2,1,0:T(2,128)(2,1)} %bitcast.3), calls=%async_computation | async-start | bytes 147456 | tf_op jit(solution)/shard_map/all_to_all | solution.py:20
  37.8 0.8 copy.93
  38.5 0.1 eq.55
  38.7 0.6 reduce-window.6
  39.3 0.2 slice_reduce_fusion
  39.6 0.1 reduce_sum.42
  39.7 0.8 copy.97
  40.5 0.1 mul.65
  40.7 0.7 multiply_add_fusion
  41.4 0.1 convert_reduce_fusion
  41.5 1.4 copy.98
  43.0 0.1 select_reduce_fusion
  43.1 0.2 pad_maximum_fusion.1
  43.3 2.3 %all-to-all-done = bf16[16,2,1152]{2,1,0:T(2,128)(2,1)S(1)} async-done(((bf16[16,2,1152]{2,1,0:T(2,128)(2,1)}), bf16[16,2,1152]{2,1,0:T(2,128)(2,1)S(1)}, u32[]{:S(2)}, u32[]{:S(2)}) %all-to-all-start) | async-done | bytes 73760 | tf_op jit(solution)/shard_map/all_to_all | solution.py:20
  45.5 0.9 broadcast_in_dim.30
  46.4 3.5 %all-to-all-start.1 = ((bf16[64,2,1152]{2,1,0:T(2,128)(2,1)}), bf16[64,2,1152]{2,1,0:T(2,128)(2,1)S(1)}, u32[]{:S(2)}, u32[]{:S(2)}) async-start(bf16[64,2,1152]{2,1,0:T(2,128)(2,1)} %bitcast.8), calls=%async_computation.1 | async-start | bytes 589824 | tf_op jit(solution)/shard_map/all_to_all | solution.py:20
  49.8 2.0 %collective-permute-start = (bf16[168,3072]{1,0:T(8,128)(2,1)S(1)}, bf16[168,3072]{1,0:T(8,128)(2,1)}, u32[]{:S(2)}, u32[]{:S(2)}) collective-permute-start(bf16[168,3072]{1,0:T(8,128)(2,1)S(1)} %pad_maximum_fusion.1), channel_id=1, source_target_pairs={{0,16},{16,0},{32,48},{48,32},{64,80},{80,64},{96,112},{112,96},{1... | collective-permute-start | bytes 3096584 | tf_op jit(solution)/shard_map/ppermute | solution.py:69
  51.8 0.1 fusion.30
  52.0 1.2 copy.101
  53.2 1.2 copy.105
  54.4 2.3 %collective-permute-start.1 = (bf16[84,3072]{1,0:T(8,128)(2,1)}, bf16[84,3072]{1,0:T(8,128)(2,1)}, u32[]{:S(2)}, u32[]{:S(2)}) collective-permute-start(bf16[84,3072]{1,0:T(8,128)(2,1)} %bitcast.7), channel_id=1, source_target_pairs={{0,16},{16,0},{32,48},{48,32},{64,80},{80,64},{96,112},{112,96},{1... | collective-permute-start | bytes 1548296 | tf_op jit(solution)/shard_map/ppermute | solution.py:69
  56.7 2.1 %fusion.31 = (bf16[84,3072]{1,0:T(8,128)(2,1)S(1)}, bf16[84,3072]{1,0:T(8,128)(2,1)}) fusion(bf16[168,3072]{1,0:T(8,128)(2,1)} %collective-permute-done), kind=kLoop, calls=%fused_computation.77 | loop fusion | bytes 2064384 | tf_op jit(solution)/shard_map/slice | solution.py:96
  58.9 1.2 copy.103
  60.1 0.8 reshape.95
  60.9 0.2 maximum_bitcast_fusion.1
  61.2 1.8 %fusion.2 = bf16[256,3072]{1,0:T(8,128)(2,1)} fusion(bf16[256,48]{0,1:T(8,128)(2,1)S(1)} %convert_reduce_fusion, bf16[3072,48]{1,0:T(8,128)(2,1)S(1)} %bitcast.100, f32[256]{0:T(256)S(1)} %broadcast_select_fusion.4), kind=kOutput, calls=%fused_computation.3 | convolution fusion | flops 78643200 | bytes 1893376 | tf_op jit(solution)/shard_map/dot_general | solution.py:13
  63.0 6.8 %all-to-all-start.2 = ((bf16[16,16,3072]{2,1,0:T(8,128)(2,1)}), bf16[16,16,3072]{2,1,0:T(8,128)(2,1)S(1)}, u32[]{:S(2)}, u32[]{:S(2)}) async-start(bf16[16,16,3072]{2,1,0:T(8,128)(2,1)} %bitcast.11), calls=%async_computation.2 | async-start | bytes 3145728 | tf_op jit(solution)/shard_map/all_to_all | solution.py:20
  69.8 2.5 %slice_bitcast_fusion.4 = (bf16[84,16,2,48]{0,3,2,1:T(8,128)(2,1)}, bf16[84,16,2,48]{0,3,2,1:T(8,128)(2,1)}, bf16[84,16,2,48]{0,3,2,1:T(8,128)(2,1)}, bf16[84,16,2,48]{0,3,2,1:T(8,128)(2,1)}) fusion(bf16[84,16,2,2,48]{0,4,3,2,1:T(8,128)(2,1)} %bitcast.102, bf16[84,16,2,2,48]{0,4,3,2,1:T(8,128)(2,1)} %bitcast.103), kind=kLoop, calls=%fused_computation.25 | loop fusion | bytes 2064384 | tf_op jit(solution)/shard_map/squeeze | solution.py:104
  72.3 2.2 %copy.107 = bf16[84,3072]{0,1:T(8,128)(2,1)} copy(bf16[84,3072]{1,0:T(8,128)(2,1)} %get-tuple-element.65) | data formatting | bytes 1032192 | tf_op jit(solution)/shard_map/slice | solution.py:96
  74.6 1.6 %slice_bitcast_fusion.2 = (bf16[84,16,2,48]{0,3,2,1:T(8,128)(2,1)S(1)}, bf16[84,16,2,48]{0,3,2,1:T(8,128)(2,1)S(1)}, bf16[84,16,2,48]{0,3,2,1:T(8,128)(2,1)S(1)}, bf16[84,16,2,48]{0,3,2,1:T(8,128)(2,1)S(1)}) fusion(bf16[84,16,2,2,48]{0,4,3,2,1:T(8,128)(2,1)} %bitcast.101, bf16[84,16,2,2,48]{0,4,3,2,1:T(8,128)(2,1)} %bitcast.104), kind=kLoop, calls=%fused_computation.23 | loop fusion | bytes 2064384 | tf_op jit(solution)/shard_map/squeeze | solution.py:104
  76.2 0.1 copy-done.4
  76.3 0.1 copy-done.5
  76.4 1.6 %maximum_select_fusion.1 = bf16[336,16,2,48]{0,3,2,1:T(8,128)(2,1)S(1)} fusion(bf16[84,16,2,48]{0,3,2,1:T(8,128)(2,1)S(1)} %get-tuple-element.77, bf16[84,16,2,48]{0,3,2,1:T(8,128)(2,1)S(1)} %get-tuple-element.73, bf16[84,16,2,48]{0,3,2,1:T(8,128)(2,1)S(1)} %copy-done.4, bf16[84,16,2,48]{0,3,2,1:T(8,128)(2,1)S(1)} %copy-done.3, ...), kind=kLoop, calls=%fused_computation.14 | loop fusion | flops 8773632 | bytes 3096577 | tf_op jit(solution)/shard_map/jit(_where)/select_n | solution.py:110
  78.0 0.1 fusion.29
  78.2 0.2 maximum_bitcast_fusion
  78.4 1.1 copy.111
  79.5 3.4 %maximum_select_fusion = bf16[336,3072]{1,0:T(8,128)(2,1)} fusion(bf16[84,3072]{1,0:T(8,128)(2,1)S(1)} %copy-done, bf16[84,3072]{1,0:T(8,128)(2,1)S(1)} %get-tuple-element.63, bf16[84,3072]{1,0:T(8,128)(2,1)S(1)} %get-tuple-element.64, bf16[84,3072]{1,0:T(8,128)(2,1)S(1)} %get-tuple-element.62, bf16[84,3072]{1,0:T(8,128)(2,1)} %bitcast.7, ...), kind=kLoop, calls=%fused_computation.10 | loop fusion | flops 17547264 | bytes 5160961 | tf_op jit(solution)/shard_map/jit(_where)/select_n | solution.py:98
  83.0 9.8 %all-to-all-done.2 = bf16[16,16,3072]{2,1,0:T(8,128)(2,1)S(1)} async-done(((bf16[16,16,3072]{2,1,0:T(8,128)(2,1)}), bf16[16,16,3072]{2,1,0:T(8,128)(2,1)S(1)}, u32[]{:S(2)}, u32[]{:S(2)}) %all-to-all-start.2) | async-done | bytes 1572896 | tf_op jit(solution)/shard_map/all_to_all | solution.py:20
  92.7 2.3 %fusion.33 = f32[336,256]{1,0:T(8,128)S(1)} fusion(bf16[336,3072]{1,0:T(8,128)(2,1)} %maximum_select_fusion, bf16[256,3072]{1,0:T(8,128)(2,1)S(1)} %bitcast.91), kind=kOutput, calls=%fused_computation.81 | convolution fusion | flops 528482304 | bytes 3981312 | tf_op jit(solution)/shard_map/dot_general | solution.py:13
  95.1 4.2 %collective-permute-start.2 = (f32[336,256]{1,0:T(8,128)S(1)}, f32[336,256]{1,0:T(8,128)S(1)}, u32[]{:S(2)}, u32[]{:S(2)}) collective-permute-start(f32[336,256]{1,0:T(8,128)S(1)} %fusion.33), channel_id=1, source_target_pairs={{0,16},{16,0},{32,48},{48,32},{64,80},{80,64},{96,112},{112,96},{1... | collective-permute-start | bytes 1032200 | tf_op jit(solution)/shard_map/ppermute | solution.py:69
  99.2 1.3 collective-permute-done.2
  100.6 0.1 multiply_convert_fusion.2
  100.7 0.6 convolution_convert_fusion.4
  101.3 0.9 copy.128
  102.2 4.7 %all-to-all-start.3 = ((bf16[32,16,768]{2,1,0:T(8,128)(2,1)}), bf16[32,16,768]{2,1,0:T(8,128)(2,1)S(1)}, u32[]{:S(2)}, u32[]{:S(2)}) async-start(bf16[32,16,768]{2,1,0:T(8,128)(2,1)} %bitcast.28), calls=%async_computation.3 | async-start | bytes 1572864 | tf_op jit(solution)/shard_map/all_to_all | solution.py:20
  106.9 2.7 %collective-permute-start.3 = (bf16[256,3072]{1,0:T(8,128)(2,1)S(1)}, bf16[256,3072]{1,0:T(8,128)(2,1)S(1)}, u32[]{:S(2)}, u32[]{:S(2)}) collective-permute-start(bf16[256,3072]{1,0:T(8,128)(2,1)S(1)} %bitcast.92), channel_id=1, source_target_pairs={{0,16},{16,0},{32,48},{48,32},{64,80},{80,64},{96,112},{112,96},{1... | collective-permute-start | bytes 4718600 | tf_op jit(solution)/shard_map/ppermute | solution.py:69
  109.7 2.8 %collective-permute-done.3 = bf16[256,3072]{1,0:T(8,128)(2,1)S(1)} collective-permute-done((bf16[256,3072]{1,0:T(8,128)(2,1)S(1)}, bf16[256,3072]{1,0:T(8,128)(2,1)S(1)}, u32[]{:S(2)}, u32[]{:S(2)}) %collective-permute-start.3) | collective-permute-done | bytes 1572896 | tf_op jit(solution)/shard_map/ppermute | solution.py:69
  112.5 0.5 fusion.3
  113.0 0.5 fusion.4
  113.5 1.3 convolution_convert_fusion.1
  114.8 0.1 pad_maximum_fusion
  114.9 4.4 %all-to-all-done.3 = bf16[32,16,768]{2,1,0:T(8,128)(2,1)S(1)} async-done(((bf16[32,16,768]{2,1,0:T(8,128)(2,1)}), bf16[32,16,768]{2,1,0:T(8,128)(2,1)S(1)}, u32[]{:S(2)}, u32[]{:S(2)}) %all-to-all-start.3) | async-done | bytes 786464 | tf_op jit(solution)/shard_map/all_to_all | solution.py:20
  119.3 0.2 convolution_convert_fusion.5
  119.6 0.2 reshape.107
  119.9 0.9 reshape.110
  120.8 23.4 %all-to-all-start.4 = ((bf16[16,2,1152]{2,1,0:T(2,128)(2,1)}), bf16[16,2,1152]{2,1,0:T(2,128)(2,1)S(1)}, u32[]{:S(2)}, u32[]{:S(2)}) async-start(bf16[16,2,1152]{2,1,0:T(2,128)(2,1)} %reshape.110), calls=%async_computation.4 | async-start | bytes 147456 | tf_op jit(solution)/shard_map/all_to_all | solution.py:20
  144.1 2.0 %copy.114 = bf16[1,2,84,3072]{3,1,2,0:T(2,128)(2,1)} copy(bf16[1,2,84,3072]{3,2,1,0:T(8,128)(2,1)S(1)} %bitcast.97) | data formatting | bytes 2064384
  146.2 2.8 %all-to-all-done.4 = bf16[16,2,1152]{2,1,0:T(2,128)(2,1)S(1)} async-done(((bf16[16,2,1152]{2,1,0:T(2,128)(2,1)}), bf16[16,2,1152]{2,1,0:T(2,128)(2,1)S(1)}, u32[]{:S(2)}, u32[]{:S(2)}) %all-to-all-start.4) | async-done | bytes 73760 | tf_op jit(solution)/shard_map/all_to_all | solution.py:20
  149.0 0.2 reshape.111
  149.2 0.6 bitcast_reduce_fusion
  (27 shorter events, 0.6 us)
Async XLA Ops:
  2.2 43.3 %all-to-all-start = ((bf16[16,2,1152]{2,1,0:T(2,128)(2,1)}), bf16[16,2,1152]{2,1,0:T(2,128)(2,1)S(1)}, u32[]{:S(2)}, u32[]{:S(2)}) async-start(bf16[16,2,1152]{2,1,0:T(2,128)(2,1)} %bitcast.3), calls=%async_computation | async-start | bytes 147456 | tf_op jit(solution)/shard_map/all_to_all | solution.py:20
  46.4 13.7 %all-to-all-start.1 = ((bf16[64,2,1152]{2,1,0:T(2,128)(2,1)}), bf16[64,2,1152]{2,1,0:T(2,128)(2,1)S(1)}, u32[]{:S(2)}, u32[]{:S(2)}) async-start(bf16[64,2,1152]{2,1,0:T(2,128)(2,1)} %bitcast.8), calls=%async_computation.1 | async-start | bytes 589824 | tf_op jit(solution)/shard_map/all_to_all | solution.py:20
  49.8 6.9 %collective-permute-start = (bf16[168,3072]{1,0:T(8,128)(2,1)S(1)}, bf16[168,3072]{1,0:T(8,128)(2,1)}, u32[]{:S(2)}, u32[]{:S(2)}) collective-permute-start(bf16[168,3072]{1,0:T(8,128)(2,1)S(1)} %pad_maximum_fusion.1), channel_id=1, source_target_pairs={{0,16},{16,0},{32,48},{48,32},{64,80},{80,64},{96,112},{112,96},{1... | collective-permute-start | bytes 3096584 | tf_op jit(solution)/shard_map/ppermute | solution.py:69
  54.4 25.1 %collective-permute-start.1 = (bf16[84,3072]{1,0:T(8,128)(2,1)}, bf16[84,3072]{1,0:T(8,128)(2,1)}, u32[]{:S(2)}, u32[]{:S(2)}) collective-permute-start(bf16[84,3072]{1,0:T(8,128)(2,1)} %bitcast.7), channel_id=1, source_target_pairs={{0,16},{16,0},{32,48},{48,32},{64,80},{80,64},{96,112},{112,96},{1... | collective-permute-start | bytes 1548296 | tf_op jit(solution)/shard_map/ppermute | solution.py:69
  63.0 29.7 %all-to-all-start.2 = ((bf16[16,16,3072]{2,1,0:T(8,128)(2,1)}), bf16[16,16,3072]{2,1,0:T(8,128)(2,1)S(1)}, u32[]{:S(2)}, u32[]{:S(2)}) async-start(bf16[16,16,3072]{2,1,0:T(8,128)(2,1)} %bitcast.11), calls=%async_computation.2 | async-start | bytes 3145728 | tf_op jit(solution)/shard_map/all_to_all | solution.py:20
  74.5 1.6 %copy-start.2 = (bf16[84,16,2,48]{0,3,2,1:T(8,128)(2,1)S(1)}, bf16[84,16,2,48]{0,3,2,1:T(8,128)(2,1)}, u32[]{:S(2)}) copy-start(bf16[84,16,2,48]{0,3,2,1:T(8,128)(2,1)} %get-tuple-element.68) | copy-start | bytes 774148
  74.5 1.6 %copy-start.3 = (bf16[84,16,2,48]{0,3,2,1:T(8,128)(2,1)S(1)}, bf16[84,16,2,48]{0,3,2,1:T(8,128)(2,1)}, u32[]{:S(2)}) copy-start(bf16[84,16,2,48]{0,3,2,1:T(8,128)(2,1)} %get-tuple-element.69) | copy-start | bytes 774148
  74.5 1.7 %copy-start.4 = (bf16[84,16,2,48]{0,3,2,1:T(8,128)(2,1)S(1)}, bf16[84,16,2,48]{0,3,2,1:T(8,128)(2,1)}, u32[]{:S(2)}) copy-start(bf16[84,16,2,48]{0,3,2,1:T(8,128)(2,1)} %get-tuple-element.79) | copy-start | bytes 774148
  74.6 1.8 %copy-start.5 = (bf16[84,16,2,48]{0,3,2,1:T(8,128)(2,1)S(1)}, bf16[84,16,2,48]{0,3,2,1:T(8,128)(2,1)}, u32[]{:S(2)}) copy-start(bf16[84,16,2,48]{0,3,2,1:T(8,128)(2,1)} %get-tuple-element.80) | copy-start | bytes 774148
  78.4 1.2 copy-start
  95.1 5.6 %copy-start.1 = (bf16[336,2,16,48]{0,3,2,1:T(8,128)(2,1)S(1)}, bf16[336,2,16,48]{0,3,2,1:T(8,128)(2,1)}, u32[]{:S(2)}) copy-start(bf16[336,2,16,48]{0,3,2,1:T(8,128)(2,1)} %copy.111) | copy-start | bytes 3096580
  95.1 5.4 %collective-permute-start.2 = (f32[336,256]{1,0:T(8,128)S(1)}, f32[336,256]{1,0:T(8,128)S(1)}, u32[]{:S(2)}, u32[]{:S(2)}) collective-permute-start(f32[336,256]{1,0:T(8,128)S(1)} %fusion.33), channel_id=1, source_target_pairs={{0,16},{16,0},{32,48},{48,32},{64,80},{80,64},{96,112},{112,96},{1... | collective-permute-start | bytes 1032200 | tf_op jit(solution)/shard_map/ppermute | solution.py:69
  102.2 17.1 %all-to-all-start.3 = ((bf16[32,16,768]{2,1,0:T(8,128)(2,1)}), bf16[32,16,768]{2,1,0:T(8,128)(2,1)S(1)}, u32[]{:S(2)}, u32[]{:S(2)}) async-start(bf16[32,16,768]{2,1,0:T(8,128)(2,1)} %bitcast.28), calls=%async_computation.3 | async-start | bytes 1572864 | tf_op jit(solution)/shard_map/all_to_all | solution.py:20
  106.9 5.6 %collective-permute-start.3 = (bf16[256,3072]{1,0:T(8,128)(2,1)S(1)}, bf16[256,3072]{1,0:T(8,128)(2,1)S(1)}, u32[]{:S(2)}, u32[]{:S(2)}) collective-permute-start(bf16[256,3072]{1,0:T(8,128)(2,1)S(1)} %bitcast.92), channel_id=1, source_target_pairs={{0,16},{16,0},{32,48},{48,32},{64,80},{80,64},{96,112},{112,96},{1... | collective-permute-start | bytes 4718600 | tf_op jit(solution)/shard_map/ppermute | solution.py:69
  120.8 28.2 %all-to-all-start.4 = ((bf16[16,2,1152]{2,1,0:T(2,128)(2,1)}), bf16[16,2,1152]{2,1,0:T(2,128)(2,1)S(1)}, u32[]{:S(2)}, u32[]{:S(2)}) async-start(bf16[16,2,1152]{2,1,0:T(2,128)(2,1)} %reshape.110), calls=%async_computation.4 | async-start | bytes 147456 | tf_op jit(solution)/shard_map/all_to_all | solution.py:20

commit v6 on v5

--- a/solution.py
+++ b/solution.py
@@ -6,7 +6,7 @@
 
 DP, EXPERT = "dp", "expert"
 F32, BF16 = jnp.float32, jnp.bfloat16
-LAST, FIRST = ((1,), (1,)), ((0,), (0,))
+LAST, FIRST, PLAIN = ((1,), (1,)), ((0,), (0,)), ((1,), (0,))
 
 
 def dot(left, right, contract, batch=((), ())):
@@ -89,54 +89,54 @@
     column = with_layout_constraint(column.reshape(width, tok_count), Layout((0, 1)))
     rows = dot(picker, column, LAST).astype(BF16)
     rows = (scale[:, None] * rows.astype(F32)).astype(BF16)
+    rows, twin_in, twin_down = hold((rows, twin_in, twin_down))
     held = exchange(rows.reshape(experts, capacity, width), EXPERT).reshape(slots, width)
 
     hidden = w_down.shape[0]
-    own = (w_in[:hidden], w_in[hidden:], w_down)
-    twin = (twin_in[:hidden], twin_in[hidden:], twin_down)
     unit = 2 * hidden
-    w_chip = jnp.where(
-        core == 0,
-        jnp.concatenate([own[0], twin[0], own[1], twin[1]]),
-        jnp.concatenate([twin[2], own[2], twin[2], own[2]]),
+    w_pair = with_layout_constraint(jnp.concatenate([w_in, twin_in]), Layout((0, 1)))
+    gap = jnp.zeros((hidden, width), BF16)
+    w_other = jnp.concatenate([w_down, gap, twin_down, gap])
+    is_gate = (jnp.arange(2 * unit) % unit < hidden)[:, None]
+    w_chip = jnp.where((core == 1) & is_gate, w_other, w_pair)
+    w_chip = with_layout_constraint(w_chip, Layout((0, 1)))
+    w_chip = with_layout_constraint(hold((w_chip,))[0], Layout((1, 0)))
+    part = (pairs // 2) * feat
+    place = jnp.arange(2 * part)
+    origin = ((place % part // feat * 2 + place // part) * 2 + core) * feat + place % feat
+    pick = (jnp.arange(4 * part)[:, None] == origin[None, :]).astype(BF16)
+    halves = [dot(w_pair[:, i : i + 4 * part], pick, PLAIN).astype(BF16) for i in (4 * part, 0)]
+    columns = jnp.concatenate(
+        [half[:, p * part : (p + 1) * part] for p in (0, 1) for half in halves], axis=1
     )
-    columns = [
-        array.reshape(hidden, pairs, 2, 2, feat)[:, :, :, c]
-        for array, c in (
-            [(own[0], 0), (twin[0], 0), (own[1], 0), (twin[1], 0)]
-            + [(twin[0], 1), (own[0], 1), (twin[1], 1), (own[1], 1)]
-        )
-    ]
-    columns = jnp.where(core == 0, jnp.concatenate(columns[:4]), jnp.concatenate(columns[4:]))
-    columns = jnp.roll(columns, -(pairs // 2), axis=1).transpose(0, 2, 1, 3)
-    columns = columns.reshape(2 * unit, 2 * pairs * feat)
     held, w_chip, columns = hold((held, w_chip, columns))
 
-    mine = dot(w_chip, held, LAST)
+    mine = hold((dot(held, w_chip, LAST),))[0].T
     theirs = swap_cores(mine)
-    gate_up_part = jnp.where(core == 0, mine, theirs)
-    gate_part, up_part = gate_up_part[:unit], gate_up_part[unit:]
-    back_grad = jnp.where(core == 0, theirs, mine)[:unit]
-    sig_gate = jax.nn.sigmoid(gate_part)
-    activated = (gate_part * sig_gate * up_part).astype(BF16)
-    grad_gate = (back_grad * up_part * sig_gate * (1.0 + gate_part * (1.0 - sig_gate))).astype(BF16)
-    grad_up = (back_grad * gate_part * sig_gate).astype(BF16)
+    grad_gate, grad_up, activated = [], [], []
+    for mine_here, theirs_here in ((mine[:unit], theirs[unit:]), (mine[unit:], theirs[:unit])):
+        gate_up_part = jnp.where(core == 0, mine_here, theirs_here)
+        gate_part, up_part = gate_up_part[:hidden], gate_up_part[hidden:]
+        back_grad = jnp.where(core == 0, theirs_here, mine_here)[:hidden]
+        sig_gate = jax.nn.sigmoid(gate_part)
+        activated.append((gate_part * sig_gate * up_part).astype(BF16))
+        slope = sig_gate * (1.0 + gate_part * (1.0 - sig_gate))
+        grad_gate.append((back_grad * up_part * slope).astype(BF16))
+        grad_up.append((back_grad * gate_part * sig_gate).astype(BF16))
 
-    share = dot(jnp.concatenate([grad_gate, grad_up]), columns, FIRST).astype(BF16)
+    grads = jnp.concatenate([grad_gate[0], grad_up[0], grad_gate[1], grad_up[1]])
+    share = dot(grads, columns, FIRST).astype(BF16)
     share = share.reshape(slots, 2, -1).transpose(1, 0, 2)
-    share, grad_gate, grad_up, activated, held = hold((share, grad_gate, grad_up, activated, held))
+    share, grad_gate, grad_up, activated, held = hold(
+        (share, grad_gate[0], grad_up[0], activated[0], held)
+    )
     share = share.reshape(2 * experts, capacity, -1)
     returned = exchange(share, (DP, EXPERT), pair_groups).reshape(2 * slots, -1)
     other = swap_cores(held)
     full_x = jnp.where(core == 0, held, other)
     full_dz = jnp.where(core == 0, other, held)
-    grad_gate, grad_up, activated = (
-        jnp.where(core == 0, both[:hidden], both[hidden:])
-        for both in (grad_gate, grad_up, activated)
-    )
-    plain = ((1,), (0,))
-    grad_in = jnp.stack([dot(grad_gate, full_x, plain), dot(grad_up, full_x, plain)]).astype(BF16)
-    grad_out = dot(activated, full_dz, plain).astype(BF16)
+    grad_in = jnp.stack([dot(grad_gate, full_x, PLAIN), dot(grad_up, full_x, PLAIN)]).astype(BF16)
+    grad_out = dot(activated, full_dz, PLAIN).astype(BF16)
     returned, grad_in, grad_out = hold((returned, grad_in, grad_out))
     summed = dot(returned, jnp.concatenate([picker, picker]), FIRST).astype(BF16)
     pieces = exchange(summed.reshape(pairs, feat, tok_count), DP, half_groups)

time: 153 us -> 149 us (0.974)
  local copies, waits for them, and re-layouts: 24.3 us -> 17 us
  matrix products: 7.29 us -> 11.2 us
  other arithmetic: 8.92 us -> 11.4 us
    slice x7 -> x2, local copies, waits for them, and re-layouts: 8.25 us -> 0.11 us  [on_device(): half[:, p * part:(p + 1) * part]]
    optimization_barrier x0 -> x1, local copies, waits for them, and re-layouts: none -> 4.15 us  [on_device(): w_chip = with_layout_constraint(hold((w_chip,))[0], Layout((1, 0)))]
    squeeze x2 -> x0, local copies, waits for them, and re-layouts: 4.12 us -> none  [on_device(): array.reshape(hidden, pairs, 2, 2, feat)[:, :, :, c]]
    dot_general x7 -> x9, matrix products: 7.29 us -> 11.2 us  [dot(): lax.dot_general(left, right, (contract, batch), preferred_element_type=F32)]
    all_to_all x5, starting transfers between devices: 73.7 us -> 70.8 us  [exchange(): lax.all_to_all(value, axis, split_axis=0, concat_axis=0, tiled=True, axis...]
    select_n x3 -> x2, other arithmetic: 5.12 us -> 7.72 us  [the longest x1 7.62 us: on_device(): w_chip = jnp.where((core == 1) & is_gate, w_other, w_pair)]
    ppermute x4, starting transfers between devices: 11.2 us -> 13 us  [swap_cores(): return lax.ppermute(value, DP, [(i, i ^ 1) for i in range(dp)])]
    unnamed x17 -> x8, local copies, waits for them, and re-layouts: 4.89 us -> 5.71 us
  transfers between devices with their start and end apart: 9 -> 9, of which waited for: 6 -> 7; matrix products, arithmetic and copies ran while one was open for 21% -> 21% of each run, Pallas kernels for 0% -> 0%
where the time goes in v6:
time: 149 us; the launch traced here: 147 us
  starting transfers between devices  83.8 us (56%)
  waiting for transfers between devices  22.2 us (15%)
  local copies, waits for them, and re-layouts  17 us (11%)
  other arithmetic  11.4 us (8%)
  matrix products  11.2 us (8%)
    all_to_all x5, starting transfers between devices, exchange(): lax.all_to_all(value, axis, split_axis=0, concat_axis=0, tiled=True, axis...  70.8 us
    all_to_all x5, waiting for transfers between devices, exchange(): lax.all_to_all(value, axis, split_axis=0, concat_axis=0, tiled=True, axis...  18.1 us
    ppermute x4, starting transfers between devices, swap_cores(): return lax.ppermute(value, DP, [(i, i ^ 1) for i in range(dp)])  13 us
    dot_general x9, matrix products, dot(): lax.dot_general(left, right, (contract, batch), preferred_element_type=F32)  11.2 us
    select_n x1, other arithmetic, on_device(): w_chip = jnp.where((core == 1) & is_gate, w_other, w_pair)  7.62 us
    unnamed x8, local copies, waits for them, and re-layouts  5.71 us
    optimization_barrier x1, local copies, waits for them, and re-layouts, on_device(): w_chip = with_layout_constraint(hold((w_chip,))[0], Layout((1, 0)))  4.15 us
    ppermute x4, waiting for transfers between devices, swap_cores(): return lax.ppermute(value, DP, [(i, i ^ 1) for i in range(dp)])  4.1 us
  transfers between devices with their start and end apart: 9, of which 7 were waited for; matrix products, arithmetic and copies ran while one was open for 21% of the time, Pallas kernels for 0%

profile of v6, /device:TPU:1, one launch (start us, length us, event | category | flops | bytes accessed | tf_op | source)
XLA Modules:
  0.0 146.6 jit_solution(5573662967191547036)
XLA Ops:
  0.6 0.7 pad_maximum_fusion.3
  1.4 0.1 copy.56
  1.5 0.1 broadcast_in_dim.24
  1.6 0.7 broadcast_in_dim.42
  2.2 35.5 %all-to-all-start = ((bf16[16,2,1152]{2,1,0:T(2,128)(2,1)}), bf16[16,2,1152]{2,1,0:T(2,128)(2,1)S(1)}, u32[]{:S(2)}, u32[]{:S(2)}) async-start(bf16[16,2,1152]{2,1,0:T(2,128)(2,1)} %bitcast.3), calls=%async_computation | async-start | bytes 147456 | tf_op jit(solution)/shard_map/all_to_all | solution.py:20
  37.8 0.8 copy.57
  38.5 0.1 eq.73
  38.7 0.6 reduce-window.6
  39.3 0.2 slice_reduce_fusion
  39.5 0.1 bitcast_bitcast_fusion.1
  39.6 0.1 reduce_sum.42
  39.7 0.8 copy.61
  40.5 0.1 mul.105
  40.6 0.1 copy.60
  40.7 0.7 multiply_add_fusion
  41.4 0.1 convert_reduce_fusion
  41.5 1.4 copy.62
  42.9 0.1 slice_bitcast_fusion.1
  43.0 0.1 select_reduce_fusion
  43.1 0.2 pad_maximum_fusion.1
  43.3 2.3 %all-to-all-done = bf16[16,2,1152]{2,1,0:T(2,128)(2,1)S(1)} async-done(((bf16[16,2,1152]{2,1,0:T(2,128)(2,1)}), bf16[16,2,1152]{2,1,0:T(2,128)(2,1)S(1)}, u32[]{:S(2)}, u32[]{:S(2)}) %all-to-all-start) | async-done | bytes 73760 | tf_op jit(solution)/shard_map/all_to_all | solution.py:20
  45.5 0.9 broadcast_in_dim.44
  46.4 3.5 %all-to-all-start.1 = ((bf16[64,2,1152]{2,1,0:T(2,128)(2,1)}), bf16[64,2,1152]{2,1,0:T(2,128)(2,1)S(1)}, u32[]{:S(2)}, u32[]{:S(2)}) async-start(bf16[64,2,1152]{2,1,0:T(2,128)(2,1)} %bitcast.8), calls=%async_computation.1 | async-start | bytes 589824 | tf_op jit(solution)/shard_map/all_to_all | solution.py:20
  49.9 2.0 %collective-permute-start = (bf16[168,3072]{1,0:T(8,128)(2,1)S(1)}, bf16[168,3072]{1,0:T(8,128)(2,1)S(1)}, u32[]{:S(2)}, u32[]{:S(2)}) collective-permute-start(bf16[168,3072]{1,0:T(8,128)(2,1)S(1)} %pad_maximum_fusion.1), channel_id=1, source_target_pairs={{0,16},{16,0},{32,48},{48,32},{64,80},{80,64},{96,112},{112,96},{1... | collective-permute-start | bytes 3096584 | tf_op jit(solution)/shard_map/ppermute | solution.py:69
  51.9 2.3 %collective-permute-start.1 = (bf16[84,3072]{1,0:T(8,128)(2,1)}, bf16[84,3072]{1,0:T(8,128)(2,1)}, u32[]{:S(2)}, u32[]{:S(2)}) collective-permute-start(bf16[84,3072]{1,0:T(8,128)(2,1)} %bitcast.7), channel_id=1, source_target_pairs={{0,16},{16,0},{32,48},{48,32},{64,80},{80,64},{96,112},{112,96},{1... | collective-permute-start | bytes 1548296 | tf_op jit(solution)/shard_map/ppermute | solution.py:69
  54.2 1.0 constant_dynamic-update-slice_fusion.1
  55.3 4.2 %all-to-all-done.1 = bf16[64,2,1152]{2,1,0:T(2,128)(2,1)S(1)} async-done(((bf16[64,2,1152]{2,1,0:T(2,128)(2,1)}), bf16[64,2,1152]{2,1,0:T(2,128)(2,1)S(1)}, u32[]{:S(2)}, u32[]{:S(2)}) %all-to-all-start.1) | async-done | bytes 294944 | tf_op jit(solution)/shard_map/all_to_all | solution.py:20
  59.5 0.8 reshape.126
  60.3 0.1 fusion.58
  60.4 0.2 maximum_bitcast_fusion
  60.5 0.1 copy.64
  60.6 1.8 %fusion.4 = bf16[256,3072]{1,0:T(8,128)(2,1)} fusion(bf16[256,48]{0,1:T(8,128)(2,1)S(1)} %convert_reduce_fusion, bf16[3072,48]{1,0:T(8,128)(2,1)S(1)} %bitcast.67, f32[256]{0:T(256)S(1)} %broadcast_select_fusion.5), kind=kOutput, calls=%fused_computation.6 | convolution fusion | flops 78643200 | bytes 1893376 | tf_op jit(solution)/shard_map/dot_general | solution.py:13
  62.4 6.8 %all-to-all-start.2 = ((bf16[16,16,3072]{2,1,0:T(8,128)(2,1)}), bf16[16,16,3072]{2,1,0:T(8,128)(2,1)S(1)}, u32[]{:S(2)}, u32[]{:S(2)}) async-start(bf16[16,16,3072]{2,1,0:T(8,128)(2,1)} %bitcast.11), calls=%async_computation.2 | async-start | bytes 3145728 | tf_op jit(solution)/shard_map/all_to_all | solution.py:20
  69.2 1.1 constant_dynamic-update-slice_fusion
  70.3 7.6 %maximum_select_fusion = bf16[336,3072]{1,0:T(8,128)(2,1)} fusion(bf16[336,3072]{1,0:T(8,128)(2,1)} %constant_dynamic-update-slice_fusion, bf16[84,3072]{1,0:T(8,128)(2,1)S(1)} %broadcast_in_dim.46, bf16[84,3072]{1,0:T(8,128)(2,1)} %collective-permute-done.1, bf16[84,3072]{1,0:T(8,128)(2,1)} %bitcast.7, pred[336]{0:T(512)(128)(4,1)S(1)} %fusion.55), kind=kLoop, calls=%fused_computation.15 | loop fusion | flops 9289728 | bytes 5677392 | tf_op jit(solution)/shard_map/jit(_where)/select_n | solution.py:101
  77.9 4.2 %copy.65 = bf16[336,3072]{0,1:T(8,128)(2,1)} copy(bf16[336,3072]{1,0:T(8,128)(2,1)} %maximum_select_fusion) | data formatting | bytes 4128768 | tf_op jit(solution)/shard_map/optimization_barrier | solution.py:103
  82.1 2.5 %fusion.11 = bf16[336,768]{1,0:T(8,128)(2,1)S(1)} fusion(s32[768]{0:T(1024)S(1)} %fusion.39, bf16[336,3072]{1,0:T(8,128)(2,1)} %constant_dynamic-update-slice_fusion), kind=kOutput, calls=%fused_computation.19 | convolution fusion | flops 794161152 | bytes 1551360 | tf_op jit(solution)/shard_map/dot_general | solution.py:13
  84.5 0.1 fusion.59
  84.6 1.2 fusion.12
  85.8 0.1 pad_maximum_fusion.2
  85.9 3.8 %all-to-all-done.2 = bf16[16,16,3072]{2,1,0:T(8,128)(2,1)S(1)} async-done(((bf16[16,16,3072]{2,1,0:T(8,128)(2,1)}), bf16[16,16,3072]{2,1,0:T(8,128)(2,1)S(1)}, u32[]{:S(2)}, u32[]{:S(2)}) %all-to-all-start.2) | async-done | bytes 1572896 | tf_op jit(solution)/shard_map/all_to_all | solution.py:20
  89.7 2.7 %fusion.61 = f32[256,336]{0,1:T(8,128)S(1)} fusion(bf16[256,3072]{1,0:T(8,128)(2,1)S(1)} %bitcast.60, bf16[336,3072]{0,1:T(8,128)(2,1)} %copy.65), kind=kOutput, calls=%fused_computation.117 | convolution fusion | flops 528482304 | bytes 3981312 | tf_op jit(solution)/shard_map/dot_general | solution.py:13
  92.4 6.1 %collective-permute-start.2 = (f32[336,256]{1,0:T(8,128)S(1)}, f32[336,256]{1,0:T(8,128)S(1)}, u32[]{:S(2)}, u32[]{:S(2)}) collective-permute-start(f32[336,256]{1,0:T(8,128)S(1)} %bitcast.68), channel_id=1, source_target_pairs={{0,16},{16,0},{32,48},{48,32},{64,80},{80,64},{96,112},{112,96},{1... | collective-permute-start | bytes 1032200 | tf_op jit(solution)/shard_map/ppermute | solution.py:69
  98.5 1.3 collective-permute-done.2
  99.7 0.1 broadcast_select_fusion.3
  99.9 0.1 fusion.23
  100.0 0.6 convolution_convert_fusion.4
  100.6 0.9 copy.76
  101.5 3.9 %all-to-all-start.3 = ((bf16[32,16,768]{2,1,0:T(8,128)(2,1)}), bf16[32,16,768]{2,1,0:T(8,128)(2,1)S(1)}, u32[]{:S(2)}, u32[]{:S(2)}) async-start(bf16[32,16,768]{2,1,0:T(8,128)(2,1)} %bitcast.15), calls=%async_computation.3 | async-start | bytes 1572864 | tf_op jit(solution)/shard_map/all_to_all | solution.py:20
  105.4 2.5 %collective-permute-start.3 = (bf16[256,3072]{1,0:T(8,128)(2,1)S(1)}, bf16[256,3072]{1,0:T(8,128)(2,1)S(1)}, u32[]{:S(2)}, u32[]{:S(2)}) collective-permute-start(bf16[256,3072]{1,0:T(8,128)(2,1)S(1)} %bitcast.61), channel_id=1, source_target_pairs={{0,16},{16,0},{32,48},{48,32},{64,80},{80,64},{96,112},{112,96},{1... | collective-permute-start | bytes 4718600 | tf_op jit(solution)/shard_map/ppermute | solution.py:69
  108.0 2.8 %collective-permute-done.3 = bf16[256,3072]{1,0:T(8,128)(2,1)S(1)} collective-permute-done((bf16[256,3072]{1,0:T(8,128)(2,1)S(1)}, bf16[256,3072]{1,0:T(8,128)(2,1)S(1)}, u32[]{:S(2)}, u32[]{:S(2)}) %collective-permute-start.3) | collective-permute-done | bytes 1572896 | tf_op jit(solution)/shard_map/ppermute | solution.py:69
  110.8 0.5 fusion.5
  111.3 0.5 fusion.6
  111.8 1.3 convolution_convert_fusion.1
  113.1 0.1 pad_maximum_fusion
  113.2 5.0 %all-to-all-done.3 = bf16[32,16,768]{2,1,0:T(8,128)(2,1)S(1)} async-done(((bf16[32,16,768]{2,1,0:T(8,128)(2,1)}), bf16[32,16,768]{2,1,0:T(8,128)(2,1)S(1)}, u32[]{:S(2)}, u32[]{:S(2)}) %all-to-all-start.3) | async-done | bytes 786464 | tf_op jit(solution)/shard_map/all_to_all | solution.py:20
  118.2 0.2 convolution_convert_fusion.5
  118.4 0.2 reshape.133
  118.7 0.9 reshape.136
  119.6 21.2 %all-to-all-start.4 = ((bf16[16,2,1152]{2,1,0:T(2,128)(2,1)}), bf16[16,2,1152]{2,1,0:T(2,128)(2,1)S(1)}, u32[]{:S(2)}, u32[]{:S(2)}) async-start(bf16[16,2,1152]{2,1,0:T(2,128)(2,1)} %reshape.136), calls=%async_computation.4 | async-start | bytes 147456 | tf_op jit(solution)/shard_map/all_to_all | solution.py:20
  140.8 2.0 %copy.68 = bf16[1,2,84,3072]{3,1,2,0:T(2,128)(2,1)} copy(bf16[1,2,84,3072]{3,2,1,0:T(8,128)(2,1)S(1)} %bitcast.65) | data formatting | bytes 2064384
  142.8 2.9 %all-to-all-done.4 = bf16[16,2,1152]{2,1,0:T(2,128)(2,1)S(1)} async-done(((bf16[16,2,1152]{2,1,0:T(2,128)(2,1)}), bf16[16,2,1152]{2,1,0:T(2,128)(2,1)S(1)}, u32[]{:S(2)}, u32[]{:S(2)}) %all-to-all-start.4) | async-done | bytes 73760 | tf_op jit(solution)/shard_map/all_to_all | solution.py:20
  145.7 0.2 reshape.137
  145.9 0.6 bitcast_reduce_fusion
  (16 shorter events, 0.3 us)
Async XLA Ops:
  2.2 43.3 %all-to-all-start = ((bf16[16,2,1152]{2,1,0:T(2,128)(2,1)}), bf16[16,2,1152]{2,1,0:T(2,128)(2,1)S(1)}, u32[]{:S(2)}, u32[]{:S(2)}) async-start(bf16[16,2,1152]{2,1,0:T(2,128)(2,1)} %bitcast.3), calls=%async_computation | async-start | bytes 147456 | tf_op jit(solution)/shard_map/all_to_all | solution.py:20
  46.4 13.1 %all-to-all-start.1 = ((bf16[64,2,1152]{2,1,0:T(2,128)(2,1)}), bf16[64,2,1152]{2,1,0:T(2,128)(2,1)S(1)}, u32[]{:S(2)}, u32[]{:S(2)}) async-start(bf16[64,2,1152]{2,1,0:T(2,128)(2,1)} %bitcast.8), calls=%async_computation.1 | async-start | bytes 589824 | tf_op jit(solution)/shard_map/all_to_all | solution.py:20
  49.9 12.5 %collective-permute-start = (bf16[168,3072]{1,0:T(8,128)(2,1)S(1)}, bf16[168,3072]{1,0:T(8,128)(2,1)S(1)}, u32[]{:S(2)}, u32[]{:S(2)}) collective-permute-start(bf16[168,3072]{1,0:T(8,128)(2,1)S(1)} %pad_maximum_fusion.1), channel_id=1, source_target_pairs={{0,16},{16,0},{32,48},{48,32},{64,80},{80,64},{96,112},{112,96},{1... | collective-permute-start | bytes 3096584 | tf_op jit(solution)/shard_map/ppermute | solution.py:69
  51.9 10.5 %collective-permute-start.1 = (bf16[84,3072]{1,0:T(8,128)(2,1)}, bf16[84,3072]{1,0:T(8,128)(2,1)}, u32[]{:S(2)}, u32[]{:S(2)}) collective-permute-start(bf16[84,3072]{1,0:T(8,128)(2,1)} %bitcast.7), channel_id=1, source_target_pairs={{0,16},{16,0},{32,48},{48,32},{64,80},{80,64},{96,112},{112,96},{1... | collective-permute-start | bytes 1548296 | tf_op jit(solution)/shard_map/ppermute | solution.py:69
  62.4 27.3 %all-to-all-start.2 = ((bf16[16,16,3072]{2,1,0:T(8,128)(2,1)}), bf16[16,16,3072]{2,1,0:T(8,128)(2,1)S(1)}, u32[]{:S(2)}, u32[]{:S(2)}) async-start(bf16[16,16,3072]{2,1,0:T(8,128)(2,1)} %bitcast.11), calls=%async_computation.2 | async-start | bytes 3145728 | tf_op jit(solution)/shard_map/all_to_all | solution.py:20
  82.1 2.5 %copy-start = (bf16[336,3072]{1,0:T(8,128)(2,1)S(1)}, bf16[336,3072]{1,0:T(8,128)(2,1)}, u32[]{:S(2)}) copy-start(bf16[336,3072]{1,0:T(8,128)(2,1)} %constant_dynamic-update-slice_fusion) | copy-start | bytes 6193156
  92.4 7.4 %collective-permute-start.2 = (f32[336,256]{1,0:T(8,128)S(1)}, f32[336,256]{1,0:T(8,128)S(1)}, u32[]{:S(2)}, u32[]{:S(2)}) collective-permute-start(f32[336,256]{1,0:T(8,128)S(1)} %bitcast.68), channel_id=1, source_target_pairs={{0,16},{16,0},{32,48},{48,32},{64,80},{80,64},{96,112},{112,96},{1... | collective-permute-start | bytes 1032200 | tf_op jit(solution)/shard_map/ppermute | solution.py:69
  101.5 16.7 %all-to-all-start.3 = ((bf16[32,16,768]{2,1,0:T(8,128)(2,1)}), bf16[32,16,768]{2,1,0:T(8,128)(2,1)S(1)}, u32[]{:S(2)}, u32[]{:S(2)}) async-start(bf16[32,16,768]{2,1,0:T(8,128)(2,1)} %bitcast.15), calls=%async_computation.3 | async-start | bytes 1572864 | tf_op jit(solution)/shard_map/all_to_all | solution.py:20
  105.4 5.4 %collective-permute-start.3 = (bf16[256,3072]{1,0:T(8,128)(2,1)S(1)}, bf16[256,3072]{1,0:T(8,128)(2,1)S(1)}, u32[]{:S(2)}, u32[]{:S(2)}) collective-permute-start(bf16[256,3072]{1,0:T(8,128)(2,1)S(1)} %bitcast.61), channel_id=1, source_target_pairs={{0,16},{16,0},{32,48},{48,32},{64,80},{80,64},{96,112},{112,96},{1... | collective-permute-start | bytes 4718600 | tf_op jit(solution)/shard_map/ppermute | solution.py:69
  119.6 26.1 %all-to-all-start.4 = ((bf16[16,2,1152]{2,1,0:T(2,128)(2,1)}), bf16[16,2,1152]{2,1,0:T(2,128)(2,1)S(1)}, u32[]{:S(2)}, u32[]{:S(2)}) async-start(bf16[16,2,1152]{2,1,0:T(2,128)(2,1)} %reshape.136), calls=%async_computation.4 | async-start | bytes 147456 | tf_op jit(solution)/shard_map/all_to_all | solution.py:20

commit v7 on v6

--- a/solution.py
+++ b/solution.py
@@ -51,11 +51,13 @@
     capacity = min(tok_count, tok_count * top_count * 4 // (3 * experts))
     slots = experts * capacity
 
-    turn = far // 2
+    turn, tilt = far // 2, near // 2
     far_order = [(j + turn) % far for j in range(far)]
     far_groups = [[(f * near + n) * 2 + c for f in far_order for c in (0, 1)] for n in range(near)]
     near_groups = [
-        [(f * near + n) * 2 + c for n in range(near)] for f in range(far) for c in (0, 1)
+        [(f * near + (n + tilt) % near) * 2 + c for n in range(near)]
+        for f in range(far)
+        for c in (0, 1)
     ]
     half_order = [(j + pairs // 2) % pairs for j in range(pairs)]
     half_groups = [[(j * 2 + p) * 2 + c for j in half_order] for p in (0, 1) for c in (0, 1)]
@@ -82,6 +84,7 @@
 
     column = jnp.broadcast_to(column[None], (near,) + column.shape).reshape(-1, *block)
     column = exchange(column, DP, near_groups)
+    column = jnp.roll(column, tilt * far * 2, axis=0)
     twin_in, twin_down = swap_cores(w_in), swap_cores(w_down)
 
     column = column.reshape(near, far, 2, feat, tok_count)
@@ -111,7 +114,8 @@
     )
     held, w_chip, columns = hold((held, w_chip, columns))
 
-    mine = hold((dot(held, w_chip, LAST),))[0].T
+    mine = with_layout_constraint(dot(held, w_chip, LAST), Layout((0, 1)))
+    mine = with_layout_constraint(hold((mine,))[0].T, Layout((0, 1)))
     theirs = swap_cores(mine)
     grad_gate, grad_up, activated = [], [], []
     for mine_here, theirs_here in ((mine[:unit], theirs[unit:]), (mine[unit:], theirs[:unit])):

time: 149 us -> 150 us (level)
  waiting for transfers between devices: 22.2 us -> 17.9 us
  starting transfers between devices: 83.8 us -> 88.1 us
    all_to_all x5, waiting for transfers between devices: 18.1 us -> 13.6 us  [exchange(): lax.all_to_all(value, axis, split_axis=0, concat_axis=0, tiled=True, axis...]
    all_to_all x5, starting transfers between devices: 70.8 us -> 74.3 us  [exchange(): lax.all_to_all(value, axis, split_axis=0, concat_axis=0, tiled=True, axis...]
  transfers between devices with their start and end apart: 9 -> 9, of which waited for: 7 -> 6; matrix products, arithmetic and copies ran while one was open for 21% -> 21% of each run, Pallas kernels for 0% -> 0%
where the time goes in v7:
time: 150 us; the launch traced here: 147 us
  starting transfers between devices  88.1 us (59%)
  waiting for transfers between devices  17.9 us (12%)
  local copies, waits for them, and re-layouts  17.3 us (12%)
  other arithmetic  11.8 us (8%)
  matrix products  11.2 us (7%)
    all_to_all x5, starting transfers between devices, exchange(): lax.all_to_all(value, axis, split_axis=0, concat_axis=0, tiled=True, axis...  74.3 us
    ppermute x4, starting transfers between devices, swap_cores(): return lax.ppermute(value, DP, [(i, i ^ 1) for i in range(dp)])  13.7 us
    all_to_all x5, waiting for transfers between devices, exchange(): lax.all_to_all(value, axis, split_axis=0, concat_axis=0, tiled=True, axis...  13.6 us
    dot_general x9, matrix products, dot(): lax.dot_general(left, right, (contract, batch), preferred_element_type=F32)  11.2 us
    select_n x1, other arithmetic, on_device(): w_chip = jnp.where((core == 1) & is_gate, w_other, w_pair)  7.63 us
    unnamed x8, local copies, waits for them, and re-layouts  5.71 us
    ppermute x4, waiting for transfers between devices, swap_cores(): return lax.ppermute(value, DP, [(i, i ^ 1) for i in range(dp)])  4.28 us
    optimization_barrier x1, local copies, waits for them, and re-layouts, on_device(): w_chip = with_layout_constraint(hold((w_chip,))[0], Layout((1, 0)))  4.15 us
  transfers between devices with their start and end apart: 9, of which 6 were waited for; matrix products, arithmetic and copies ran while one was open for 21% of the time, Pallas kernels for 0%

profile of v7, /device:TPU:1, one launch (start us, length us, event | category | flops | bytes accessed | tf_op | source)
XLA Modules:
  0.0 147.3 jit_solution(7092374288430167324)
XLA Ops:
  0.6 0.7 pad_maximum_fusion.4
  1.4 0.1 copy.60
  1.5 0.1 broadcast_in_dim.24
  1.6 0.7 broadcast_in_dim.42
  2.2 35.5 %all-to-all-start = ((bf16[16,2,1152]{2,1,0:T(2,128)(2,1)}), bf16[16,2,1152]{2,1,0:T(2,128)(2,1)S(1)}, u32[]{:S(2)}, u32[]{:S(2)}) async-start(bf16[16,2,1152]{2,1,0:T(2,128)(2,1)} %bitcast.3), calls=%async_computation | async-start | bytes 147456 | tf_op jit(solution)/shard_map/all_to_all | solution.py:20
  37.8 0.8 copy.61
  38.5 0.1 eq.73
  38.7 0.6 reduce-window.6
  39.3 0.2 slice_reduce_fusion
  39.5 0.1 bitcast_bitcast_fusion.1
  39.6 0.1 reduce_sum.42
  39.7 0.8 copy.65
  40.5 0.1 mul.105
  40.6 0.1 copy.64
  40.7 0.7 multiply_add_fusion
  41.4 0.1 convert_reduce_fusion
  41.5 1.4 copy.66
  42.9 0.1 slice_bitcast_fusion.1
  43.0 0.1 select_reduce_fusion
  43.1 0.2 pad_maximum_fusion.1
  43.3 2.3 %all-to-all-done = bf16[16,2,1152]{2,1,0:T(2,128)(2,1)S(1)} async-done(((bf16[16,2,1152]{2,1,0:T(2,128)(2,1)}), bf16[16,2,1152]{2,1,0:T(2,128)(2,1)S(1)}, u32[]{:S(2)}, u32[]{:S(2)}) %all-to-all-start) | async-done | bytes 73760 | tf_op jit(solution)/shard_map/all_to_all | solution.py:20
  45.5 0.9 broadcast_in_dim.44
  46.4 3.7 %all-to-all-start.1 = ((bf16[64,2,1152]{2,1,0:T(2,128)(2,1)}), bf16[64,2,1152]{2,1,0:T(2,128)(2,1)S(1)}, u32[]{:S(2)}, u32[]{:S(2)}) async-start(bf16[64,2,1152]{2,1,0:T(2,128)(2,1)} %bitcast.8), calls=%async_computation.1 | async-start | bytes 589824 | tf_op jit(solution)/shard_map/all_to_all | solution.py:20
  50.1 3.4 %collective-permute-start = (bf16[168,3072]{1,0:T(8,128)(2,1)S(1)}, bf16[168,3072]{1,0:T(8,128)(2,1)S(1)}, u32[]{:S(2)}, u32[]{:S(2)}) collective-permute-start(bf16[168,3072]{1,0:T(8,128)(2,1)S(1)} %pad_maximum_fusion.1), channel_id=1, source_target_pairs={{0,16},{16,0},{32,48},{48,32},{64,80},{80,64},{96,112},{112,96},{1... | collective-permute-start | bytes 3096584 | tf_op jit(solution)/shard_map/ppermute | solution.py:71
  53.5 1.9 %collective-permute-start.1 = (bf16[84,3072]{1,0:T(8,128)(2,1)}, bf16[84,3072]{1,0:T(8,128)(2,1)}, u32[]{:S(2)}, u32[]{:S(2)}) collective-permute-start(bf16[84,3072]{1,0:T(8,128)(2,1)} %bitcast.7), channel_id=1, source_target_pairs={{0,16},{16,0},{32,48},{48,32},{64,80},{80,64},{96,112},{112,96},{1... | collective-permute-start | bytes 1548296 | tf_op jit(solution)/shard_map/ppermute | solution.py:71
  55.4 1.0 constant_dynamic-update-slice_fusion.1
  56.5 0.2 fusion.61
  56.7 0.4 pad_maximum_fusion.3
  57.1 0.8 reshape.126
  57.8 0.1 fusion.58
  57.9 0.2 maximum_bitcast_fusion
  58.2 1.8 %fusion.4 = bf16[256,3072]{1,0:T(8,128)(2,1)} fusion(bf16[256,48]{0,1:T(8,128)(2,1)S(1)} %convert_reduce_fusion, bf16[3072,48]{1,0:T(8,128)(2,1)S(1)} %bitcast.67, f32[256]{0:T(256)S(1)} %broadcast_select_fusion.5), kind=kOutput, calls=%fused_computation.6 | convolution fusion | flops 78643200 | bytes 1893376 | tf_op jit(solution)/shard_map/dot_general | solution.py:13
  59.9 6.8 %all-to-all-start.2 = ((bf16[16,16,3072]{2,1,0:T(8,128)(2,1)}), bf16[16,16,3072]{2,1,0:T(8,128)(2,1)S(1)}, u32[]{:S(2)}, u32[]{:S(2)}) async-start(bf16[16,16,3072]{2,1,0:T(8,128)(2,1)} %bitcast.11), calls=%async_computation.2 | async-start | bytes 3145728 | tf_op jit(solution)/shard_map/all_to_all | solution.py:20
  66.7 1.1 constant_dynamic-update-slice_fusion
  67.8 7.6 %maximum_select_fusion = bf16[336,3072]{1,0:T(8,128)(2,1)} fusion(bf16[336,3072]{1,0:T(8,128)(2,1)} %constant_dynamic-update-slice_fusion, bf16[84,3072]{1,0:T(8,128)(2,1)S(1)} %broadcast_in_dim.46, bf16[84,3072]{1,0:T(8,128)(2,1)} %collective-permute-done.1, bf16[84,3072]{1,0:T(8,128)(2,1)} %bitcast.7, pred[336]{0:T(512)(128)(4,1)S(1)} %fusion.55), kind=kLoop, calls=%fused_computation.15 | loop fusion | flops 9289728 | bytes 5677392 | tf_op jit(solution)/shard_map/jit(_where)/select_n | solution.py:104
  75.5 4.1 %copy.69 = bf16[336,3072]{0,1:T(8,128)(2,1)} copy(bf16[336,3072]{1,0:T(8,128)(2,1)} %maximum_select_fusion) | data formatting | bytes 4128768 | tf_op jit(solution)/shard_map/optimization_barrier | solution.py:106
  79.6 2.5 %fusion.11 = bf16[336,768]{1,0:T(8,128)(2,1)S(1)} fusion(s32[768]{0:T(1024)S(1)} %fusion.39, bf16[336,3072]{1,0:T(8,128)(2,1)} %constant_dynamic-update-slice_fusion), kind=kOutput, calls=%fused_computation.19 | convolution fusion | flops 794161152 | bytes 1551360 | tf_op jit(solution)/shard_map/dot_general | solution.py:13
  82.2 1.2 fusion.12
  83.4 0.1 pad_maximum_fusion.2
  83.5 3.5 %all-to-all-done.2 = bf16[16,16,3072]{2,1,0:T(8,128)(2,1)S(1)} async-done(((bf16[16,16,3072]{2,1,0:T(8,128)(2,1)}), bf16[16,16,3072]{2,1,0:T(8,128)(2,1)S(1)}, u32[]{:S(2)}, u32[]{:S(2)}) %all-to-all-start.2) | async-done | bytes 1572896 | tf_op jit(solution)/shard_map/all_to_all | solution.py:20
  87.0 2.6 %fusion.62 = f32[256,336]{1,0:T(8,128)S(1)} fusion(bf16[256,3072]{1,0:T(8,128)(2,1)S(1)} %bitcast.60, bf16[336,3072]{0,1:T(8,128)(2,1)} %copy.69), kind=kOutput, calls=%fused_computation.119 | convolution fusion | flops 528482304 | bytes 3981312 | tf_op jit(solution)/shard_map/dot_general | solution.py:13
  89.7 0.2 copy.70
  89.8 6.2 %collective-permute-start.2 = (f32[336,256]{1,0:T(8,128)S(1)}, f32[336,256]{1,0:T(8,128)S(1)}, u32[]{:S(2)}, u32[]{:S(2)}) collective-permute-start(f32[336,256]{1,0:T(8,128)S(1)} %bitcast.68), channel_id=1, source_target_pairs={{0,16},{16,0},{32,48},{48,32},{64,80},{80,64},{96,112},{112,96},{1... | collective-permute-start | bytes 1032200 | tf_op jit(solution)/shard_map/ppermute | solution.py:71
  96.0 1.3 collective-permute-done.2
  97.3 0.1 broadcast_select_fusion.3
  97.3 0.1 fusion.23
  97.5 0.6 convolution_convert_fusion.4
  98.1 0.9 copy.81
  99.0 4.1 %all-to-all-start.3 = ((bf16[32,16,768]{2,1,0:T(8,128)(2,1)}), bf16[32,16,768]{2,1,0:T(8,128)(2,1)S(1)}, u32[]{:S(2)}, u32[]{:S(2)}) async-start(bf16[32,16,768]{2,1,0:T(8,128)(2,1)} %bitcast.15), calls=%async_computation.3 | async-start | bytes 1572864 | tf_op jit(solution)/shard_map/all_to_all | solution.py:20
  103.1 2.3 %collective-permute-start.3 = (bf16[256,3072]{1,0:T(8,128)(2,1)S(1)}, bf16[256,3072]{1,0:T(8,128)(2,1)S(1)}, u32[]{:S(2)}, u32[]{:S(2)}) collective-permute-start(bf16[256,3072]{1,0:T(8,128)(2,1)S(1)} %bitcast.61), channel_id=1, source_target_pairs={{0,16},{16,0},{32,48},{48,32},{64,80},{80,64},{96,112},{112,96},{1... | collective-permute-start | bytes 4718600 | tf_op jit(solution)/shard_map/ppermute | solution.py:71
  105.4 3.0 %collective-permute-done.3 = bf16[256,3072]{1,0:T(8,128)(2,1)S(1)} collective-permute-done((bf16[256,3072]{1,0:T(8,128)(2,1)S(1)}, bf16[256,3072]{1,0:T(8,128)(2,1)S(1)}, u32[]{:S(2)}, u32[]{:S(2)}) %collective-permute-start.3) | collective-permute-done | bytes 1572896 | tf_op jit(solution)/shard_map/ppermute | solution.py:71
  108.4 0.5 fusion.5
  108.9 0.5 fusion.6
  109.4 1.3 convolution_convert_fusion.1
  110.7 0.1 pad_maximum_fusion
  110.8 5.1 %all-to-all-done.3 = bf16[32,16,768]{2,1,0:T(8,128)(2,1)S(1)} async-done(((bf16[32,16,768]{2,1,0:T(8,128)(2,1)}), bf16[32,16,768]{2,1,0:T(8,128)(2,1)S(1)}, u32[]{:S(2)}, u32[]{:S(2)}) %all-to-all-start.3) | async-done | bytes 786464 | tf_op jit(solution)/shard_map/all_to_all | solution.py:20
  115.9 0.2 convolution_convert_fusion.5
  116.1 0.2 reshape.133
  116.4 0.9 reshape.136
  117.3 24.3 %all-to-all-start.4 = ((bf16[16,2,1152]{2,1,0:T(2,128)(2,1)}), bf16[16,2,1152]{2,1,0:T(2,128)(2,1)S(1)}, u32[]{:S(2)}, u32[]{:S(2)}) async-start(bf16[16,2,1152]{2,1,0:T(2,128)(2,1)} %reshape.136), calls=%async_computation.4 | async-start | bytes 147456 | tf_op jit(solution)/shard_map/all_to_all | solution.py:20
  141.6 2.0 %copy.73 = bf16[1,2,84,3072]{3,1,2,0:T(2,128)(2,1)} copy(bf16[1,2,84,3072]{3,2,1,0:T(8,128)(2,1)S(1)} %bitcast.65) | data formatting | bytes 2064384
  143.6 2.8 %all-to-all-done.4 = bf16[16,2,1152]{2,1,0:T(2,128)(2,1)S(1)} async-done(((bf16[16,2,1152]{2,1,0:T(2,128)(2,1)}), bf16[16,2,1152]{2,1,0:T(2,128)(2,1)S(1)}, u32[]{:S(2)}, u32[]{:S(2)}) %all-to-all-start.4) | async-done | bytes 73760 | tf_op jit(solution)/shard_map/all_to_all | solution.py:20
  146.4 0.2 reshape.137
  146.6 0.6 bitcast_reduce_fusion
  (19 shorter events, 0.4 us)
Async XLA Ops:
  2.2 43.3 %all-to-all-start = ((bf16[16,2,1152]{2,1,0:T(2,128)(2,1)}), bf16[16,2,1152]{2,1,0:T(2,128)(2,1)S(1)}, u32[]{:S(2)}, u32[]{:S(2)}) async-start(bf16[16,2,1152]{2,1,0:T(2,128)(2,1)} %bitcast.3), calls=%async_computation | async-start | bytes 147456 | tf_op jit(solution)/shard_map/all_to_all | solution.py:20
  46.4 10.1 %all-to-all-start.1 = ((bf16[64,2,1152]{2,1,0:T(2,128)(2,1)}), bf16[64,2,1152]{2,1,0:T(2,128)(2,1)S(1)}, u32[]{:S(2)}, u32[]{:S(2)}) async-start(bf16[64,2,1152]{2,1,0:T(2,128)(2,1)} %bitcast.8), calls=%async_computation.1 | async-start | bytes 589824 | tf_op jit(solution)/shard_map/all_to_all | solution.py:20
  50.1 9.8 %collective-permute-start = (bf16[168,3072]{1,0:T(8,128)(2,1)S(1)}, bf16[168,3072]{1,0:T(8,128)(2,1)S(1)}, u32[]{:S(2)}, u32[]{:S(2)}) collective-permute-start(bf16[168,3072]{1,0:T(8,128)(2,1)S(1)} %pad_maximum_fusion.1), channel_id=1, source_target_pairs={{0,16},{16,0},{32,48},{48,32},{64,80},{80,64},{96,112},{112,96},{1... | collective-permute-start | bytes 3096584 | tf_op jit(solution)/shard_map/ppermute | solution.py:71
  53.5 6.5 %collective-permute-start.1 = (bf16[84,3072]{1,0:T(8,128)(2,1)}, bf16[84,3072]{1,0:T(8,128)(2,1)}, u32[]{:S(2)}, u32[]{:S(2)}) collective-permute-start(bf16[84,3072]{1,0:T(8,128)(2,1)} %bitcast.7), channel_id=1, source_target_pairs={{0,16},{16,0},{32,48},{48,32},{64,80},{80,64},{96,112},{112,96},{1... | collective-permute-start | bytes 1548296 | tf_op jit(solution)/shard_map/ppermute | solution.py:71
  59.9 27.1 %all-to-all-start.2 = ((bf16[16,16,3072]{2,1,0:T(8,128)(2,1)}), bf16[16,16,3072]{2,1,0:T(8,128)(2,1)S(1)}, u32[]{:S(2)}, u32[]{:S(2)}) async-start(bf16[16,16,3072]{2,1,0:T(8,128)(2,1)} %bitcast.11), calls=%async_computation.2 | async-start | bytes 3145728 | tf_op jit(solution)/shard_map/all_to_all | solution.py:20
  79.6 2.5 %copy-start = (bf16[336,3072]{1,0:T(8,128)(2,1)S(1)}, bf16[336,3072]{1,0:T(8,128)(2,1)}, u32[]{:S(2)}) copy-start(bf16[336,3072]{1,0:T(8,128)(2,1)} %constant_dynamic-update-slice_fusion) | copy-start | bytes 6193156
  89.8 7.4 %collective-permute-start.2 = (f32[336,256]{1,0:T(8,128)S(1)}, f32[336,256]{1,0:T(8,128)S(1)}, u32[]{:S(2)}, u32[]{:S(2)}) collective-permute-start(f32[336,256]{1,0:T(8,128)S(1)} %bitcast.68), channel_id=1, source_target_pairs={{0,16},{16,0},{32,48},{48,32},{64,80},{80,64},{96,112},{112,96},{1... | collective-permute-start | bytes 1032200 | tf_op jit(solution)/shard_map/ppermute | solution.py:71
  99.0 16.9 %all-to-all-start.3 = ((bf16[32,16,768]{2,1,0:T(8,128)(2,1)}), bf16[32,16,768]{2,1,0:T(8,128)(2,1)S(1)}, u32[]{:S(2)}, u32[]{:S(2)}) async-start(bf16[32,16,768]{2,1,0:T(8,128)(2,1)} %bitcast.15), calls=%async_computation.3 | async-start | bytes 1572864 | tf_op jit(solution)/shard_map/all_to_all | solution.py:20
  103.1 5.3 %collective-permute-start.3 = (bf16[256,3072]{1,0:T(8,128)(2,1)S(1)}, bf16[256,3072]{1,0:T(8,128)(2,1)S(1)}, u32[]{:S(2)}, u32[]{:S(2)}) collective-permute-start(bf16[256,3072]{1,0:T(8,128)(2,1)S(1)} %bitcast.61), channel_id=1, source_target_pairs={{0,16},{16,0},{32,48},{48,32},{64,80},{80,64},{96,112},{112,96},{1... | collective-permute-start | bytes 4718600 | tf_op jit(solution)/shard_map/ppermute | solution.py:71
  117.3 29.1 %all-to-all-start.4 = ((bf16[16,2,1152]{2,1,0:T(2,128)(2,1)}), bf16[16,2,1152]{2,1,0:T(2,128)(2,1)S(1)}, u32[]{:S(2)}, u32[]{:S(2)}) async-start(bf16[16,2,1152]{2,1,0:T(2,128)(2,1)} %reshape.136), calls=%async_computation.4 | async-start | bytes 147456 | tf_op jit(solution)/shard_map/all_to_all | solution.py:20

commit v8 on v7

--- a/solution.py
+++ b/solution.py
@@ -99,11 +99,9 @@
     unit = 2 * hidden
     w_pair = with_layout_constraint(jnp.concatenate([w_in, twin_in]), Layout((0, 1)))
     gap = jnp.zeros((hidden, width), BF16)
-    w_other = jnp.concatenate([w_down, gap, twin_down, gap])
-    is_gate = (jnp.arange(2 * unit) % unit < hidden)[:, None]
-    w_chip = jnp.where((core == 1) & is_gate, w_other, w_pair)
-    w_chip = with_layout_constraint(w_chip, Layout((0, 1)))
-    w_chip = with_layout_constraint(hold((w_chip,))[0], Layout((1, 0)))
+    takes_down = (core == 1) & (jnp.arange(unit) < hidden)[:, None]
+    w_own = jnp.where(takes_down, jnp.concatenate([w_down, gap]), w_in)
+    w_twin = jnp.where(takes_down, jnp.concatenate([twin_down, gap]), twin_in)
     part = (pairs // 2) * feat
     place = jnp.arange(2 * part)
     origin = ((place % part // feat * 2 + place // part) * 2 + core) * feat + place % feat
@@ -112,10 +110,9 @@
     columns = jnp.concatenate(
         [half[:, p * part : (p + 1) * part] for p in (0, 1) for half in halves], axis=1
     )
-    held, w_chip, columns = hold((held, w_chip, columns))
+    held, w_own, w_twin, columns = hold((held, w_own, w_twin, columns))
 
-    mine = with_layout_constraint(dot(held, w_chip, LAST), Layout((0, 1)))
-    mine = with_layout_constraint(hold((mine,))[0].T, Layout((0, 1)))
+    mine = jnp.concatenate([dot(w_own, held, LAST), dot(w_twin, held, LAST)])
     theirs = swap_cores(mine)
     grad_gate, grad_up, activated = [], [], []
     for mine_here, theirs_here in ((mine[:unit], theirs[unit:]), (mine[unit:], theirs[:unit])):

time: 150 us -> 150 us (level)
  waiting for transfers between devices: 17.9 us -> 27.4 us
  local copies, waits for them, and re-layouts: 17.3 us -> 10.9 us
  starting transfers between devices: 88.1 us -> 86.6 us
    all_to_all x5, waiting for transfers between devices: 13.6 us -> 23.1 us  [exchange(): lax.all_to_all(value, axis, split_axis=0, concat_axis=0, tiled=True, axis...]
    select_n x2 -> x0, other arithmetic: 7.71 us -> none  [the longest x1 7.63 us: on_device(): w_chip = jnp.where((core == 1) & is_gate, w_other, w_pair)]
    optimization_barrier x2 -> x0, local copies, waits for them, and re-layouts: 4.3 us -> none  [the longest x1 4.15 us: on_device(): w_chip = with_layout_constraint(hold((w_chip,))[0], Layout((1, 0)))]
    concatenate x0 -> x2, other arithmetic: none -> 3.09 us  [the longest x1 3.07 us: on_device(): jnp.concatenate([w_in, twin_in])]
    unnamed x0 -> x1, other arithmetic: none -> 2.42 us
    unnamed x8 -> x9, local copies, waits for them, and re-layouts: 5.71 us -> 4.68 us
    dot_general x9 -> x10, matrix products: 11.2 us -> 11.1 us  [dot(): lax.dot_general(left, right, (contract, batch), preferred_element_type=F32)]
  transfers between devices with their start and end apart: 9 -> 9, of which waited for: 6 -> 6; matrix products, arithmetic and copies ran while one was open for 21% -> 16% of each run, Pallas kernels for 0% -> 0%
where the time goes in v8:
time: 150 us; the launch traced here: 148 us
  starting transfers between devices  86.6 us (58%)
  waiting for transfers between devices  27.4 us (18%)
  matrix products  11.1 us (7%)
  local copies, waits for them, and re-layouts  10.9 us (7%)
  other arithmetic  10.6 us (7%)
    all_to_all x5, starting transfers between devices, exchange(): lax.all_to_all(value, axis, split_axis=0, concat_axis=0, tiled=True, axis...  73.1 us
    all_to_all x5, waiting for transfers between devices, exchange(): lax.all_to_all(value, axis, split_axis=0, concat_axis=0, tiled=True, axis...  23.1 us
    ppermute x4, starting transfers between devices, swap_cores(): return lax.ppermute(value, DP, [(i, i ^ 1) for i in range(dp)])  13.5 us
    dot_general x10, matrix products, dot(): lax.dot_general(left, right, (contract, batch), preferred_element_type=F32)  11.1 us
    unnamed x9, local copies, waits for them, and re-layouts  4.68 us
    ppermute x4, waiting for transfers between devices, swap_cores(): return lax.ppermute(value, DP, [(i, i ^ 1) for i in range(dp)])  4.28 us
    concatenate x1, other arithmetic, on_device(): jnp.concatenate([w_in, twin_in])  3.07 us
  transfers between devices with their start and end apart: 9, of which 6 were waited for; matrix products, arithmetic and copies ran while one was open for 16% of the time, Pallas kernels for 0%

profile of v8, /device:TPU:1, one launch (start us, length us, event | category | flops | bytes accessed | tf_op | source)
XLA Modules:
  0.0 147.6 jit_solution(12090203636832506509)
XLA Ops:
  0.6 0.7 pad_maximum_fusion.5
  1.4 0.1 copy.52
  1.5 0.1 broadcast_in_dim.42
  1.6 0.7 broadcast_in_dim.43
  2.2 35.5 %all-to-all-start = ((bf16[16,2,1152]{2,1,0:T(2,128)(2,1)}), bf16[16,2,1152]{2,1,0:T(2,128)(2,1)S(1)}, u32[]{:S(2)}, u32[]{:S(2)}) async-start(bf16[16,2,1152]{2,1,0:T(2,128)(2,1)} %bitcast.3), calls=%async_computation | async-start | bytes 147456 | tf_op jit(solution)/shard_map/all_to_all | solution.py:20
  37.8 0.8 copy.53
  38.5 0.1 eq.71
  38.7 0.6 reduce-window.6
  39.3 0.2 slice_reduce_fusion
  39.5 0.1 bitcast_bitcast_fusion.1
  39.6 0.1 reduce_sum.42
  39.7 0.1 copy.56
  39.8 0.7 multiply_add_fusion
  40.5 0.1 convert_reduce_fusion
  40.6 0.8 copy.57
  41.4 0.1 mul.105
  41.5 1.4 copy.58
  42.9 0.1 slice_bitcast_fusion.1
  43.0 0.1 select_reduce_fusion
  43.1 0.2 pad_maximum_fusion.1
  43.3 2.3 %all-to-all-done = bf16[16,2,1152]{2,1,0:T(2,128)(2,1)S(1)} async-done(((bf16[16,2,1152]{2,1,0:T(2,128)(2,1)}), bf16[16,2,1152]{2,1,0:T(2,128)(2,1)S(1)}, u32[]{:S(2)}, u32[]{:S(2)}) %all-to-all-start) | async-done | bytes 73760 | tf_op jit(solution)/shard_map/all_to_all | solution.py:20
  45.5 0.9 broadcast_in_dim.45
  46.4 3.7 %all-to-all-start.1 = ((bf16[64,2,1152]{2,1,0:T(2,128)(2,1)}), bf16[64,2,1152]{2,1,0:T(2,128)(2,1)S(1)}, u32[]{:S(2)}, u32[]{:S(2)}) async-start(bf16[64,2,1152]{2,1,0:T(2,128)(2,1)} %bitcast.8), calls=%async_computation.1 | async-start | bytes 589824 | tf_op jit(solution)/shard_map/all_to_all | solution.py:20
  50.1 3.4 %collective-permute-start = (bf16[168,3072]{1,0:T(8,128)(2,1)S(1)}, bf16[168,3072]{1,0:T(8,128)(2,1)}, u32[]{:S(2)}, u32[]{:S(2)}) collective-permute-start(bf16[168,3072]{1,0:T(8,128)(2,1)S(1)} %pad_maximum_fusion.1), channel_id=1, source_target_pairs={{0,16},{16,0},{32,48},{48,32},{64,80},{80,64},{96,112},{112,96},{1... | collective-permute-start | bytes 3096584 | tf_op jit(solution)/shard_map/ppermute | solution.py:71
  53.5 1.9 %collective-permute-start.1 = (bf16[84,3072]{1,0:T(8,128)(2,1)}, bf16[84,3072]{1,0:T(8,128)(2,1)}, u32[]{:S(2)}, u32[]{:S(2)}) collective-permute-start(bf16[84,3072]{1,0:T(8,128)(2,1)} %bitcast.7), channel_id=1, source_target_pairs={{0,16},{16,0},{32,48},{48,32},{64,80},{80,64},{96,112},{112,96},{1... | collective-permute-start | bytes 1548296 | tf_op jit(solution)/shard_map/ppermute | solution.py:71
  55.4 2.4 %constant_dynamic-update-slice_fusion.1 = (bf16[336,3072]{1,0:T(8,128)(2,1)}, bf16[168,3072]{1,0:T(8,128)(2,1)S(1)}) fusion(bf16[168,3072]{1,0:T(8,128)(2,1)S(1)} %pad_maximum_fusion.1, bf16[84,3072]{1,0:T(8,128)(2,1)} %bitcast.7, pred[168]{0:T(512)(128)(4,1)S(1)} %compare_and_fusion), kind=kLoop, calls=%fused_computation.80 | loop fusion | flops 516095 | bytes 3612840
  57.8 0.2 fusion.57
  58.0 0.4 pad_maximum_fusion.4
  58.4 0.8 reshape.120
  59.2 0.1 fusion.53
  59.3 0.2 maximum_bitcast_fusion
  59.4 0.1 copy.60
  59.5 1.8 %fusion.4 = bf16[256,3072]{1,0:T(8,128)(2,1)} fusion(bf16[256,48]{0,1:T(8,128)(2,1)S(1)} %convert_reduce_fusion, bf16[3072,48]{1,0:T(8,128)(2,1)S(1)} %bitcast.69, f32[256]{0:T(256)S(1)} %broadcast_select_fusion.5), kind=kOutput, calls=%fused_computation.6 | convolution fusion | flops 78643200 | bytes 1893376 | tf_op jit(solution)/shard_map/dot_general | solution.py:13
  61.3 6.8 %all-to-all-start.2 = ((bf16[16,16,3072]{2,1,0:T(8,128)(2,1)}), bf16[16,16,3072]{2,1,0:T(8,128)(2,1)S(1)}, u32[]{:S(2)}, u32[]{:S(2)}) async-start(bf16[16,16,3072]{2,1,0:T(8,128)(2,1)} %bitcast.11), calls=%async_computation.2 | async-start | bytes 3145728 | tf_op jit(solution)/shard_map/all_to_all | solution.py:20
  68.1 3.1 %constant_dynamic-update-slice_fusion = (bf16[336,3072]{1,0:T(8,128)(2,1)}, bf16[168,3072]{1,0:T(8,128)(2,1)}) fusion(bf16[336,3072]{1,0:T(8,128)(2,1)} %get-tuple-element.68, bf16[168,3072]{1,0:T(8,128)(2,1)} %collective-permute-done, bf16[84,3072]{1,0:T(8,128)(2,1)} %collective-permute-done.1, pred[168]{0:T(512)(128)(4,1)S(1)} %compare_and_fusion), kind=kLoop, calls=%fused_computation.79 | loop fusion | flops 516096 | bytes 3637416 | tf_op jit(solution)/shard_map/concatenate | solution.py:100
  71.2 2.5 %fusion.12 = bf16[336,768]{1,0:T(8,128)(2,1)S(1)} fusion(s32[768]{0:T(1024)S(1)} %fusion.39, bf16[336,3072]{1,0:T(8,128)(2,1)} %get-tuple-element.66), kind=kOutput, calls=%fused_computation.19 | convolution fusion | flops 794161152 | bytes 1551360 | tf_op jit(solution)/shard_map/dot_general | solution.py:13
  73.6 0.1 fusion.55
  73.7 1.2 fusion.11
  74.9 0.1 fusion.54
  74.9 1.1 pad_maximum_fusion.2
  76.0 13.2 %all-to-all-done.2 = bf16[16,16,3072]{2,1,0:T(8,128)(2,1)S(1)} async-done(((bf16[16,16,3072]{2,1,0:T(8,128)(2,1)}), bf16[16,16,3072]{2,1,0:T(8,128)(2,1)S(1)}, u32[]{:S(2)}, u32[]{:S(2)}) %all-to-all-start.2) | async-done | bytes 1572896 | tf_op jit(solution)/shard_map/all_to_all | solution.py:20
  89.2 1.9 %fusion.59 = f32[168,256]{1,0:T(8,128)S(1)} fusion(bf16[168,3072]{1,0:T(8,128)(2,1)} %get-tuple-element.39, bf16[256,3072]{1,0:T(8,128)(2,1)S(1)} %bitcast.61), kind=kOutput, calls=%fused_computation.117 | convolution fusion | flops 264241152 | bytes 2777088 | tf_op jit(solution)/shard_map/dot_general | solution.py:13
  91.1 0.7 fusion.58
  91.8 5.8 %collective-permute-start.2 = (f32[336,256]{1,0:T(8,128)S(1)}, f32[336,256]{1,0:T(8,128)S(1)}, u32[]{:S(2)}, u32[]{:S(2)}) collective-permute-start(f32[336,256]{1,0:T(8,128)S(1)} %pad_maximum_fusion.3), channel_id=1, source_target_pairs={{0,16},{16,0},{32,48},{48,32},{64,80},{80,64},{96,112},{112,96},{1... | collective-permute-start | bytes 1032200 | tf_op jit(solution)/shard_map/ppermute | solution.py:71
  97.6 1.3 collective-permute-done.2
  98.9 0.1 fusion.23
  99.0 0.6 convolution_convert_fusion.4
  99.6 0.9 copy.71
  100.6 3.9 %all-to-all-start.3 = ((bf16[32,16,768]{2,1,0:T(8,128)(2,1)}), bf16[32,16,768]{2,1,0:T(8,128)(2,1)S(1)}, u32[]{:S(2)}, u32[]{:S(2)}) async-start(bf16[32,16,768]{2,1,0:T(8,128)(2,1)} %bitcast.14), calls=%async_computation.3 | async-start | bytes 1572864 | tf_op jit(solution)/shard_map/all_to_all | solution.py:20
  104.5 2.4 %collective-permute-start.3 = (bf16[256,3072]{1,0:T(8,128)(2,1)S(1)}, bf16[256,3072]{1,0:T(8,128)(2,1)S(1)}, u32[]{:S(2)}, u32[]{:S(2)}) collective-permute-start(bf16[256,3072]{1,0:T(8,128)(2,1)S(1)} %bitcast.63), channel_id=1, source_target_pairs={{0,16},{16,0},{32,48},{48,32},{64,80},{80,64},{96,112},{112,96},{1... | collective-permute-start | bytes 4718600 | tf_op jit(solution)/shard_map/ppermute | solution.py:71
  106.9 3.0 %collective-permute-done.3 = bf16[256,3072]{1,0:T(8,128)(2,1)S(1)} collective-permute-done((bf16[256,3072]{1,0:T(8,128)(2,1)S(1)}, bf16[256,3072]{1,0:T(8,128)(2,1)S(1)}, u32[]{:S(2)}, u32[]{:S(2)}) %collective-permute-start.3) | collective-permute-done | bytes 1572896 | tf_op jit(solution)/shard_map/ppermute | solution.py:71
  109.9 0.5 fusion.6
  110.4 0.5 fusion.5
  110.9 1.3 convolution_convert_fusion.1
  112.2 0.1 pad_maximum_fusion
  112.3 4.8 %all-to-all-done.3 = bf16[32,16,768]{2,1,0:T(8,128)(2,1)S(1)} async-done(((bf16[32,16,768]{2,1,0:T(8,128)(2,1)}), bf16[32,16,768]{2,1,0:T(8,128)(2,1)S(1)}, u32[]{:S(2)}, u32[]{:S(2)}) %all-to-all-start.3) | async-done | bytes 786464 | tf_op jit(solution)/shard_map/all_to_all | solution.py:20
  117.2 0.2 convolution_convert_fusion.5
  117.4 0.2 reshape.127
  117.7 0.9 reshape.130
  118.6 23.3 %all-to-all-start.4 = ((bf16[16,2,1152]{2,1,0:T(2,128)(2,1)}), bf16[16,2,1152]{2,1,0:T(2,128)(2,1)S(1)}, u32[]{:S(2)}, u32[]{:S(2)}) async-start(bf16[16,2,1152]{2,1,0:T(2,128)(2,1)} %reshape.130), calls=%async_computation.4 | async-start | bytes 147456 | tf_op jit(solution)/shard_map/all_to_all | solution.py:20
  141.9 2.0 %copy.63 = bf16[1,2,84,3072]{3,1,2,0:T(2,128)(2,1)} copy(bf16[1,2,84,3072]{3,2,1,0:T(8,128)(2,1)S(1)} %bitcast.67) | data formatting | bytes 2064384
  143.9 2.8 %all-to-all-done.4 = bf16[16,2,1152]{2,1,0:T(2,128)(2,1)S(1)} async-done(((bf16[16,2,1152]{2,1,0:T(2,128)(2,1)}), bf16[16,2,1152]{2,1,0:T(2,128)(2,1)S(1)}, u32[]{:S(2)}, u32[]{:S(2)}) %all-to-all-start.4) | async-done | bytes 73760 | tf_op jit(solution)/shard_map/all_to_all | solution.py:20
  146.7 0.2 reshape.131
  147.0 0.6 bitcast_reduce_fusion
  (19 shorter events, 0.3 us)
Async XLA Ops:
  2.2 43.3 %all-to-all-start = ((bf16[16,2,1152]{2,1,0:T(2,128)(2,1)}), bf16[16,2,1152]{2,1,0:T(2,128)(2,1)S(1)}, u32[]{:S(2)}, u32[]{:S(2)}) async-start(bf16[16,2,1152]{2,1,0:T(2,128)(2,1)} %bitcast.3), calls=%async_computation | async-start | bytes 147456 | tf_op jit(solution)/shard_map/all_to_all | solution.py:20
  46.4 11.4 %all-to-all-start.1 = ((bf16[64,2,1152]{2,1,0:T(2,128)(2,1)}), bf16[64,2,1152]{2,1,0:T(2,128)(2,1)S(1)}, u32[]{:S(2)}, u32[]{:S(2)}) async-start(bf16[64,2,1152]{2,1,0:T(2,128)(2,1)} %bitcast.8), calls=%async_computation.1 | async-start | bytes 589824 | tf_op jit(solution)/shard_map/all_to_all | solution.py:20
  50.1 11.2 %collective-permute-start = (bf16[168,3072]{1,0:T(8,128)(2,1)S(1)}, bf16[168,3072]{1,0:T(8,128)(2,1)}, u32[]{:S(2)}, u32[]{:S(2)}) collective-permute-start(bf16[168,3072]{1,0:T(8,128)(2,1)S(1)} %pad_maximum_fusion.1), channel_id=1, source_target_pairs={{0,16},{16,0},{32,48},{48,32},{64,80},{80,64},{96,112},{112,96},{1... | collective-permute-start | bytes 3096584 | tf_op jit(solution)/shard_map/ppermute | solution.py:71
  53.5 7.8 %collective-permute-start.1 = (bf16[84,3072]{1,0:T(8,128)(2,1)}, bf16[84,3072]{1,0:T(8,128)(2,1)}, u32[]{:S(2)}, u32[]{:S(2)}) collective-permute-start(bf16[84,3072]{1,0:T(8,128)(2,1)} %bitcast.7), channel_id=1, source_target_pairs={{0,16},{16,0},{32,48},{48,32},{64,80},{80,64},{96,112},{112,96},{1... | collective-permute-start | bytes 1548296 | tf_op jit(solution)/shard_map/ppermute | solution.py:71
  61.3 27.9 %all-to-all-start.2 = ((bf16[16,16,3072]{2,1,0:T(8,128)(2,1)}), bf16[16,16,3072]{2,1,0:T(8,128)(2,1)S(1)}, u32[]{:S(2)}, u32[]{:S(2)}) async-start(bf16[16,16,3072]{2,1,0:T(8,128)(2,1)} %bitcast.11), calls=%async_computation.2 | async-start | bytes 3145728 | tf_op jit(solution)/shard_map/all_to_all | solution.py:20
  71.1 2.5 %copy-start.1 = (bf16[336,3072]{1,0:T(8,128)(2,1)S(1)}, bf16[336,3072]{1,0:T(8,128)(2,1)}, u32[]{:S(2)}) copy-start(bf16[336,3072]{1,0:T(8,128)(2,1)} %get-tuple-element.66) | copy-start | bytes 6193156
  91.8 7.3 %copy-start = (bf16[336,1536]{1,0:T(8,128)(2,1)S(1)}, bf16[336,1536]{1,0:T(8,128)(2,1)}, u32[]{:S(2)}) copy-start(bf16[336,1536]{1,0:T(8,128)(2,1)} %pad_maximum_fusion.2) | copy-start | bytes 3096580
  91.8 7.0 %collective-permute-start.2 = (f32[336,256]{1,0:T(8,128)S(1)}, f32[336,256]{1,0:T(8,128)S(1)}, u32[]{:S(2)}, u32[]{:S(2)}) collective-permute-start(f32[336,256]{1,0:T(8,128)S(1)} %pad_maximum_fusion.3), channel_id=1, source_target_pairs={{0,16},{16,0},{32,48},{48,32},{64,80},{80,64},{96,112},{112,96},{1... | collective-permute-start | bytes 1032200 | tf_op jit(solution)/shard_map/ppermute | solution.py:71
  100.6 16.6 %all-to-all-start.3 = ((bf16[32,16,768]{2,1,0:T(8,128)(2,1)}), bf16[32,16,768]{2,1,0:T(8,128)(2,1)S(1)}, u32[]{:S(2)}, u32[]{:S(2)}) async-start(bf16[32,16,768]{2,1,0:T(8,128)(2,1)} %bitcast.14), calls=%async_computation.3 | async-start | bytes 1572864 | tf_op jit(solution)/shard_map/all_to_all | solution.py:20
  104.5 5.5 %collective-permute-start.3 = (bf16[256,3072]{1,0:T(8,128)(2,1)S(1)}, bf16[256,3072]{1,0:T(8,128)(2,1)S(1)}, u32[]{:S(2)}, u32[]{:S(2)}) collective-permute-start(bf16[256,3072]{1,0:T(8,128)(2,1)S(1)} %bitcast.63), channel_id=1, source_target_pairs={{0,16},{16,0},{32,48},{48,32},{64,80},{80,64},{96,112},{112,96},{1... | collective-permute-start | bytes 4718600 | tf_op jit(solution)/shard_map/ppermute | solution.py:71
  118.6 28.1 %all-to-all-start.4 = ((bf16[16,2,1152]{2,1,0:T(2,128)(2,1)}), bf16[16,2,1152]{2,1,0:T(2,128)(2,1)S(1)}, u32[]{:S(2)}, u32[]{:S(2)}) async-start(bf16[16,2,1152]{2,1,0:T(2,128)(2,1)} %reshape.130), calls=%async_computation.4 | async-start | bytes 147456 | tf_op jit(solution)/shard_map/all_to_all | solution.py:20
